TPU v7x, 32 devices: a whole 2x2x4 slice. The times are simulated.
32 devices in a mesh: row: 8 (over z, core), col: 4 (over y, x).
Axes of the slice: x: 2, y: 2, z: 4, core: 2. Of those that a mesh axis runs over, the one named last changes fastest.
Arguments:
- tensor: float32 [16, 2048, 1024], P(None, 'row', 'col'), may hold values from -270 to 270
- factor_b: float32 [64, 1024], P(None, 'col'), may hold values from -6 to 6
- factor_c: float32 [16, 64], replicated, may hold values from -6 to 6
Outputs:
- result_a: float32 [64, 2048], P(None, 'row')
- result_b: float32 [64, 1024], P(None, 'col')
- column_scales: float32 [2, 64], replicated
All inputs are finite; a program needn't handle non-finite values.
Results may differ from a plain program's by a relative error of at most 0.0003.
Values sent between devices are 32-bit elements; how exact they have to be, the bound alone decides.
No kernel may reach another device: no remote copies, remote signals or barrier semaphores. Data moves between devices by JAX's collectives and lax.ppermute only.
A program may use at most 64 MiB of HBM per device.

v0:
```python
import jax
import jax.numpy as jnp
from jax import lax
from jax.sharding import PartitionSpec as P

SWEEPS = 3


epsilon = 1e-06


def gram_of(factor):
    return jnp.dot(
        factor, factor.T, precision=lax.Precision.HIGHEST, preferred_element_type=jnp.float32
    )


def settle_left(solved, count):
    squares = lax.psum(jnp.sum(solved * solved, axis=1), "row")
    scales = jnp.sqrt(squares / count + epsilon)
    normed = solved / scales[:, None]
    return (normed, scales, lax.psum(gram_of(normed), "row"))


def settle_right(solved, count):
    squares = lax.psum(jnp.sum(solved * solved, axis=1), "col")
    scales = jnp.sqrt(squares / count + epsilon)
    normed = solved / scales[:, None]
    return (normed, scales, lax.psum(gram_of(normed), "col"))


def shards(tensor, factor_b, factor_c):
    highest = lax.Precision.HIGHEST
    rows_all = tensor.shape[1] * lax.axis_size("row")
    cols_all = tensor.shape[2] * lax.axis_size("col")
    rank = factor_c.shape[1]
    identity = jnp.eye(rank, dtype=jnp.float32)
    gram_c = jnp.dot(factor_c.T, factor_c, precision=highest, preferred_element_type=jnp.float32)
    current_b = factor_b
    gram_b = lax.psum(gram_of(current_b), "col")
    current_a = jnp.zeros((rank, tensor.shape[1]), jnp.float32)
    scales_a = jnp.zeros((rank,), jnp.float32)
    scales_b = jnp.zeros((rank,), jnp.float32)
    for sweep in range(SWEEPS):
        lower_a = jnp.linalg.cholesky(gram_c * gram_b + cols_all * identity)
        inner = jnp.einsum("kij,rj->kir", tensor, current_b, precision=highest)
        partial_a = jnp.einsum("kir,kr->ri", inner, factor_c, precision=highest)
        summed_a = lax.psum(partial_a, "col")
        solved_a = jax.scipy.linalg.cho_solve((lower_a, True), summed_a)
        current_a, scales_a, gram_a = settle_left(solved_a, rows_all)
        lower_b = jnp.linalg.cholesky(gram_c * gram_a + rows_all * identity)
        outer = jnp.einsum("ri,kij->krj", current_a, tensor, precision=highest)
        partial_b = jnp.einsum("krj,kr->rj", outer, factor_c, precision=highest)
        summed_b = lax.psum(partial_b, "row")
        solved_b = jax.scipy.linalg.cho_solve((lower_b, True), summed_b)
        current_b, scales_b, gram_b = settle_right(solved_b, cols_all)
    return (current_a, current_b, jnp.stack([scales_a, scales_b]))


def solution(mesh):
    in_specs = (P(None, "row", "col"), P(None, "col"), P())
    out_specs = (P(None, "row"), P(None, "col"), P())
    return jax.shard_map(shards, mesh=mesh, in_specs=in_specs, out_specs=out_specs, check_vma=False)
```

profile of v0, /device:TPU:0, one launch (start us, length us, event | category | flops | bytes accessed | tf_op | source)
XLA Modules:
  0.0 564.7 jit_solution(6560141974948027514)
XLA Ops:
  7.2 0.8 copy-done
  8.0 5.6 multiply_reduce_fusion
  13.6 0.7 copy.32
  14.6 17.7 %psum.126 = f32[64,64]{0,1:T(8,128)S(1)} all-reduce(f32[64,64]{0,1:T(8,128)S(1)} %fusion.76), channel_id=1, replica_groups=mesh['row'=8,'col'=4] {'col'}, use_global_device_ids=true, to_apply=%region_0.0 | all-reduce | flops 4096 | bytes 32768 | tf_op jit(solution)/shard_map/psum | solution.py:40
  32.7 5.8 %cholesky.104 = f32[64,64]{1,0:T(8,128)S(1)} custom-call(f32[64,64]{1,0:T(8,128)S(1)} %fusion.61), custom_call_target="Cholesky" | custom-call | tf_op jit(solution)/shard_map/jit(cholesky)/cholesky | solution.py:45
  38.6 0.6 compare_reduce_fusion.5
  39.3 0.7 fusion.26
  40.0 4.9 custom-call.12
  44.9 14.2 %all-reduce.7.cloned.1.call-done = f32[64,256]{1,0:T(8,128)} async-done(((f32[64,256]{1,0:T(8,128)}), f32[64,256]{1,0:T(8,128)}) %all-reduce.7.cloned.1.call-update) | async-done | bytes 65552 | tf_op jit(solution)/shard_map/psum | solution.py:48
  59.1 1.1 fusion.59
  60.5 16.0 %psum.128 = f32[64]{0:T(128)S(1)} all-reduce(f32[64]{0:T(128)S(1)} %get-tuple-element.11), channel_id=1, replica_groups=mesh['row'=8,'col'=4] {'row'}, use_global_device_ids=true, to_apply=%region_5.0 | all-reduce | flops 64 | bytes 512 | tf_op jit(solution)/shard_map/psum | solution.py:19
  76.8 4.8 fusion.23
  81.6 25.9 %psum.129 = f32[64,64]{0,1:T(8,128)S(1)} all-reduce(f32[64,64]{0,1:T(8,128)S(1)} %fusion.70), channel_id=1, replica_groups=mesh['row'=8,'col'=4] {'row'}, use_global_device_ids=true, to_apply=%region_6.0 | all-reduce | flops 4096 | bytes 32768 | tf_op jit(solution)/shard_map/psum | solution.py:22
  107.7 5.8 %cholesky.115 = f32[64,64]{1,0:T(8,128)S(1)} custom-call(f32[64,64]{1,0:T(8,128)S(1)} %fusion.56), custom_call_target="Cholesky" | custom-call | tf_op jit(solution)/shard_map/jit(cholesky)/cholesky | solution.py:51
  113.6 0.6 compare_reduce_fusion.4
  114.2 1.3 fusion.8
  115.5 0.6 copy.79
  116.4 0.7 fusion.27
  117.1 4.9 custom-call.13
  121.9 45.2 %all-reduce.9.cloned.1.call-done = f32[64,256]{1,0:T(8,128)} async-done(((f32[64,256]{1,0:T(8,128)}), f32[64,256]{1,0:T(8,128)}) %all-reduce.9.cloned.1.call-update) | async-done | bytes 65552 | tf_op jit(solution)/shard_map/psum | solution.py:54
  167.2 1.1 fusion.54
  168.6 9.8 %psum.131 = f32[64]{0:T(128)S(1)} all-reduce(f32[64]{0:T(128)S(1)} %get-tuple-element.13), channel_id=1, replica_groups=mesh['row'=8,'col'=4] {'col'}, use_global_device_ids=true, to_apply=%region_9.0 | all-reduce | flops 64 | bytes 512 | tf_op jit(solution)/shard_map/psum | solution.py:26
  178.7 6.3 %fusion.21 = f32[64,16,256]{2,0,1:T(8,128)S(1)} fusion(f32[16,256,256]{2,1,0:T(8,128)} %param.6, f32[64,256]{1,0:T(8,128)S(1)} %get-tuple-element.14, f32[64]{0:T(128)S(1)} %add_sqrt_fusion.4), kind=kOutput, calls=%fused_computation.22 | convolution fusion | flops 805322752 | bytes 5308672 | tf_op jit(solution)/shard_map/kij,rj->kir/dot_general | solution.py:46
  185.0 14.4 %psum.132 = f32[64,64]{0,1:T(8,128)S(1)} all-reduce(f32[64,64]{0,1:T(8,128)S(1)} %fusion.71), channel_id=1, replica_groups=mesh['row'=8,'col'=4] {'col'}, use_global_device_ids=true, to_apply=%region_10.0 | all-reduce | flops 4096 | bytes 32768 | tf_op jit(solution)/shard_map/psum | solution.py:29
  199.5 5.8 %cholesky.126 = f32[64,64]{1,0:T(8,128)S(1)} custom-call(f32[64,64]{1,0:T(8,128)S(1)} %fusion.51), custom_call_target="Cholesky" | custom-call | tf_op jit(solution)/shard_map/jit(cholesky)/cholesky | solution.py:45
  205.3 0.6 compare_reduce_fusion.3
  206.0 1.3 fusion.6
  207.3 0.6 copy.78
  208.0 0.7 fusion.28
  208.7 4.9 custom-call.14
  213.6 34.1 %all-reduce.11.cloned.1.call-done = f32[64,256]{1,0:T(8,128)} async-done(((f32[64,256]{1,0:T(8,128)}), f32[64,256]{1,0:T(8,128)}) %all-reduce.11.cloned.1.call-update) | async-done | bytes 65552 | tf_op jit(solution)/shard_map/psum | solution.py:48
  247.7 1.1 fusion.49
  249.1 16.0 %psum.134 = f32[64]{0:T(128)S(1)} all-reduce(f32[64]{0:T(128)S(1)} %get-tuple-element.15), channel_id=1, replica_groups=mesh['row'=8,'col'=4] {'row'}, use_global_device_ids=true, to_apply=%region_13.0 | all-reduce | flops 64 | bytes 512 | tf_op jit(solution)/shard_map/psum | solution.py:19
  265.4 4.8 fusion.19
  270.2 26.2 %psum.135 = f32[64,64]{0,1:T(8,128)S(1)} all-reduce(f32[64,64]{0,1:T(8,128)S(1)} %fusion.72), channel_id=1, replica_groups=mesh['row'=8,'col'=4] {'row'}, use_global_device_ids=true, to_apply=%region_14.0 | all-reduce | flops 4096 | bytes 32768 | tf_op jit(solution)/shard_map/psum | solution.py:22
  296.5 5.8 %cholesky.137 = f32[64,64]{1,0:T(8,128)S(1)} custom-call(f32[64,64]{1,0:T(8,128)S(1)} %fusion.46), custom_call_target="Cholesky" | custom-call | tf_op jit(solution)/shard_map/jit(cholesky)/cholesky | solution.py:51
  302.4 0.6 compare_reduce_fusion.2
  303.0 1.3 fusion.4
  305.0 0.7 fusion.29
  305.7 4.9 custom-call.15
  310.6 45.5 %all-reduce.13.cloned.1.call-done = f32[64,256]{1,0:T(8,128)} async-done(((f32[64,256]{1,0:T(8,128)}), f32[64,256]{1,0:T(8,128)}) %all-reduce.13.cloned.1.call-update) | async-done | bytes 65552 | tf_op jit(solution)/shard_map/psum | solution.py:54
  356.0 1.1 fusion.44
  357.4 9.8 %psum.137 = f32[64]{0:T(128)S(1)} all-reduce(f32[64]{0:T(128)S(1)} %get-tuple-element.17), channel_id=1, replica_groups=mesh['row'=8,'col'=4] {'col'}, use_global_device_ids=true, to_apply=%region_17.0 | all-reduce | flops 64 | bytes 512 | tf_op jit(solution)/shard_map/psum | solution.py:26
  367.6 6.3 %fusion.17 = f32[64,16,256]{2,0,1:T(8,128)S(1)} fusion(f32[16,256,256]{2,1,0:T(8,128)} %param.6, f32[64,256]{1,0:T(8,128)S(1)} %get-tuple-element.18, f32[64]{0:T(128)S(1)} %add_sqrt_fusion.2), kind=kOutput, calls=%fused_computation.18 | convolution fusion | flops 805322752 | bytes 5308672 | tf_op jit(solution)/shard_map/kij,rj->kir/dot_general | solution.py:46
  373.8 14.4 %psum.138 = f32[64,64]{0,1:T(8,128)S(1)} all-reduce(f32[64,64]{0,1:T(8,128)S(1)} %fusion.73), channel_id=1, replica_groups=mesh['row'=8,'col'=4] {'col'}, use_global_device_ids=true, to_apply=%region_18.0 | all-reduce | flops 4096 | bytes 32768 | tf_op jit(solution)/shard_map/psum | solution.py:29
  388.3 5.8 %cholesky.148 = f32[64,64]{1,0:T(8,128)S(1)} custom-call(f32[64,64]{1,0:T(8,128)S(1)} %fusion.41), custom_call_target="Cholesky" | custom-call | tf_op jit(solution)/shard_map/jit(cholesky)/cholesky | solution.py:45
  394.2 0.6 compare_reduce_fusion.1
  394.8 1.3 fusion.2
  396.9 0.7 fusion.30
  397.5 4.9 custom-call.16
  402.4 34.1 %all-reduce.15.cloned.1.call-done = f32[64,256]{1,0:T(8,128)} async-done(((f32[64,256]{1,0:T(8,128)}), f32[64,256]{1,0:T(8,128)}) %all-reduce.15.cloned.1.call-update) | async-done | bytes 65552 | tf_op jit(solution)/shard_map/psum | solution.py:48
  436.6 1.1 fusion.39
  438.0 16.2 %psum.140 = f32[64]{0:T(128)S(1)} all-reduce(f32[64]{0:T(128)S(1)} %get-tuple-element.19), channel_id=1, replica_groups=mesh['row'=8,'col'=4] {'row'}, use_global_device_ids=true, to_apply=%region_21.0 | all-reduce | flops 64 | bytes 512 | tf_op jit(solution)/shard_map/psum | solution.py:19
  454.5 4.8 fusion.15
  459.3 25.9 %psum.141 = f32[64,64]{0,1:T(8,128)S(1)} all-reduce(f32[64,64]{0,1:T(8,128)S(1)} %fusion.77), channel_id=1, replica_groups=mesh['row'=8,'col'=4] {'row'}, use_global_device_ids=true, to_apply=%region_22.0 | all-reduce | flops 4096 | bytes 32768 | tf_op jit(solution)/shard_map/psum | solution.py:22
  485.4 5.8 %cholesky.159 = f32[64,64]{1,0:T(8,128)S(1)} custom-call(f32[64,64]{1,0:T(8,128)S(1)} %fusion.36), custom_call_target="Cholesky" | custom-call | tf_op jit(solution)/shard_map/jit(cholesky)/cholesky | solution.py:51
  491.2 0.6 compare_reduce_fusion
  491.9 1.3 fusion
  493.9 0.7 fusion.31
  494.5 4.9 custom-call.17
  499.4 45.5 %all-reduce.17.cloned.1.call-done = f32[64,256]{1,0:T(8,128)} async-done(((f32[64,256]{1,0:T(8,128)}), f32[64,256]{1,0:T(8,128)}) %all-reduce.17.cloned.1.call-update) | async-done | bytes 65552 | tf_op jit(solution)/shard_map/psum | solution.py:54
  544.9 1.1 fusion.34
  546.3 9.8 %psum.143 = f32[64]{0:T(128)S(1)} all-reduce(f32[64]{0:T(128)S(1)} %get-tuple-element.21), channel_id=1, replica_groups=mesh['row'=8,'col'=4] {'col'}, use_global_device_ids=true, to_apply=%region_25.28 | all-reduce | flops 64 | bytes 512 | tf_op jit(solution)/shard_map/psum | solution.py:26
  556.7 0.7 broadcast_divide_fusion
  (65 shorter events, 7.5 us)
Async XLA Ops:
  7.2 0.8 copy-start
  7.2 25.2 %copy-start.2 = (f32[16,64]{1,0:T(8,128)S(1)}, f32[16,64]{1,0:T(8,128)}, u32[]{:S(2)}) copy-start(f32[16,64]{1,0:T(8,128)} %param.8) | copy-start | bytes 12292
  7.2 51.9 %all-reduce.7.cloned.1.call-start = ((), (), s32[]{:S(2)}) async-start(), calls=%async_computation | async-start | bytes 131072 | tf_op jit(solution)/shard_map/psum | solution.py:48
  14.4 152.8 %all-reduce.9.cloned.1.call-start = ((), (), s32[]{:S(2)}) async-start(), calls=%async_computation.1 | async-start | bytes 131072 | tf_op jit(solution)/shard_map/psum | solution.py:54
  116.2 131.5 %all-reduce.11.cloned.1.call-start = ((), (), s32[]{:S(2)}) async-start(), calls=%async_computation.2 | async-start | bytes 131072 | tf_op jit(solution)/shard_map/psum | solution.py:48
  208.0 148.1 %all-reduce.13.cloned.1.call-start = ((), (), s32[]{:S(2)}) async-start(), calls=%async_computation.3 | async-start | bytes 131072 | tf_op jit(solution)/shard_map/psum | solution.py:54
  305.0 131.6 %all-reduce.15.cloned.1.call-start = ((), (), s32[]{:S(2)}) async-start(), calls=%async_computation.4 | async-start | bytes 131072 | tf_op jit(solution)/shard_map/psum | solution.py:48
  396.8 148.1 %all-reduce.17.cloned.1.call-start = ((), (), s32[]{:S(2)}) async-start(), calls=%async_computation.5 | async-start | bytes 131072 | tf_op jit(solution)/shard_map/psum | solution.py:54
  454.3 103.1 %copy-start.1 = (f32[64,256]{1,0:T(8,128)}, f32[64,256]{1,0:T(8,128)S(1)}, u32[]{:S(2)}) copy-start(f32[64,256]{1,0:T(8,128)S(1)} %broadcast_divide_fusion.1) | copy-start | bytes 196612
Sparse Core Ops, SparseCore 0:
  14.5 44.6 all-reduce.6
  116.3 50.8 all-reduce.8
  208.1 39.5 all-reduce.10
  305.1 50.8 all-reduce.12
  396.9 39.5 all-reduce.14
  494.0 50.8 all-reduce.16
where the time goes:
time: 574 us; the launch traced here: 565 us
  waiting for transfers between devices  219 us (38%)
  blocking collectives  202 us (35%)
  other arithmetic  74 us (13%)
  matrix products  49.1 us (9%)
  between operations  14.9 us (3%)
    psum x3, waiting for transfers between devices, shards(): summed_b = lax.psum(partial_b, 'row')  136 us
    psum x3, waiting for transfers between devices, shards(): summed_a = lax.psum(partial_a, 'col')  82.5 us
    psum x3, blocking collectives, settle_left(): return (normed, scales, lax.psum(gram_of(normed), 'row'))  78.1 us
    psum x3, blocking collectives, settle_left(): squares = lax.psum(jnp.sum(solved * solved, axis=1), 'row')  48.2 us
    psum x3, blocking collectives, settle_right(): squares = lax.psum(jnp.sum(solved * solved, axis=1), 'col')  29.5 us
    psum x2, blocking collectives, settle_right(): return (normed, scales, lax.psum(gram_of(normed), 'col'))  28.7 us
    another operation x9, other arithmetic, shards(): lower_a = jnp.linalg.cholesky(gram_c * gram_b + cols_all * identity)  19.6 us
    another operation x9, other arithmetic, shards(): lower_b = jnp.linalg.cholesky(gram_c * gram_a + rows_all * identity)  19.6 us
  transfers between devices with their start and end apart: 6, of which 6 were waited for; matrix products, arithmetic and copies ran while one was open for 7% of the time, Pallas kernels for 0%

commit v1 on v0

v1 whole, which is shorter than its diff:
```python
import functools

import jax
import jax.numpy as jnp
from jax import lax
from jax.experimental import pallas as pl
from jax.experimental.pallas import tpu as pltpu
from jax.sharding import PartitionSpec as P

SWEEPS = 3
EPSILON = 1e-06
TOLERANCE = 2e-06
RELAX = 0.95
VMEM_LIMIT = 16 * 1024 * 1024


def dot(x, y, contract=(1, 0), precision=None):
    return lax.dot_general(
        x,
        y,
        (((contract[0],), (contract[1],)), ((), ())),
        precision=precision,
        preferred_element_type=jnp.float32,
    )


exact_dot = functools.partial(dot, precision=lax.Precision.HIGHEST)


def split(x):
    high = x.astype(jnp.bfloat16)
    return high, (x - high.astype(jnp.float32)).astype(jnp.bfloat16)


def split_dot(x, y, contract=(1, 0)):
    rows = x[0].shape[0]
    both = dot(jnp.concatenate(x, axis=0), y[0], contract)
    return both[:rows] + (both[rows:] + dot(x[0], y[1], contract))


def identity_mask(rank):
    rows = lax.broadcasted_iota(jnp.int32, (rank, rank), 0)
    return rows == lax.broadcasted_iota(jnp.int32, (rank, rank), 1)


def groups(depth):
    ends = list(range(4, depth - 3, 4)) + list(range(max(depth - 2, 1), depth + 1, 2))
    return [range(start, end) for start, end in zip([0] + ends, ends)]


def mttkrp(factor, columns_c, high_ref, low_ref, ready=None):
    rank = factor.shape[0]
    both, cross = None, None
    for k in range(high_ref.shape[0]):
        if ready is not None:
            ready(k)
        high, low = split(factor * columns_c[:, k : k + 1])
        first = dot(jnp.concatenate([high, low], axis=0), high_ref[k])
        second = dot(high, low_ref[k])
        both = first if both is None else both + first
        cross = second if cross is None else cross + second
    return both[:rank] + (both[rank:] + cross)


def pack_gram(gram, width):
    rank = gram.shape[0]
    parts = width // rank
    rows = rank // parts
    return jnp.concatenate([gram[q * rows : (q + 1) * rows] for q in range(parts)], axis=1)


def unpack_gram(packed, rank):
    parts = packed.shape[1] // rank
    return jnp.concatenate([packed[:, q * rank : (q + 1) * rank] for q in range(parts)], axis=0)


def tree_sum(pieces):
    pieces = list(pieces)
    while len(pieces) > 1:
        pieces = [pieces[i] + pieces[i + 1] for i in range(0, len(pieces), 2)]
    return pieces[0]


def scale_system(gram_c, gram, mask, count, normalized):
    if normalized:
        system = gram_c * gram + jnp.where(mask, gram + count * EPSILON, 0.0)
    else:
        system = gram_c * gram + jnp.where(mask, jnp.float32(count), 0.0)
    diagonal = jnp.where(mask, system, 0.0)
    row, column = [jnp.sum(diagonal, axis=axis, keepdims=True) for axis in (0, 1)]
    error = jnp.where(mask, 1.0 - RELAX, -system * (RELAX / row))
    return error, row, column


def series(error, rhs, doublings):
    power = error
    for step in range(doublings - 1):
        parts = split(power)
        rhs = rhs + split_dot(parts, split(rhs))
        power = split_dot(parts, parts) if step < doublings - 2 else dot(parts[0], parts[0])
    return rhs + dot(power.astype(jnp.bfloat16), rhs.astype(jnp.bfloat16)), power


def careful_inverse(error, mask, total_ref, power_ref):
    unit = jnp.where(mask, 1.0, 0.0)
    system = unit - error
    bound = jnp.max(jnp.sum(jnp.abs(system), axis=0, keepdims=True), axis=1, keepdims=True)
    omega = jnp.minimum(1.0, 1.9 / bound)
    power = unit - omega * system
    total_ref[...] = unit + power
    power_ref[...] = power

    def unfinished(state):
        step, rest = state
        return jnp.logical_and(step < 48, rest > 1e-7)

    def double(state):
        power = exact_dot(power_ref[...], power_ref[...])
        power_ref[...] = power
        total = total_ref[...]
        total_ref[...] = total + exact_dot(total, power)
        return state[0] + 1, jnp.sum(power * power)

    lax.while_loop(unfinished, double, (jnp.int32(0), jnp.float32(1.0)))
    return omega * total_ref[...]


def start_kernel(tensor_hbm, factor_hbm, c_hbm, high_ref, low_ref, turned_high_ref, turned_low_ref, *refs):
    gram_c_ref, columns_ref, out_ref, tensor_ref, factor_ref, c_ref, padded_ref, sems = refs
    depth, rank = c_hbm.shape
    small = [
        pltpu.make_async_copy(c_hbm, c_ref, sems.at[depth]),
        pltpu.make_async_copy(factor_hbm, factor_ref, sems.at[depth + 1]),
    ]
    slices = {}
    for group in groups(depth):
        some = pl.ds(group[0], len(group))
        slices[group[0]] = pltpu.make_async_copy(tensor_hbm.at[some], tensor_ref.at[some], sems.at[group[0]])
    for copy in small + list(slices.values()):
        copy.start()
    for copy in small:
        copy.wait()
    padded_ref[:depth, :rank] = c_ref[...]
    columns_c = padded_ref[...].T[:rank, :depth]
    columns_ref[...] = columns_c
    factor = factor_ref[...]

    def ready(k):
        if k == groups(depth)[-1][0]:
            gram_c_ref[...] = exact_dot(columns_c, columns_c, (1, 1))
            parts = split(factor)
            out_ref[rank:] = pack_gram(split_dot(parts, parts, (1, 1)), factor.shape[1])
        if k in slices:
            slices[k].wait()
        high, low = split(tensor_ref[k])
        high_ref[k], low_ref[k] = high, low
        turned_high_ref[k], turned_low_ref[k] = high.T, low.T

    out_ref[:rank] = mttkrp(factor, columns_c, turned_high_ref, turned_low_ref, ready)


def own_core():
    return lax.axis_index("row") % 2


def own_half(rows):
    return pl.ds(pl.multiple_of(own_core() * (rows // 2), 8), rows // 2)


def merge(sum_ref, trade_refs, full_ref):
    if len(trade_refs) < 3:
        return tree_sum([ref[...] for ref in (sum_ref, *trade_refs)])
    got_ref, half_ref, swapped_ref = trade_refs
    rows = sum_ref.shape[0]
    core = own_core()
    full_ref[core] = got_ref[...]
    full_ref[1 - core] = swapped_ref[:rows]
    full_ref[2, own_half(rows)] = half_ref[...]
    full_ref[2, pl.ds(pl.multiple_of((1 - core) * (rows // 2), 8), rows // 2)] = swapped_ref[rows:]
    return (sum_ref[...] + full_ref[0]) + (full_ref[1] + full_ref[2])


def merge_kernel(count, sum_ref, *refs):
    trade_refs, (out_ref, half_ref, full_ref) = refs[:count], refs[count:]
    out_ref[...] = merge(sum_ref, trade_refs, full_ref)
    half_ref[...] = out_ref[own_half(out_ref.shape[0])]


def solve_kernel(count, normalized, summed, gram_c_ref, columns_ref, high_ref, low_ref, refs, scratch):
    rank = gram_c_ref.shape[0]
    mask = identity_mask(rank)
    gram = unpack_gram(summed[rank:], rank)
    error, row, column = scale_system(gram_c_ref[...], gram, mask, count, normalized)
    outer = RELAX / column
    if normalized:
        diagonal = jnp.where(mask, gram, 0.0)
        scales = [jnp.sqrt(jnp.sum(diagonal, axis=axis, keepdims=True) / count + EPSILON) for axis in (0, 1)]
        outer = outer * scales[1]
    packed_ref, solved_ref, squares_ref, scales_ref = refs
    if scales_ref is not None:
        scales_ref[...] = scales[0]

    def emit(solved):
        if solved_ref is not None:
            solved_ref[...] = solved
        if squares_ref is not None:
            squares = jnp.sum(solved * solved, axis=1, keepdims=True)
            row = jnp.sum(jnp.where(mask, squares, 0.0), axis=0, keepdims=True)
            squares_ref[...] = jnp.concatenate([row, row], axis=1) * jnp.ones((8, 1), jnp.float32)
        if packed_ref is not None:
            parts = split(solved)
            packed_ref[rank:] = pack_gram(split_dot(parts, parts, (1, 1)), solved.shape[1])
            packed_ref[:rank] = mttkrp(solved, columns_ref[...], high_ref, low_ref)

    solved, power = series(error, summed[:rank], 4)
    emit(outer * solved)
    roots = 1.0 / jnp.sqrt(column), jnp.sqrt(row)
    rest = jnp.sum(jnp.square(power * roots[0] * roots[1]))

    @pl.when(jnp.logical_not(rest <= TOLERANCE))
    def _():
        symmetric = error * roots[0] * roots[1]
        inverse = careful_inverse(symmetric, mask, *scratch)
        emit(outer / roots[0] * exact_dot(inverse, roots[0] * summed[:rank]))


def left_kernel(pieces_count, count, normalized, last, *refs):
    pieces, refs = refs[:pieces_count], refs[pieces_count:]
    parts, (packed_ref, *solved_ref), scratch = refs[:4], refs[4:-2], refs[-2:]
    summed = tree_sum([ref[...] for ref in pieces])
    outs = (packed_ref, solved_ref[0] if last else None, None, None)
    solve_kernel(count, normalized, summed, *parts, outs, scratch)


def right_kernel(pieces_count, count, last, sum_ref, *refs):
    pieces, refs = refs[:pieces_count], refs[pieces_count:]
    parts, outs, (full_ref, *scratch) = refs[:4], refs[4:-3], refs[-3:]
    outs = (None, *outs) if last else (*outs, None, None, None)
    solve_kernel(count, True, merge(sum_ref, pieces, full_ref), *parts, outs, scratch)


def finish_kernel(pieces_count, count, *refs):
    pieces, refs = refs[:pieces_count], refs[pieces_count:]
    scales_a_ref, solved_a_ref, solved_b_ref, result_a_ref, result_b_ref, scales_ref = refs
    rank = solved_b_ref.shape[0]
    mask = identity_mask(rank)
    row_b = jnp.sqrt(tree_sum([ref[...] for ref in pieces])[0:1, :rank] / count + EPSILON)
    row_a = scales_a_ref[...]
    column_a, column_b = [jnp.sum(jnp.where(mask, row, 0.0), axis=1, keepdims=True) for row in (row_a, row_b)]
    result_a_ref[...] = solved_a_ref[...] / column_a
    result_b_ref[...] = solved_b_ref[...] / column_b
    scales_ref[...] = jnp.concatenate([row_a, row_b], axis=0)


def call(kernel, out_shape, *args, scratch=(), **options):
    return pl.pallas_call(
        kernel,
        out_shape=out_shape,
        scratch_shapes=scratch,
        compiler_params=pltpu.CompilerParams(vmem_limit_bytes=VMEM_LIMIT),
        **options,
    )(*args)


def swap(x, axis, stride):
    return lax.ppermute(x, axis, [(d, d ^ stride) for d in range(lax.axis_size(axis))])


def exchange(x, axis, stride=1, radix=4):
    size = lax.axis_size(axis)
    while True:
        group = min(radix, size // stride)
        order = (1, 3, 2) if group == 4 else range(1, group)
        got = {m: swap(x, axis, m * stride) for m in order}
        pieces = [x] + [got[m] for m in range(1, group)]
        stride *= group
        if stride >= size:
            return pieces
        x = tree_sum(pieces)


def exchange_by_cores(x, axis):
    size = lax.axis_size(axis)
    half = jax.ShapeDtypeStruct((x.shape[0] // 2, x.shape[1]), x.dtype)
    scratch = [pltpu.VMEM((3,) + x.shape, x.dtype)]
    stride, trades = 2, (swap(x, axis, 1),)
    while stride < size:
        x, own = call(functools.partial(merge_kernel, len(trades)), (x, half), x, *trades, scratch=scratch)
        if 2 * stride < size:
            pairs = [(d, d ^ (stride if d % 2 == 0 else 2 * stride)) for d in range(size)]
            half_got = swap(own, axis, 3 * stride)
            got = lax.ppermute(x, axis, pairs)
            trades = (got, half_got, swap(jnp.concatenate([got, half_got], axis=0), axis, 1))
        else:
            trades = (swap(x, axis, stride),)
        stride *= 4
    return x, trades


def shards(tensor, factor_b, factor_c):
    rows_all = tensor.shape[1] * lax.axis_size("row")
    cols_all = tensor.shape[2] * lax.axis_size("col")
    depth, height, width = tensor.shape
    rank = factor_c.shape[1]
    f32 = functools.partial(jax.ShapeDtypeStruct, dtype=jnp.float32)
    part = jax.ShapeDtypeStruct(tensor.shape, jnp.bfloat16)
    turned = jax.ShapeDtypeStruct((depth, width, height), jnp.bfloat16)
    left, right = (rank, height), (rank, width)
    packed_a, packed_b = [(rank + rank * rank // n, n) for n in (height, width)]
    inverse = [pltpu.VMEM((rank, rank), jnp.float32)] * 2
    scratch = [pltpu.VMEM((3,) + packed_b, jnp.float32)] + inverse
    high, low, turned_high, turned_low, gram_c, columns, partial = call(
        start_kernel,
        (part, part, turned, turned, f32((rank, rank)), f32((rank, depth)), f32(packed_a)),
        *[pltpu.with_memory_space_constraint(x, pltpu.HBM) for x in (tensor, factor_b, factor_c)],
        in_specs=[pl.BlockSpec(memory_space=pltpu.HBM)] * 3,
        scratch=[
            pltpu.VMEM(tensor.shape, jnp.float32),
            pltpu.VMEM(factor_b.shape, jnp.float32),
            pltpu.VMEM(factor_c.shape, jnp.float32),
            pltpu.VMEM((128, 128), jnp.float32),
            pltpu.SemaphoreType.DMA((depth + 2,)),
        ],
    )
    parts, turned_parts = (gram_c, columns, high, low), (gram_c, columns, turned_high, turned_low)
    for sweep in range(SWEEPS):
        last = sweep == SWEEPS - 1
        pieces = exchange(partial, "col")
        kernel = functools.partial(left_kernel, len(pieces), cols_all, sweep > 0, last)
        outs = (f32(packed_b), f32(left)) if last else (f32(packed_b),)
        partial, *solved_a = call(kernel, outs, *pieces, *parts, scratch=inverse)
        partial, pieces = exchange_by_cores(partial, "row")
        kernel = functools.partial(right_kernel, len(pieces), rows_all, last)
        outs = (f32(right), f32((8, 2 * rank)), f32((1, rank))) if last else (f32(packed_a),)
        partial, *rest = call(kernel, outs, partial, *pieces, *turned_parts, scratch=scratch)
    solved_b, (squares, scales_a) = partial, rest
    pieces = exchange(squares, "col")
    kernel = functools.partial(finish_kernel, len(pieces), cols_all)
    outs = (f32(left), f32(right), f32((2, rank)))
    return tuple(call(kernel, outs, *pieces, scales_a, *solved_a, solved_b))


def solution(mesh):
    in_specs = (P(None, "row", "col"), P(None, "col"), P())
    out_specs = (P(None, "row"), P(None, "col"), P())
    return jax.shard_map(shards, mesh=mesh, in_specs=in_specs, out_specs=out_specs, check_vma=False)
```

time: 574 us -> 96.3 us (0.17); the launches traced: 565 us -> 95.5 us
  blocking collectives: 202 us -> 0 us
  waiting for transfers between devices: 219 us -> 31.8 us
  other arithmetic: 74 us -> 0.03 us
  matrix products: 49.1 us -> 0 us
  Pallas kernels: 0 us -> 36.4 us
  starting transfers between devices: 0.42 us -> 26.6 us
  between operations: 14.9 us -> 0.75 us
    psum x6 -> x0, waiting for transfers between devices: 219 us -> none  [the longest x3 136 us: shards(): summed_b = lax.psum(partial_b, 'row')]
    psum x12 -> x0, blocking collectives: 202 us -> none  [the longest x3 78.1 us: settle_left(): return (normed, scales, lax.psum(gram_of(normed), 'row'))]
    another operation x33 -> x0, other arithmetic: 73 us -> none  [the longest x9 19.6 us: shards(): lower_a = jnp.linalg.cholesky(gram_c * gram_b + cols_all * identity)]
    dot_general x18 -> x0, matrix products: 40.9 us -> none  [the longest x3 18.1 us: shards(): inner = jnp.einsum('kij,rj->kir', tensor, current_b, precision=highest)]
    pallas_call x0 -> x11, Pallas kernels: none -> 36.4 us  [call(): pl.pallas_call(kernel, out_shape=out_shape, scratch_shapes=scratch, compi...]
    ppermute x0 -> x24, waiting for transfers between devices: none -> 31.8 us  [the longest x21 31.7 us: swap(): lax.ppermute(x, axis, [(d, d ^ stride) for d in range(lax.axis_size(axis))])]
    ppermute x0 -> x24, starting transfers between devices: none -> 26.6 us  [the longest x21 24.6 us: swap(): lax.ppermute(x, axis, [(d, d ^ stride) for d in range(lax.axis_size(axis))])]
    another operation x12 -> x0, matrix products: 8.28 us -> none  [the longest x6 4.14 us: shards(): solved_b = jax.scipy.linalg.cho_solve((lower_b, True), summed_b)]
  transfers between devices with their start and end apart: 6 -> 24, of which waited for: 6 -> 20; matrix products, arithmetic and copies ran while one was open for 7% -> 0% of each run, Pallas kernels for 0% -> 0%
where the time goes in v1:
time: 96.3 us; the launch traced here: 95.5 us
  Pallas kernels  36.4 us (38%)
  waiting for transfers between devices  31.8 us (33%)
  starting transfers between devices  26.6 us (28%)
    pallas_call x11, Pallas kernels, call(): pl.pallas_call(kernel, out_shape=out_shape, scratch_shapes=scratch, compi...  36.4 us
    ppermute x21, waiting for transfers between devices, swap(): lax.ppermute(x, axis, [(d, d ^ stride) for d in range(lax.axis_size(axis))])  31.7 us
    ppermute x21, starting transfers between devices, swap(): lax.ppermute(x, axis, [(d, d ^ stride) for d in range(lax.axis_size(axis))])  24.6 us
    ppermute x3, starting transfers between devices, exchange_by_cores(): got = lax.ppermute(x, axis, pairs)  1.98 us
  transfers between devices with their start and end apart: 24, of which 20 were waited for; matrix products, arithmetic and copies ran while one was open for 0% of the time, Pallas kernels for 0%

profile of v1, /device:TPU:0, one launch (start us, length us, event | category | flops | bytes accessed | tf_op | source)
XLA Modules:
  0.0 95.5 jit_solution(3871604516483372003)
XLA Ops:
  0.6 3.7 %shard_map.58 = (bf16[16,256,256]{2,1,0:T(8,128)(2,1)S(1)}, bf16[16,256,256]{2,1,0:T(8,128)(2,1)S(1)}, bf16[16,256,256]{2,1,0:T(8,128)(2,1)S(1)}, bf16[16,256,25...) custom-call(f32[16,256,256]{2,1,0:T(8,128)} %tensor_hbm.1, ...), custom_call_target="tpu_custom_call" | custom-call | tf_op jit(solution)/shard_map/pallas_call | solution.py:256
  4.3 4.0 %collective-permute-start.2 = (f32[80,256]{1,0:T(8,128)S(1)}, f32[80,256]{1,0:T(8,128)S(1)}, u32[]{:S(2)}, u32[]{:S(2)}) collective-permute-start(f32[80,256]{1,0:T(8,128)S(1)} %get-tuple-element.21.refs_0_), channel_id=1, source_target_pairs={{0,3},{1,2},{2,1},{3,0},{4,7},{5,6},{6,5},{7,4},{8,11},{9,10},{10,... | collective-permute-start | bytes 245768 | tf_op jit(solution)/shard_map/ppermute | solution.py:266
  8.2 0.5 collective-permute-start.1
  8.8 0.1 collective-permute-start
  8.9 1.9 %collective-permute-done.2.refs_3_ = f32[80,256]{1,0:T(8,128)S(1)} collective-permute-done((f32[80,256]{1,0:T(8,128)S(1)}, f32[80,256]{1,0:T(8,128)S(1)}, u32[]{:S(2)}, u32[]{:S(2)}) %collective-permute-start.2) | collective-permute-done | bytes 81952 | tf_op jit(solution)/shard_map/ppermute | solution.py:266
  10.8 1.9 %collective-permute-done.1.refs_2_ = f32[80,256]{1,0:T(8,128)S(1)} collective-permute-done((f32[80,256]{1,0:T(8,128)S(1)}, f32[80,256]{1,0:T(8,128)S(1)}, u32[]{:S(2)}, u32[]{:S(2)}) %collective-permute-start.1) | collective-permute-done | bytes 81952 | tf_op jit(solution)/shard_map/ppermute | solution.py:266
  12.7 0.5 collective-permute-done.refs_1_
  13.2 4.4 %shard_map.59.sum_ref = f32[80,256]{1,0:T(8,128)S(1)} custom-call(f32[80,256]{1,0:T(8,128)S(1)} %get-tuple-element.21.refs_0_, f32[80,256]{1,0:T(8,128)S(1)} %collective-permute-done.refs_1_, f32[80,256]{1,0:T(8,128)S(1)} %collective-permute-done.1.refs_2_, f32[80,256]{1,0:T(8,128)S(1)} %collective-permute-done.2.refs_3_, ...), custom_call_target="tpu_custom_call" | custom-call | tf_op jit(solution)/shard_map/pallas_call | solution.py:256
  17.6 0.1 collective-permute-start.3
  17.7 1.3 %collective-permute-done.3.refs_0_ = f32[80,256]{1,0:T(8,128)S(1)} collective-permute-done((f32[80,256]{1,0:T(8,128)S(1)}, f32[80,256]{1,0:T(8,128)S(1)}, u32[]{:S(2)}, u32[]{:S(2)}) %collective-permute-start.3) | collective-permute-done | bytes 81952 | tf_op jit(solution)/shard_map/ppermute | solution.py:266
  19.0 1.6 %collective-permute-start.4 = (f32[80,256]{1,0:T(8,128)S(1)}, f32[80,256]{1,0:T(8,128)S(1)}, u32[]{:S(2)}, u32[]{:S(2)}) collective-permute-start(f32[80,256]{1,0:T(8,128)S(1)} %get-tuple-element.26.sum_ref), channel_id=1, source_target_pairs={{0,8},{4,20},{8,0},{12,28},{16,24},{20,4},{24,16},{28,12},{1,9},{5... | collective-permute-start | bytes 245768 | tf_op jit(solution)/shard_map/ppermute | solution.py:292
  20.6 2.5 %collective-permute-start.5 = (f32[40,256]{1,0:T(8,128)S(1)}, f32[40,256]{1,0:T(8,128)S(1)}, u32[]{:S(2)}, u32[]{:S(2)}) collective-permute-start(f32[40,256]{1,0:T(8,128)S(1)} %get-tuple-element.27), channel_id=1, source_target_pairs={{0,24},{4,28},{8,16},{12,20},{16,8},{20,12},{24,0},{28,4},{1,25},{... | collective-permute-start | bytes 122888 | tf_op jit(solution)/shard_map/ppermute | solution.py:266
  23.1 3.7 %collective-permute-done.5.refs_1_ = f32[40,256]{1,0:T(8,128)S(1)} collective-permute-done((f32[40,256]{1,0:T(8,128)S(1)}, f32[40,256]{1,0:T(8,128)S(1)}, u32[]{:S(2)}, u32[]{:S(2)}) %collective-permute-start.5) | collective-permute-done | bytes 40992 | tf_op jit(solution)/shard_map/ppermute | solution.py:266
  26.8 0.0 collective-permute-done.4.refs_0_
  26.8 0.1 collective-permute-start.6
  26.9 1.3 %collective-permute-done.6.refs_2_ = f32[120,256]{1,0:T(8,128)S(1)} collective-permute-done((f32[120,256]{1,0:T(8,128)S(1)}, f32[120,256]{1,0:T(8,128)S(1)}, u32[]{:S(2)}, u32[]{:S(2)}) %collective-permute-start.6) | collective-permute-done | bytes 122912 | tf_op jit(solution)/shard_map/ppermute | solution.py:266
  28.2 5.1 %shard_map.61.refs_0_ = f32[80,256]{1,0:T(8,128)S(1)} custom-call(f32[80,256]{1,0:T(8,128)S(1)} %get-tuple-element.26.sum_ref, f32[80,256]{1,0:T(8,128)S(1)} %collective-permute-done.4.refs_0_, f32[40,256]{1,0:T(8,128)S(1)} %collective-permute-done.5.refs_1_, f32[120,256]{1,0:T(8,128)S(1)} %collective-permute-done.6.refs_2_, ...), custom_call_target="tpu_custom_call" | custom-call | tf_op jit(solution)/shard_map/pallas_call | solution.py:256
  33.3 1.5 %collective-permute-start.9 = (f32[80,256]{1,0:T(8,128)S(1)}, f32[80,256]{1,0:T(8,128)S(1)}, u32[]{:S(2)}, u32[]{:S(2)}) collective-permute-start(f32[80,256]{1,0:T(8,128)S(1)} %shard_map.61.refs_0_), channel_id=1, source_target_pairs={{0,3},{1,2},{2,1},{3,0},{4,7},{5,6},{6,5},{7,4},{8,11},{9,10},{10,... | collective-permute-start | bytes 245768 | tf_op jit(solution)/shard_map/ppermute | solution.py:266
  34.9 1.0 %collective-permute-start.8 = (f32[80,256]{1,0:T(8,128)S(1)}, f32[80,256]{1,0:T(8,128)S(1)}, u32[]{:S(2)}, u32[]{:S(2)}) collective-permute-start(f32[80,256]{1,0:T(8,128)S(1)} %shard_map.61.refs_0_), channel_id=1, source_target_pairs={{0,2},{1,3},{2,0},{3,1},{4,6},{5,7},{6,4},{7,5},{8,10},{9,11},{10,... | collective-permute-start | bytes 245768 | tf_op jit(solution)/shard_map/ppermute | solution.py:266
  35.9 1.0 %collective-permute-start.7 = (f32[80,256]{1,0:T(8,128)S(1)}, f32[80,256]{1,0:T(8,128)S(1)}, u32[]{:S(2)}, u32[]{:S(2)}) collective-permute-start(f32[80,256]{1,0:T(8,128)S(1)} %shard_map.61.refs_0_), channel_id=1, source_target_pairs={{0,1},{1,0},{2,3},{3,2},{4,5},{5,4},{6,7},{7,6},{8,9},{9,8},{10,11... | collective-permute-start | bytes 245768 | tf_op jit(solution)/shard_map/ppermute | solution.py:266
  36.9 2.2 %collective-permute-done.9.refs_3_ = f32[80,256]{1,0:T(8,128)S(1)} collective-permute-done((f32[80,256]{1,0:T(8,128)S(1)}, f32[80,256]{1,0:T(8,128)S(1)}, u32[]{:S(2)}, u32[]{:S(2)}) %collective-permute-start.9) | collective-permute-done | bytes 81952 | tf_op jit(solution)/shard_map/ppermute | solution.py:266
  39.1 1.4 %collective-permute-done.8.refs_2_ = f32[80,256]{1,0:T(8,128)S(1)} collective-permute-done((f32[80,256]{1,0:T(8,128)S(1)}, f32[80,256]{1,0:T(8,128)S(1)}, u32[]{:S(2)}, u32[]{:S(2)}) %collective-permute-start.8) | collective-permute-done | bytes 81952 | tf_op jit(solution)/shard_map/ppermute | solution.py:266
  40.6 0.1 collective-permute-done.7.refs_1_
  40.7 6.1 %shard_map.62.sum_ref = f32[80,256]{1,0:T(8,128)S(1)} custom-call(f32[80,256]{1,0:T(8,128)S(1)} %shard_map.61.refs_0_, f32[80,256]{1,0:T(8,128)S(1)} %collective-permute-done.7.refs_1_, f32[80,256]{1,0:T(8,128)S(1)} %collective-permute-done.8.refs_2_, f32[80,256]{1,0:T(8,128)S(1)} %collective-permute-done.9.refs_3_, ...), custom_call_target="tpu_custom_call" | custom-call | tf_op jit(solution)/shard_map/pallas_call | solution.py:256
  46.8 0.1 collective-permute-start.10
  46.9 1.3 %collective-permute-done.10.refs_0_ = f32[80,256]{1,0:T(8,128)S(1)} collective-permute-done((f32[80,256]{1,0:T(8,128)S(1)}, f32[80,256]{1,0:T(8,128)S(1)}, u32[]{:S(2)}, u32[]{:S(2)}) %collective-permute-start.10) | collective-permute-done | bytes 81952 | tf_op jit(solution)/shard_map/ppermute | solution.py:266
  48.2 0.2 collective-permute-start.11
  48.4 3.2 %collective-permute-start.12 = (f32[40,256]{1,0:T(8,128)S(1)}, f32[40,256]{1,0:T(8,128)S(1)}, u32[]{:S(2)}, u32[]{:S(2)}) collective-permute-start(f32[40,256]{1,0:T(8,128)S(1)} %get-tuple-element.31), channel_id=1, source_target_pairs={{0,24},{4,28},{8,16},{12,20},{16,8},{20,12},{24,0},{28,4},{1,25},{... | collective-permute-start | bytes 122888 | tf_op jit(solution)/shard_map/ppermute | solution.py:266
  51.7 2.9 %collective-permute-done.12.refs_1_ = f32[40,256]{1,0:T(8,128)S(1)} collective-permute-done((f32[40,256]{1,0:T(8,128)S(1)}, f32[40,256]{1,0:T(8,128)S(1)}, u32[]{:S(2)}, u32[]{:S(2)}) %collective-permute-start.12) | collective-permute-done | bytes 40992 | tf_op jit(solution)/shard_map/ppermute | solution.py:266
  54.6 0.0 collective-permute-done.11.refs_0_
  54.6 0.3 collective-permute-start.13
  54.9 1.1 %collective-permute-done.13.refs_2_ = f32[120,256]{1,0:T(8,128)S(1)} collective-permute-done((f32[120,256]{1,0:T(8,128)S(1)}, f32[120,256]{1,0:T(8,128)S(1)}, u32[]{:S(2)}, u32[]{:S(2)}) %collective-permute-start.13) | collective-permute-done | bytes 122912 | tf_op jit(solution)/shard_map/ppermute | solution.py:266
  56.0 6.0 %shard_map.64.refs_0_ = f32[80,256]{1,0:T(8,128)S(1)} custom-call(f32[80,256]{1,0:T(8,128)S(1)} %get-tuple-element.30.sum_ref, f32[80,256]{1,0:T(8,128)S(1)} %collective-permute-done.11.refs_0_, f32[40,256]{1,0:T(8,128)S(1)} %collective-permute-done.12.refs_1_, f32[120,256]{1,0:T(8,128)S(1)} %collective-permute-done.13.refs_2_, ...), custom_call_target="tpu_custom_call" | custom-call | tf_op jit(solution)/shard_map/pallas_call | solution.py:256
  62.0 1.6 %collective-permute-start.16 = (f32[80,256]{1,0:T(8,128)S(1)}, f32[80,256]{1,0:T(8,128)S(1)}, u32[]{:S(2)}, u32[]{:S(2)}) collective-permute-start(f32[80,256]{1,0:T(8,128)S(1)} %shard_map.64.refs_0_), channel_id=1, source_target_pairs={{0,3},{1,2},{2,1},{3,0},{4,7},{5,6},{6,5},{7,4},{8,11},{9,10},{10,... | collective-permute-start | bytes 245768 | tf_op jit(solution)/shard_map/ppermute | solution.py:266
  63.6 0.8 collective-permute-start.15
  64.5 1.1 %collective-permute-start.14 = (f32[80,256]{1,0:T(8,128)S(1)}, f32[80,256]{1,0:T(8,128)S(1)}, u32[]{:S(2)}, u32[]{:S(2)}) collective-permute-start(f32[80,256]{1,0:T(8,128)S(1)} %shard_map.64.refs_0_), channel_id=1, source_target_pairs={{0,1},{1,0},{2,3},{3,2},{4,5},{5,4},{6,7},{7,6},{8,9},{9,8},{10,11... | collective-permute-start | bytes 245768 | tf_op jit(solution)/shard_map/ppermute | solution.py:266
  65.6 2.2 %collective-permute-done.16.refs_3_ = f32[80,256]{1,0:T(8,128)S(1)} collective-permute-done((f32[80,256]{1,0:T(8,128)S(1)}, f32[80,256]{1,0:T(8,128)S(1)}, u32[]{:S(2)}, u32[]{:S(2)}) %collective-permute-start.16) | collective-permute-done | bytes 81952 | tf_op jit(solution)/shard_map/ppermute | solution.py:266
  67.8 1.6 %collective-permute-done.15.refs_2_ = f32[80,256]{1,0:T(8,128)S(1)} collective-permute-done((f32[80,256]{1,0:T(8,128)S(1)}, f32[80,256]{1,0:T(8,128)S(1)}, u32[]{:S(2)}, u32[]{:S(2)}) %collective-permute-start.15) | collective-permute-done | bytes 81952 | tf_op jit(solution)/shard_map/ppermute | solution.py:266
  69.3 0.0 collective-permute-done.14.refs_1_
  69.3 5.8 %shard_map.65 = (f32[80,256]{1,0:T(8,128)S(1)}, f32[64,256]{1,0:T(8,128)S(1)}) custom-call(f32[80,256]{1,0:T(8,128)S(1)} %shard_map.64.refs_0_, f32[80,256]{1,0:T(8,128)S(1)} %collective-permute-done.14.refs_1_, f32[80,256]{1,0:T(8,128)S(1)} %collective-permute-done.15.refs_2_, f32[80,256]{1,0:T(8,128)S(1)} %collective-permute-done.16.refs_3_, ...), custom_call_target="tpu_custom_call" | custom-call | tf_op jit(solution)/shard_map/pallas_call | solution.py:256
  75.1 0.1 collective-permute-start.17
  75.2 1.3 %collective-permute-done.17.refs_0_ = f32[80,256]{1,0:T(8,128)S(1)} collective-permute-done((f32[80,256]{1,0:T(8,128)S(1)}, f32[80,256]{1,0:T(8,128)S(1)}, u32[]{:S(2)}, u32[]{:S(2)}) %collective-permute-start.17) | collective-permute-done | bytes 81952 | tf_op jit(solution)/shard_map/ppermute | solution.py:266
  76.5 0.1 collective-permute-start.18
  76.6 2.9 %collective-permute-start.19 = (f32[40,256]{1,0:T(8,128)S(1)}, f32[40,256]{1,0:T(8,128)S(1)}, u32[]{:S(2)}, u32[]{:S(2)}) collective-permute-start(f32[40,256]{1,0:T(8,128)S(1)} %get-tuple-element.34), channel_id=1, source_target_pairs={{0,24},{4,28},{8,16},{12,20},{16,8},{20,12},{24,0},{28,4},{1,25},{... | collective-permute-start | bytes 122888 | tf_op jit(solution)/shard_map/ppermute | solution.py:266
  79.5 3.4 %collective-permute-done.19.refs_1_ = f32[40,256]{1,0:T(8,128)S(1)} collective-permute-done((f32[40,256]{1,0:T(8,128)S(1)}, f32[40,256]{1,0:T(8,128)S(1)}, u32[]{:S(2)}, u32[]{:S(2)}) %collective-permute-start.19) | collective-permute-done | bytes 40992 | tf_op jit(solution)/shard_map/ppermute | solution.py:266
  82.9 0.0 collective-permute-done.18.refs_0_
  83.0 0.1 collective-permute-start.20
  83.1 1.3 %collective-permute-done.20.refs_2_ = f32[120,256]{1,0:T(8,128)S(1)} collective-permute-done((f32[120,256]{1,0:T(8,128)S(1)}, f32[120,256]{1,0:T(8,128)S(1)}, u32[]{:S(2)}, u32[]{:S(2)}) %collective-permute-start.20) | collective-permute-done | bytes 122912 | tf_op jit(solution)/shard_map/ppermute | solution.py:266
  84.4 4.5 %shard_map.67 = (f32[64,256]{1,0:T(8,128)S(1)}, f32[8,128]{1,0:T(8,128)S(1)}, f32[1,64]{1,0:T(1,128)S(1)}) custom-call(f32[80,256]{1,0:T(8,128)S(1)} %get-tuple-element.33.sum_ref, f32[80,256]{1,0:T(8,128)S(1)} %collective-permute-done.18.refs_0_, f32[40,256]{1,0:T(8,128)S(1)} %collective-permute-done.19.refs_1_, ...), custom_call_target="tpu_custom_call" | custom-call | tf_op jit(solution)/shard_map/pallas_call | solution.py:256
  88.8 1.6 %collective-permute-start.23 = (f32[8,128]{1,0:T(8,128)S(1)}, f32[8,128]{1,0:T(8,128)S(1)}, u32[]{:S(2)}, u32[]{:S(2)}) collective-permute-start(f32[8,128]{1,0:T(8,128)S(1)} %get-tuple-element.35.refs_0_), channel_id=1, source_target_pairs={{0,3},{1,2},{2,1},{3,0},{4,7},{5,6},{6,5},{7,4},{8,11},{9,10},{10,... | collective-permute-start | bytes 12296 | tf_op jit(solution)/shard_map/ppermute | solution.py:266
  90.5 0.7 collective-permute-start.22
  91.2 1.1 %collective-permute-start.21 = (f32[8,128]{1,0:T(8,128)S(1)}, f32[8,128]{1,0:T(8,128)S(1)}, u32[]{:S(2)}, u32[]{:S(2)}) collective-permute-start(f32[8,128]{1,0:T(8,128)S(1)} %get-tuple-element.35.refs_0_), channel_id=1, source_target_pairs={{0,1},{1,0},{2,3},{3,2},{4,5},{5,4},{6,7},{7,6},{8,9},{9,8},{10,11... | collective-permute-start | bytes 12296 | tf_op jit(solution)/shard_map/ppermute | solution.py:266
  92.3 1.0 %collective-permute-done.23.refs_3_ = f32[8,128]{1,0:T(8,128)S(1)} collective-permute-done((f32[8,128]{1,0:T(8,128)S(1)}, f32[8,128]{1,0:T(8,128)S(1)}, u32[]{:S(2)}, u32[]{:S(2)}) %collective-permute-start.23) | collective-permute-done | bytes 4128 | tf_op jit(solution)/shard_map/ppermute | solution.py:266
  93.3 0.7 collective-permute-done.22.refs_2_
  94.1 0.7 collective-permute-done.21.refs_1_
  94.8 0.8 shard_map.68
  (6 shorter events, 0.1 us)
Async XLA Ops:
  4.3 6.5 %collective-permute-start.2 = (f32[80,256]{1,0:T(8,128)S(1)}, f32[80,256]{1,0:T(8,128)S(1)}, u32[]{:S(2)}, u32[]{:S(2)}) collective-permute-start(f32[80,256]{1,0:T(8,128)S(1)} %get-tuple-element.21.refs_0_), channel_id=1, source_target_pairs={{0,3},{1,2},{2,1},{3,0},{4,7},{5,6},{6,5},{7,4},{8,11},{9,10},{10,... | collective-permute-start | bytes 245768 | tf_op jit(solution)/shard_map/ppermute | solution.py:266
  8.2 4.4 %collective-permute-start.1 = (f32[80,256]{1,0:T(8,128)S(1)}, f32[80,256]{1,0:T(8,128)S(1)}, u32[]{:S(2)}, u32[]{:S(2)}) collective-permute-start(f32[80,256]{1,0:T(8,128)S(1)} %get-tuple-element.21.refs_0_), channel_id=1, source_target_pairs={{0,2},{1,3},{2,0},{3,1},{4,6},{5,7},{6,4},{7,5},{8,10},{9,11},{10,... | collective-permute-start | bytes 245768 | tf_op jit(solution)/shard_map/ppermute | solution.py:266
  8.8 4.4 %collective-permute-start = (f32[80,256]{1,0:T(8,128)S(1)}, f32[80,256]{1,0:T(8,128)S(1)}, u32[]{:S(2)}, u32[]{:S(2)}) collective-permute-start(f32[80,256]{1,0:T(8,128)S(1)} %get-tuple-element.21.refs_0_), channel_id=1, source_target_pairs={{0,1},{1,0},{2,3},{3,2},{4,5},{5,4},{6,7},{7,6},{8,9},{9,8},{10,11... | collective-permute-start | bytes 245768 | tf_op jit(solution)/shard_map/ppermute | solution.py:266
  17.6 1.3 %collective-permute-start.3 = (f32[80,256]{1,0:T(8,128)S(1)}, f32[80,256]{1,0:T(8,128)S(1)}, u32[]{:S(2)}, u32[]{:S(2)}) collective-permute-start(f32[80,256]{1,0:T(8,128)S(1)} %shard_map.59.sum_ref), channel_id=1, source_target_pairs={{0,4},{4,0},{8,12},{12,8},{16,20},{20,16},{24,28},{28,24},{1,5},{5... | collective-permute-start | bytes 245768 | tf_op jit(solution)/shard_map/ppermute | solution.py:266
  19.0 7.8 %collective-permute-start.4 = (f32[80,256]{1,0:T(8,128)S(1)}, f32[80,256]{1,0:T(8,128)S(1)}, u32[]{:S(2)}, u32[]{:S(2)}) collective-permute-start(f32[80,256]{1,0:T(8,128)S(1)} %get-tuple-element.26.sum_ref), channel_id=1, source_target_pairs={{0,8},{4,20},{8,0},{12,28},{16,24},{20,4},{24,16},{28,12},{1,9},{5... | collective-permute-start | bytes 245768 | tf_op jit(solution)/shard_map/ppermute | solution.py:292
  20.6 6.2 %collective-permute-start.5 = (f32[40,256]{1,0:T(8,128)S(1)}, f32[40,256]{1,0:T(8,128)S(1)}, u32[]{:S(2)}, u32[]{:S(2)}) collective-permute-start(f32[40,256]{1,0:T(8,128)S(1)} %get-tuple-element.27), channel_id=1, source_target_pairs={{0,24},{4,28},{8,16},{12,20},{16,8},{20,12},{24,0},{28,4},{1,25},{... | collective-permute-start | bytes 122888 | tf_op jit(solution)/shard_map/ppermute | solution.py:266
  26.8 1.4 %collective-permute-start.6 = (f32[120,256]{1,0:T(8,128)S(1)}, f32[120,256]{1,0:T(8,128)S(1)}, u32[]{:S(2)}, u32[]{:S(2)}) collective-permute-start(f32[120,256]{1,0:T(8,128)S(1)} %pad_maximum_fusion), channel_id=1, source_target_pairs={{0,4},{4,0},{8,12},{12,8},{16,20},{20,16},{24,28},{28,24},{1,5},{5... | collective-permute-start | bytes 368648 | tf_op jit(solution)/shard_map/ppermute | solution.py:266
  33.3 5.8 %collective-permute-start.9 = (f32[80,256]{1,0:T(8,128)S(1)}, f32[80,256]{1,0:T(8,128)S(1)}, u32[]{:S(2)}, u32[]{:S(2)}) collective-permute-start(f32[80,256]{1,0:T(8,128)S(1)} %shard_map.61.refs_0_), channel_id=1, source_target_pairs={{0,3},{1,2},{2,1},{3,0},{4,7},{5,6},{6,5},{7,4},{8,11},{9,10},{10,... | collective-permute-start | bytes 245768 | tf_op jit(solution)/shard_map/ppermute | solution.py:266
  34.9 5.7 %collective-permute-start.8 = (f32[80,256]{1,0:T(8,128)S(1)}, f32[80,256]{1,0:T(8,128)S(1)}, u32[]{:S(2)}, u32[]{:S(2)}) collective-permute-start(f32[80,256]{1,0:T(8,128)S(1)} %shard_map.61.refs_0_), channel_id=1, source_target_pairs={{0,2},{1,3},{2,0},{3,1},{4,6},{5,7},{6,4},{7,5},{8,10},{9,11},{10,... | collective-permute-start | bytes 245768 | tf_op jit(solution)/shard_map/ppermute | solution.py:266
  35.9 4.8 %collective-permute-start.7 = (f32[80,256]{1,0:T(8,128)S(1)}, f32[80,256]{1,0:T(8,128)S(1)}, u32[]{:S(2)}, u32[]{:S(2)}) collective-permute-start(f32[80,256]{1,0:T(8,128)S(1)} %shard_map.61.refs_0_), channel_id=1, source_target_pairs={{0,1},{1,0},{2,3},{3,2},{4,5},{5,4},{6,7},{7,6},{8,9},{9,8},{10,11... | collective-permute-start | bytes 245768 | tf_op jit(solution)/shard_map/ppermute | solution.py:266
  46.8 1.3 %collective-permute-start.10 = (f32[80,256]{1,0:T(8,128)S(1)}, f32[80,256]{1,0:T(8,128)S(1)}, u32[]{:S(2)}, u32[]{:S(2)}) collective-permute-start(f32[80,256]{1,0:T(8,128)S(1)} %shard_map.62.sum_ref), channel_id=1, source_target_pairs={{0,4},{4,0},{8,12},{12,8},{16,20},{20,16},{24,28},{28,24},{1,5},{5... | collective-permute-start | bytes 245768 | tf_op jit(solution)/shard_map/ppermute | solution.py:266
  48.2 6.4 %collective-permute-start.11 = (f32[80,256]{1,0:T(8,128)S(1)}, f32[80,256]{1,0:T(8,128)S(1)}, u32[]{:S(2)}, u32[]{:S(2)}) collective-permute-start(f32[80,256]{1,0:T(8,128)S(1)} %get-tuple-element.30.sum_ref), channel_id=1, source_target_pairs={{0,8},{4,20},{8,0},{12,28},{16,24},{20,4},{24,16},{28,12},{1,9},{5... | collective-permute-start | bytes 245768 | tf_op jit(solution)/shard_map/ppermute | solution.py:292
  48.4 6.2 %collective-permute-start.12 = (f32[40,256]{1,0:T(8,128)S(1)}, f32[40,256]{1,0:T(8,128)S(1)}, u32[]{:S(2)}, u32[]{:S(2)}) collective-permute-start(f32[40,256]{1,0:T(8,128)S(1)} %get-tuple-element.31), channel_id=1, source_target_pairs={{0,24},{4,28},{8,16},{12,20},{16,8},{20,12},{24,0},{28,4},{1,25},{... | collective-permute-start | bytes 122888 | tf_op jit(solution)/shard_map/ppermute | solution.py:266
  54.6 1.4 %collective-permute-start.13 = (f32[120,256]{1,0:T(8,128)S(1)}, f32[120,256]{1,0:T(8,128)S(1)}, u32[]{:S(2)}, u32[]{:S(2)}) collective-permute-start(f32[120,256]{1,0:T(8,128)S(1)} %pad_maximum_fusion.1), channel_id=1, source_target_pairs={{0,4},{4,0},{8,12},{12,8},{16,20},{20,16},{24,28},{28,24},{1,5},{5... | collective-permute-start | bytes 368648 | tf_op jit(solution)/shard_map/ppermute | solution.py:266
  62.0 5.8 %collective-permute-start.16 = (f32[80,256]{1,0:T(8,128)S(1)}, f32[80,256]{1,0:T(8,128)S(1)}, u32[]{:S(2)}, u32[]{:S(2)}) collective-permute-start(f32[80,256]{1,0:T(8,128)S(1)} %shard_map.64.refs_0_), channel_id=1, source_target_pairs={{0,3},{1,2},{2,1},{3,0},{4,7},{5,6},{6,5},{7,4},{8,11},{9,10},{10,... | collective-permute-start | bytes 245768 | tf_op jit(solution)/shard_map/ppermute | solution.py:266
  63.6 5.7 %collective-permute-start.15 = (f32[80,256]{1,0:T(8,128)S(1)}, f32[80,256]{1,0:T(8,128)S(1)}, u32[]{:S(2)}, u32[]{:S(2)}) collective-permute-start(f32[80,256]{1,0:T(8,128)S(1)} %shard_map.64.refs_0_), channel_id=1, source_target_pairs={{0,2},{1,3},{2,0},{3,1},{4,6},{5,7},{6,4},{7,5},{8,10},{9,11},{10,... | collective-permute-start | bytes 245768 | tf_op jit(solution)/shard_map/ppermute | solution.py:266
  64.5 4.9 %collective-permute-start.14 = (f32[80,256]{1,0:T(8,128)S(1)}, f32[80,256]{1,0:T(8,128)S(1)}, u32[]{:S(2)}, u32[]{:S(2)}) collective-permute-start(f32[80,256]{1,0:T(8,128)S(1)} %shard_map.64.refs_0_), channel_id=1, source_target_pairs={{0,1},{1,0},{2,3},{3,2},{4,5},{5,4},{6,7},{7,6},{8,9},{9,8},{10,11... | collective-permute-start | bytes 245768 | tf_op jit(solution)/shard_map/ppermute | solution.py:266
  75.1 1.3 %collective-permute-start.17 = (f32[80,256]{1,0:T(8,128)S(1)}, f32[80,256]{1,0:T(8,128)S(1)}, u32[]{:S(2)}, u32[]{:S(2)}) collective-permute-start(f32[80,256]{1,0:T(8,128)S(1)} %get-tuple-element.32.sum_ref), channel_id=1, source_target_pairs={{0,4},{4,0},{8,12},{12,8},{16,20},{20,16},{24,28},{28,24},{1,5},{5... | collective-permute-start | bytes 245768 | tf_op jit(solution)/shard_map/ppermute | solution.py:266
  76.5 6.4 %collective-permute-start.18 = (f32[80,256]{1,0:T(8,128)S(1)}, f32[80,256]{1,0:T(8,128)S(1)}, u32[]{:S(2)}, u32[]{:S(2)}) collective-permute-start(f32[80,256]{1,0:T(8,128)S(1)} %get-tuple-element.33.sum_ref), channel_id=1, source_target_pairs={{0,8},{4,20},{8,0},{12,28},{16,24},{20,4},{24,16},{28,12},{1,9},{5... | collective-permute-start | bytes 245768 | tf_op jit(solution)/shard_map/ppermute | solution.py:292
  76.6 6.3 %collective-permute-start.19 = (f32[40,256]{1,0:T(8,128)S(1)}, f32[40,256]{1,0:T(8,128)S(1)}, u32[]{:S(2)}, u32[]{:S(2)}) collective-permute-start(f32[40,256]{1,0:T(8,128)S(1)} %get-tuple-element.34), channel_id=1, source_target_pairs={{0,24},{4,28},{8,16},{12,20},{16,8},{20,12},{24,0},{28,4},{1,25},{... | collective-permute-start | bytes 122888 | tf_op jit(solution)/shard_map/ppermute | solution.py:266
  83.0 1.4 %collective-permute-start.20 = (f32[120,256]{1,0:T(8,128)S(1)}, f32[120,256]{1,0:T(8,128)S(1)}, u32[]{:S(2)}, u32[]{:S(2)}) collective-permute-start(f32[120,256]{1,0:T(8,128)S(1)} %pad_maximum_fusion.2), channel_id=1, source_target_pairs={{0,4},{4,0},{8,12},{12,8},{16,20},{20,16},{24,28},{28,24},{1,5},{5... | collective-permute-start | bytes 368648 | tf_op jit(solution)/shard_map/ppermute | solution.py:266
  88.8 4.5 %collective-permute-start.23 = (f32[8,128]{1,0:T(8,128)S(1)}, f32[8,128]{1,0:T(8,128)S(1)}, u32[]{:S(2)}, u32[]{:S(2)}) collective-permute-start(f32[8,128]{1,0:T(8,128)S(1)} %get-tuple-element.35.refs_0_), channel_id=1, source_target_pairs={{0,3},{1,2},{2,1},{3,0},{4,7},{5,6},{6,5},{7,4},{8,11},{9,10},{10,... | collective-permute-start | bytes 12296 | tf_op jit(solution)/shard_map/ppermute | solution.py:266
  90.5 3.6 %collective-permute-start.22 = (f32[8,128]{1,0:T(8,128)S(1)}, f32[8,128]{1,0:T(8,128)S(1)}, u32[]{:S(2)}, u32[]{:S(2)}) collective-permute-start(f32[8,128]{1,0:T(8,128)S(1)} %get-tuple-element.35.refs_0_), channel_id=1, source_target_pairs={{0,2},{1,3},{2,0},{3,1},{4,6},{5,7},{6,4},{7,5},{8,10},{9,11},{10,... | collective-permute-start | bytes 12296 | tf_op jit(solution)/shard_map/ppermute | solution.py:266
  91.2 3.6 %collective-permute-start.21 = (f32[8,128]{1,0:T(8,128)S(1)}, f32[8,128]{1,0:T(8,128)S(1)}, u32[]{:S(2)}, u32[]{:S(2)}) collective-permute-start(f32[8,128]{1,0:T(8,128)S(1)} %get-tuple-element.35.refs_0_), channel_id=1, source_target_pairs={{0,1},{1,0},{2,3},{3,2},{4,5},{5,4},{6,7},{7,6},{8,9},{9,8},{10,11... | collective-permute-start | bytes 12296 | tf_op jit(solution)/shard_map/ppermute | solution.py:266

commit v2 on v1

v2 whole, which is shorter than its diff:
```python
import functools

import jax
import jax.numpy as jnp
from jax import lax
from jax.experimental import pallas as pl
from jax.experimental.pallas import tpu as pltpu
from jax.sharding import PartitionSpec as P

SWEEPS = 3
EPSILON = 1e-06
TOLERANCE = 2e-06
RELAX = 0.95
GROUP = 4
VMEM_LIMIT = 16 * 1024 * 1024


def dot(x, y, contract=(1, 0), precision=None):
    return lax.dot_general(
        x,
        y,
        (((contract[0],), (contract[1],)), ((), ())),
        precision=precision,
        preferred_element_type=jnp.float32,
    )


exact_dot = functools.partial(dot, precision=lax.Precision.HIGHEST)


def split(x):
    high = x.astype(jnp.bfloat16)
    return high, (x - high.astype(jnp.float32)).astype(jnp.bfloat16)


def split_dot(x, y, contract=(1, 0)):
    rows = x[0].shape[0]
    both = dot(jnp.concatenate(x, axis=0), y[0], contract)
    return both[:rows] + (both[rows:] + dot(x[0], y[1], contract))


def identity_mask(rank):
    rows = lax.broadcasted_iota(jnp.int32, (rank, rank), 0)
    return rows == lax.broadcasted_iota(jnp.int32, (rank, rank), 1)


def mttkrp(factor, columns_c, high_ref, low_ref, ready=None):
    rank = factor.shape[0]
    both, cross = None, None
    for k in range(high_ref.shape[0]):
        if ready is not None:
            ready(k)
        high, low = split(factor * columns_c[:, k : k + 1])
        first = dot(jnp.concatenate([high, low], axis=0), high_ref[k])
        second = dot(high, low_ref[k])
        both = first if both is None else both + first
        cross = second if cross is None else cross + second
    return both[:rank] + (both[rank:] + cross)


def pack_gram(gram, width):
    rank = gram.shape[0]
    parts = width // rank
    rows = rank // parts
    return jnp.concatenate([gram[q * rows : (q + 1) * rows] for q in range(parts)], axis=1)


def pack(solved, columns_ref, high_ref, low_ref, packed_ref):
    rank, width = solved.shape
    parts = split(solved)
    packed_ref[rank:] = pack_gram(split_dot(parts, parts, (1, 1)), width)
    packed_ref[:rank] = mttkrp(solved, columns_ref[...], high_ref, low_ref)


def unpack_gram(packed, rank):
    parts = packed.shape[1] // rank
    return jnp.concatenate([packed[:, q * rank : (q + 1) * rank] for q in range(parts)], axis=0)


def tree_sum(pieces):
    pieces = list(pieces)
    while len(pieces) > 1:
        pieces = [pieces[i] + pieces[i + 1] for i in range(0, len(pieces), 2)]
    return pieces[0]


def scale_system(gram_c, gram, mask, count, normalized):
    if normalized:
        system = gram_c * gram + jnp.where(mask, gram + count * EPSILON, 0.0)
    else:
        system = gram_c * gram + jnp.where(mask, jnp.float32(count), 0.0)
    diagonal = jnp.where(mask, system, 0.0)
    row, column = [jnp.sum(diagonal, axis=axis, keepdims=True) for axis in (0, 1)]
    error = jnp.where(mask, 1.0 - RELAX, -system * (RELAX / row))
    return error, row, column


def series(error, rhs, doublings):
    power = error
    for step in range(doublings - 1):
        parts = split(power)
        rhs = rhs + split_dot(parts, split(rhs))
        power = split_dot(parts, parts) if step < doublings - 2 else dot(parts[0], parts[0])
    return rhs + dot(power.astype(jnp.bfloat16), rhs.astype(jnp.bfloat16)), power


def inverse_series(error, mask, doublings):
    total, power = jnp.where(mask, 1.0, 0.0) + error, error
    for step in range(doublings - 1):
        parts = split(power)
        power = split_dot(parts, parts) if step < doublings - 2 else dot(parts[0], parts[0])
        total = total + split_dot(split(power), split(total))
    return total, power


def careful_inverse(error, mask, total_ref, power_ref):
    unit = jnp.where(mask, 1.0, 0.0)
    system = unit - error
    bound = jnp.max(jnp.sum(jnp.abs(system), axis=0, keepdims=True), axis=1, keepdims=True)
    omega = jnp.minimum(1.0, 1.9 / bound)
    power = unit - omega * system
    total_ref[...] = unit + power
    power_ref[...] = power

    def unfinished(state):
        step, rest = state
        return jnp.logical_and(step < 48, rest > 1e-7)

    def double(state):
        power = exact_dot(power_ref[...], power_ref[...])
        power_ref[...] = power
        total = total_ref[...]
        total_ref[...] = total + exact_dot(total, power)
        return state[0] + 1, jnp.sum(power * power)

    lax.while_loop(unfinished, double, (jnp.int32(0), jnp.float32(1.0)))
    return omega * total_ref[...]


def start_kernel(tensor_hbm, factor_hbm, c_hbm, high_ref, low_ref, turned_high_ref, turned_low_ref, *refs):
    gram_c_ref, columns_ref, out_ref, tensor_ref, factor_ref, c_ref, padded_ref, sems = refs
    depth, rank = c_hbm.shape
    small = [
        pltpu.make_async_copy(c_hbm, c_ref, sems.at[depth]),
        pltpu.make_async_copy(factor_hbm, factor_ref, sems.at[depth + 1]),
    ]
    slices = []
    for k in range(0, depth, GROUP):
        some = pl.ds(k, min(GROUP, depth - k))
        slices.append(pltpu.make_async_copy(tensor_hbm.at[some], tensor_ref.at[some], sems.at[k]))
    for copy in small + slices:
        copy.start()
    for copy in small:
        copy.wait()
    padded_ref[:depth, :rank] = c_ref[...]
    columns_c = padded_ref[...].T[:rank, :depth]
    columns_ref[...] = columns_c
    factor = factor_ref[...]

    def arrive(k):
        if k % GROUP == 0 and k < depth:
            slices[k // GROUP].wait()
            for k in range(k, min(k + GROUP, depth)):
                high, low = split(tensor_ref[k])
                high_ref[k], low_ref[k] = high, low
                turned_high_ref[k], turned_low_ref[k] = high.T, low.T

    def ready(k):
        if k == 0:
            arrive(0)
        arrive(k + GROUP)
        if k == GROUP:
            gram_c_ref[...] = exact_dot(columns_c, columns_c, (1, 1))
            parts = split(factor)
            out_ref[rank:] = pack_gram(split_dot(parts, parts, (1, 1)), factor.shape[1])

    out_ref[:rank] = mttkrp(factor, columns_c, turned_high_ref, turned_low_ref, ready)


def own_core():
    return lax.axis_index("row") % 2


def own_half(rows, core):
    return pl.ds(pl.multiple_of(core * (rows // 2), 8), rows // 2)


def traded_gram(rank, sum_ref, got_ref, half_ref, swapped_ref):
    here, got, swapped = [ref[rank:] for ref in (sum_ref, got_ref, swapped_ref)]
    first = own_core() == 0
    return (here + jnp.where(first, got, swapped)) + (jnp.where(first, swapped, got) + half_ref[rank // 2 :])


def traded_sum(rank, sum_ref, got_ref, half_ref, swapped_ref, other_ref, full_ref):
    core = own_core()
    full_ref[core] = got_ref[:rank]
    full_ref[1 - core] = swapped_ref[:rank]
    full_ref[2, own_half(rank, core)] = half_ref[: rank // 2]
    full_ref[2, own_half(rank, 1 - core)] = other_ref[...]
    return (sum_ref[:rank] + full_ref[0]) + (full_ref[1] + full_ref[2])


def merge_kernel(rank, *refs):
    pieces, (out_ref, half_ref, full_ref) = refs[:-3], refs[-3:]
    if len(pieces) == 2:
        out_ref[...] = pieces[0][...] + pieces[1][...]
    else:
        out_ref[rank:] = traded_gram(rank, *pieces[:4])
        out_ref[:rank] = traded_sum(rank, *pieces, full_ref)
    half_ref[: rank // 2] = out_ref[own_half(rank, own_core())]
    half_ref[rank // 2 :] = out_ref[rank:]


def factor_scales(gram, mask, count):
    diagonal = jnp.where(mask, gram, 0.0)
    return [jnp.sqrt(jnp.sum(diagonal, axis=axis, keepdims=True) / count + EPSILON) for axis in (0, 1)]


def invert_kernel(count, *refs):
    trades, (gram_c_ref, inverse_ref, *scales_ref), scratch = refs[:4], refs[4:-2], refs[-2:]
    rank = gram_c_ref.shape[0]
    mask = identity_mask(rank)
    gram = unpack_gram(traded_gram(rank, *trades), rank)
    error, row, column = scale_system(gram_c_ref[...], gram, mask, count, True)
    scales = factor_scales(gram, mask, count)
    if scales_ref:
        scales_ref[0][...] = scales[0]
    outer = RELAX * scales[1] / column
    total, power = inverse_series(error, mask, 4)
    inverse_ref[...] = outer * total
    roots = 1.0 / jnp.sqrt(column), jnp.sqrt(row)
    rest = jnp.sum(jnp.square(power * roots[0] * roots[1]))

    @pl.when(jnp.logical_not(rest <= TOLERANCE))
    def _():
        symmetric = error * roots[0] * roots[1]
        inverse_ref[...] = (outer / roots[0]) * careful_inverse(symmetric, mask, *scratch) / roots[1]


def left_kernel(pieces_count, count, normalized, last, *refs):
    pieces, refs = refs[:pieces_count], refs[pieces_count:]
    (gram_c_ref, *parts), (packed_ref, *solved_ref), scratch = refs[:4], refs[4:-2], refs[-2:]
    rank = gram_c_ref.shape[0]
    mask = identity_mask(rank)
    summed = tree_sum([ref[...] for ref in pieces])
    gram = unpack_gram(summed[rank:], rank)
    error, row, column = scale_system(gram_c_ref[...], gram, mask, count, normalized)
    outer = RELAX / column
    if normalized:
        outer = outer * factor_scales(gram, mask, count)[1]

    def emit(solved):
        if last:
            solved_ref[0][...] = solved
        pack(solved, *parts, packed_ref)

    solved, power = series(error, summed[:rank], 4)
    emit(outer * solved)
    roots = 1.0 / jnp.sqrt(column), jnp.sqrt(row)
    rest = jnp.sum(jnp.square(power * roots[0] * roots[1]))

    @pl.when(jnp.logical_not(rest <= TOLERANCE))
    def _():
        symmetric = error * roots[0] * roots[1]
        inverse = careful_inverse(symmetric, mask, *scratch)
        emit(outer / roots[0] * exact_dot(inverse, roots[0] * summed[:rank]))


def right_kernel(last, *refs):
    trades, inverse_ref, refs, full_ref = refs[:5], refs[5], refs[6:-1], refs[-1]
    rank = inverse_ref.shape[0]
    solved = split_dot(split(inverse_ref[...]), split(traded_sum(rank, *trades, full_ref)))
    if last:
        solved_ref, squares_ref = refs
        solved_ref[...] = solved
        squares = jnp.sum(solved * solved, axis=1, keepdims=True)
        row = jnp.sum(jnp.where(identity_mask(rank), squares, 0.0), axis=0, keepdims=True)
        squares_ref[...] = jnp.concatenate([row, row], axis=1) * jnp.ones((8, 1), jnp.float32)
    else:
        pack(solved, *refs)


def result_kernel(scales_ref, solved_ref, result_ref, out_ref):
    row = scales_ref[...]
    mask = identity_mask(row.shape[1])
    result_ref[...] = solved_ref[...] / jnp.sum(jnp.where(mask, row, 0.0), axis=1, keepdims=True)
    out_ref[...] = row


def finish_kernel(pieces_count, count, *refs):
    pieces, (scales_a_ref, solved_ref, result_ref, scales_ref) = refs[:pieces_count], refs[pieces_count:]
    rank = solved_ref.shape[0]
    row = jnp.sqrt(tree_sum([ref[...] for ref in pieces])[0:1, :rank] / count + EPSILON)
    result_ref[...] = solved_ref[...] / jnp.sum(jnp.where(identity_mask(rank), row, 0.0), axis=1, keepdims=True)
    scales_ref[...] = jnp.concatenate([scales_a_ref[...], row], axis=0)


def call(kernel, out_shape, *args, scratch=(), **options):
    return pl.pallas_call(
        kernel,
        out_shape=out_shape,
        scratch_shapes=scratch,
        compiler_params=pltpu.CompilerParams(vmem_limit_bytes=VMEM_LIMIT),
        **options,
    )(*args)


def swap(x, axis, stride):
    return lax.ppermute(x, axis, [(d, d ^ stride) for d in range(lax.axis_size(axis))])


def exchange(x, axis, stride=1, radix=4):
    size = lax.axis_size(axis)
    while True:
        group = min(radix, size // stride)
        pieces = [x] + [swap(x, axis, m * stride) for m in range(1, group)]
        stride *= group
        if stride >= size:
            return pieces
        x = tree_sum(pieces)


def exchange_by_cores(x, axis, rank):
    size = lax.axis_size(axis)
    out = jax.ShapeDtypeStruct((x.shape[0] - rank // 2, x.shape[1]), x.dtype)
    scratch = [pltpu.VMEM((3, rank, x.shape[1]), x.dtype)]
    stride, pieces = 2, (x, swap(x, axis, 1))
    while stride < size:
        x, own = call(functools.partial(merge_kernel, rank), (x, out), *pieces, scratch=scratch)
        half = swap(own, axis, 3 * stride)
        got = lax.ppermute(x, axis, [(d, d ^ (stride if d % 2 == 0 else 2 * stride)) for d in range(size)])
        pieces = (x, got, half, swap(got, axis, 1), swap(half[: rank // 2], axis, 1))
        stride *= 4
    return pieces


def shards(tensor, factor_b, factor_c):
    rows_all = tensor.shape[1] * lax.axis_size("row")
    cols_all = tensor.shape[2] * lax.axis_size("col")
    depth, height, width = tensor.shape
    rank = factor_c.shape[1]
    f32 = functools.partial(jax.ShapeDtypeStruct, dtype=jnp.float32)
    part = jax.ShapeDtypeStruct(tensor.shape, jnp.bfloat16)
    turned = jax.ShapeDtypeStruct((depth, width, height), jnp.bfloat16)
    left, right = (rank, height), (rank, width)
    packed_a, packed_b = [(rank + rank * rank // n, n) for n in (height, width)]
    scratch = [pltpu.VMEM((rank, rank), jnp.float32)] * 2
    full = [pltpu.VMEM((3, rank, width), jnp.float32)]
    high, low, turned_high, turned_low, gram_c, columns, partial = call(
        start_kernel,
        (part, part, turned, turned, f32((rank, rank)), f32((rank, depth)), f32(packed_a)),
        *[pltpu.with_memory_space_constraint(x, pltpu.HBM) for x in (tensor, factor_b, factor_c)],
        in_specs=[pl.BlockSpec(memory_space=pltpu.HBM)] * 3,
        scratch=[
            pltpu.VMEM(tensor.shape, jnp.float32),
            pltpu.VMEM(factor_b.shape, jnp.float32),
            pltpu.VMEM(factor_c.shape, jnp.float32),
            pltpu.VMEM((128, 128), jnp.float32),
            pltpu.SemaphoreType.DMA((depth + 2,)),
        ],
    )
    cost = pl.CostEstimate(flops=0, bytes_accessed=4 * tensor.size, transcendentals=0)
    for sweep in range(SWEEPS):
        last = sweep == SWEEPS - 1
        pieces = exchange(partial, "col")
        kernel = functools.partial(left_kernel, len(pieces), cols_all, sweep > 0, last)
        outs = (f32(packed_b), f32(left)) if last else (f32(packed_b),)
        partial, *solved_a = call(kernel, outs, *pieces, gram_c, columns, high, low, scratch=scratch)
        pieces = exchange_by_cores(partial, "row", rank)
        kernel = functools.partial(invert_kernel, rows_all)
        outs = (f32((rank, rank)), f32((1, rank))) if last else (f32((rank, rank)),)
        inverse, *scales_a = call(kernel, outs, *pieces[:4], gram_c, scratch=scratch, cost_estimate=cost)
        kernel = functools.partial(right_kernel, last)
        if not last:
            partial = call(
                kernel, f32(packed_a), *pieces, inverse, columns, turned_high, turned_low, scratch=full
            )
        else:
            solved_b, squares = call(kernel, (f32(right), f32((8, 2 * rank))), *pieces, inverse, scratch=full)
    pieces = exchange(squares, "col")
    result_a, scales_a = call(result_kernel, (f32(left), f32((1, rank))), *scales_a, *solved_a, cost_estimate=cost)
    kernel = functools.partial(finish_kernel, len(pieces), cols_all)
    result_b, scales = call(kernel, (f32(right), f32((2, rank))), *pieces, scales_a, solved_b)
    return result_a, result_b, scales


def solution(mesh):
    in_specs = (P(None, "row", "col"), P(None, "col"), P())
    out_specs = (P(None, "row"), P(None, "col"), P())
    return jax.shard_map(shards, mesh=mesh, in_specs=in_specs, out_specs=out_specs, check_vma=False)
```

time: 96.3 us -> 92.2 us (0.957)
  waiting for transfers between devices: 31.8 us -> 27.8 us
  Pallas kernels: 36.4 us -> 34.6 us
  starting transfers between devices: 26.6 us -> 28.1 us
    ppermute x21 -> x24, waiting for transfers between devices: 31.7 us -> 23.8 us  [swap(): lax.ppermute(x, axis, [(d, d ^ stride) for d in range(lax.axis_size(axis))])]
    ppermute x3, waiting for transfers between devices: 0.01 us -> 3.99 us  [exchange_by_cores(): lax.ppermute(x, axis, [(d, d ^ (stride if d % 2 == 0 else 2 * stride)) fo...]
    pallas_call x11 -> x15, Pallas kernels: 36.4 us -> 34.6 us  [call(): pl.pallas_call(kernel, out_shape=out_shape, scratch_shapes=scratch, compi...]
    ppermute x3, starting transfers between devices: 1.98 us -> 3.16 us  [exchange_by_cores(): lax.ppermute(x, axis, [(d, d ^ (stride if d % 2 == 0 else 2 * stride)) fo...]
    ppermute x21 -> x24, starting transfers between devices: 24.6 us -> 24.9 us  [swap(): lax.ppermute(x, axis, [(d, d ^ stride) for d in range(lax.axis_size(axis))])]
  transfers between devices with their start and end apart: 24 -> 27, of which waited for: 20 -> 20; matrix products, arithmetic and copies ran while one was open for 0% -> 0% of each run, Pallas kernels for 0% -> 13%
where the time goes in v2:
time: 92.2 us; the launch traced here: 91.3 us
  Pallas kernels  34.6 us (38%)
  starting transfers between devices  28.1 us (30%)
  waiting for transfers between devices  27.8 us (30%)
    pallas_call x15, Pallas kernels, call(): pl.pallas_call(kernel, out_shape=out_shape, scratch_shapes=scratch, compi...  34.6 us
    ppermute x24, starting transfers between devices, swap(): lax.ppermute(x, axis, [(d, d ^ stride) for d in range(lax.axis_size(axis))])  24.9 us
    ppermute x24, waiting for transfers between devices, swap(): lax.ppermute(x, axis, [(d, d ^ stride) for d in range(lax.axis_size(axis))])  23.8 us
    ppermute x3, waiting for transfers between devices, exchange_by_cores(): lax.ppermute(x, axis, [(d, d ^ (stride if d % 2 == 0 else 2 * stride)) fo...  3.99 us
    ppermute x3, starting transfers between devices, exchange_by_cores(): lax.ppermute(x, axis, [(d, d ^ (stride if d % 2 == 0 else 2 * stride)) fo...  3.16 us
  transfers between devices with their start and end apart: 27, of which 20 were waited for; matrix products, arithmetic and copies ran while one was open for 0% of the time, Pallas kernels for 13%

profile of v2, /device:TPU:0, one launch (start us, length us, event | category | flops | bytes accessed | tf_op | source)
XLA Modules:
  0.0 91.3 jit_solution(6842686091188008273)
XLA Ops:
  0.6 3.5 %shard_map.58 = (bf16[16,256,256]{2,1,0:T(8,128)(2,1)S(1)}, bf16[16,256,256]{2,1,0:T(8,128)(2,1)S(1)}, bf16[16,256,256]{2,1,0:T(8,128)(2,1)S(1)}, bf16[16,256,25...) custom-call(f32[16,256,256]{2,1,0:T(8,128)} %tensor_hbm.1, ...), custom_call_target="tpu_custom_call" | custom-call | tf_op jit(solution)/shard_map/pallas_call | solution.py:299
  4.2 4.0 %collective-permute-start.2 = (f32[80,256]{1,0:T(8,128)S(1)}, f32[80,256]{1,0:T(8,128)S(1)}, u32[]{:S(2)}, u32[]{:S(2)}) collective-permute-start(f32[80,256]{1,0:T(8,128)S(1)} %get-tuple-element.26.refs_0_), channel_id=1, source_target_pairs={{0,3},{1,2},{2,1},{3,0},{4,7},{5,6},{6,5},{7,4},{8,11},{9,10},{10,... | collective-permute-start | bytes 245768 | tf_op jit(solution)/shard_map/ppermute | solution.py:309
  8.1 0.5 collective-permute-start.1
  8.6 0.1 collective-permute-start
  8.8 1.9 %collective-permute-done.2.refs_3_ = f32[80,256]{1,0:T(8,128)S(1)} collective-permute-done((f32[80,256]{1,0:T(8,128)S(1)}, f32[80,256]{1,0:T(8,128)S(1)}, u32[]{:S(2)}, u32[]{:S(2)}) %collective-permute-start.2) | collective-permute-done | bytes 81952 | tf_op jit(solution)/shard_map/ppermute | solution.py:309
  10.7 1.9 %collective-permute-done.1.refs_2_ = f32[80,256]{1,0:T(8,128)S(1)} collective-permute-done((f32[80,256]{1,0:T(8,128)S(1)}, f32[80,256]{1,0:T(8,128)S(1)}, u32[]{:S(2)}, u32[]{:S(2)}) %collective-permute-start.1) | collective-permute-done | bytes 81952 | tf_op jit(solution)/shard_map/ppermute | solution.py:309
  12.6 0.5 collective-permute-done.refs_1_
  13.1 4.4 %shard_map.59.refs_0_ = f32[80,256]{1,0:T(8,128)S(1)} custom-call(f32[80,256]{1,0:T(8,128)S(1)} %get-tuple-element.26.refs_0_, f32[80,256]{1,0:T(8,128)S(1)} %collective-permute-done.refs_1_, f32[80,256]{1,0:T(8,128)S(1)} %collective-permute-done.1.refs_2_, f32[80,256]{1,0:T(8,128)S(1)} %collective-permute-done.2.refs_3_, ...), custom_call_target="tpu_custom_call" | custom-call | tf_op jit(solution)/shard_map/pallas_call | solution.py:299
  17.5 0.1 collective-permute-start.3
  17.6 1.3 %collective-permute-done.3.refs_1_ = f32[80,256]{1,0:T(8,128)S(1)} collective-permute-done((f32[80,256]{1,0:T(8,128)S(1)}, f32[80,256]{1,0:T(8,128)S(1)}, u32[]{:S(2)}, u32[]{:S(2)}) %collective-permute-start.3) | collective-permute-done | bytes 81952 | tf_op jit(solution)/shard_map/ppermute | solution.py:309
  18.9 1.6 %collective-permute-start.4 = (f32[80,256]{1,0:T(8,128)S(1)}, f32[80,256]{1,0:T(8,128)S(1)}, u32[]{:S(2)}, u32[]{:S(2)}) collective-permute-start(f32[80,256]{1,0:T(8,128)S(1)} %get-tuple-element.31.refs_0_), channel_id=1, source_target_pairs={{0,8},{4,20},{8,0},{12,28},{16,24},{20,4},{24,16},{28,12},{1,9},{5... | collective-permute-start | bytes 245768 | tf_op jit(solution)/shard_map/ppermute | solution.py:331
  20.5 2.5 %collective-permute-start.5 = (f32[48,256]{1,0:T(8,128)S(1)}, f32[48,256]{1,0:T(8,128)S(1)}, u32[]{:S(2)}, u32[]{:S(2)}) collective-permute-start(f32[48,256]{1,0:T(8,128)S(1)} %get-tuple-element.32), channel_id=1, source_target_pairs={{0,24},{4,28},{8,16},{12,20},{16,8},{20,12},{24,0},{28,4},{1,25},{... | collective-permute-start | bytes 147464 | tf_op jit(solution)/shard_map/ppermute | solution.py:309
  23.0 1.3 %collective-permute-done.4.refs_1_ = f32[80,256]{1,0:T(8,128)S(1)} collective-permute-done((f32[80,256]{1,0:T(8,128)S(1)}, f32[80,256]{1,0:T(8,128)S(1)}, u32[]{:S(2)}, u32[]{:S(2)}) %collective-permute-start.4) | collective-permute-done | bytes 81952 | tf_op jit(solution)/shard_map/ppermute | solution.py:331
  24.2 0.0 collective-permute-start.6
  24.2 2.6 %collective-permute-done.5.refs_2_ = f32[48,256]{1,0:T(8,128)S(1)} collective-permute-done((f32[48,256]{1,0:T(8,128)S(1)}, f32[48,256]{1,0:T(8,128)S(1)}, u32[]{:S(2)}, u32[]{:S(2)}) %collective-permute-start.5) | collective-permute-done | bytes 49184 | tf_op jit(solution)/shard_map/ppermute | solution.py:309
  26.8 0.0 collective-permute-start.7
  26.9 0.0 collective-permute-done.6.refs_3_
  26.9 2.9 %shard_map.61.refs_5_ = f32[64,64]{1,0:T(8,128)S(1)} custom-call(f32[80,256]{1,0:T(8,128)S(1)} %get-tuple-element.31.refs_0_, f32[80,256]{1,0:T(8,128)S(1)} %collective-permute-done.4.refs_1_, f32[48,256]{1,0:T(8,128)S(1)} %collective-permute-done.5.refs_2_, f32[80,256]{1,0:T(8,128)S(1)} %collective-permute-done.6.refs_3_, ...), custom_call_target="tpu_custom_call" | custom-call | bytes 4194304 | tf_op jit(solution)/shard_map/pallas_call | solution.py:299
  29.8 0.0 collective-permute-done.7.refs_4_
  29.8 0.9 shard_map.62.refs_0_
  30.7 1.6 %collective-permute-start.10 = (f32[80,256]{1,0:T(8,128)S(1)}, f32[80,256]{1,0:T(8,128)S(1)}, u32[]{:S(2)}, u32[]{:S(2)}) collective-permute-start(f32[80,256]{1,0:T(8,128)S(1)} %shard_map.62.refs_0_), channel_id=1, source_target_pairs={{0,3},{1,2},{2,1},{3,0},{4,7},{5,6},{6,5},{7,4},{8,11},{9,10},{10,... | collective-permute-start | bytes 245768 | tf_op jit(solution)/shard_map/ppermute | solution.py:309
  32.2 1.0 %collective-permute-start.9 = (f32[80,256]{1,0:T(8,128)S(1)}, f32[80,256]{1,0:T(8,128)S(1)}, u32[]{:S(2)}, u32[]{:S(2)}) collective-permute-start(f32[80,256]{1,0:T(8,128)S(1)} %shard_map.62.refs_0_), channel_id=1, source_target_pairs={{0,2},{1,3},{2,0},{3,1},{4,6},{5,7},{6,4},{7,5},{8,10},{9,11},{10,... | collective-permute-start | bytes 245768 | tf_op jit(solution)/shard_map/ppermute | solution.py:309
  33.2 1.0 %collective-permute-start.8 = (f32[80,256]{1,0:T(8,128)S(1)}, f32[80,256]{1,0:T(8,128)S(1)}, u32[]{:S(2)}, u32[]{:S(2)}) collective-permute-start(f32[80,256]{1,0:T(8,128)S(1)} %shard_map.62.refs_0_), channel_id=1, source_target_pairs={{0,1},{1,0},{2,3},{3,2},{4,5},{5,4},{6,7},{7,6},{8,9},{9,8},{10,11... | collective-permute-start | bytes 245768 | tf_op jit(solution)/shard_map/ppermute | solution.py:309
  34.2 2.5 %collective-permute-done.10.refs_3_ = f32[80,256]{1,0:T(8,128)S(1)} collective-permute-done((f32[80,256]{1,0:T(8,128)S(1)}, f32[80,256]{1,0:T(8,128)S(1)}, u32[]{:S(2)}, u32[]{:S(2)}) %collective-permute-start.10) | collective-permute-done | bytes 81952 | tf_op jit(solution)/shard_map/ppermute | solution.py:309
  36.7 1.5 %collective-permute-done.9.refs_2_ = f32[80,256]{1,0:T(8,128)S(1)} collective-permute-done((f32[80,256]{1,0:T(8,128)S(1)}, f32[80,256]{1,0:T(8,128)S(1)}, u32[]{:S(2)}, u32[]{:S(2)}) %collective-permute-start.9) | collective-permute-done | bytes 81952 | tf_op jit(solution)/shard_map/ppermute | solution.py:309
  38.2 0.1 collective-permute-done.8.refs_1_
  38.3 6.1 %shard_map.63.refs_0_ = f32[80,256]{1,0:T(8,128)S(1)} custom-call(f32[80,256]{1,0:T(8,128)S(1)} %shard_map.62.refs_0_, f32[80,256]{1,0:T(8,128)S(1)} %collective-permute-done.8.refs_1_, f32[80,256]{1,0:T(8,128)S(1)} %collective-permute-done.9.refs_2_, f32[80,256]{1,0:T(8,128)S(1)} %collective-permute-done.10.refs_3_, ...), custom_call_target="tpu_custom_call" | custom-call | tf_op jit(solution)/shard_map/pallas_call | solution.py:299
  44.5 0.1 collective-permute-start.11
  44.6 1.3 %collective-permute-done.11.refs_1_ = f32[80,256]{1,0:T(8,128)S(1)} collective-permute-done((f32[80,256]{1,0:T(8,128)S(1)}, f32[80,256]{1,0:T(8,128)S(1)}, u32[]{:S(2)}, u32[]{:S(2)}) %collective-permute-start.11) | collective-permute-done | bytes 81952 | tf_op jit(solution)/shard_map/ppermute | solution.py:309
  45.8 0.3 collective-permute-start.12
  46.1 3.4 %collective-permute-start.13 = (f32[48,256]{1,0:T(8,128)S(1)}, f32[48,256]{1,0:T(8,128)S(1)}, u32[]{:S(2)}, u32[]{:S(2)}) collective-permute-start(f32[48,256]{1,0:T(8,128)S(1)} %get-tuple-element.36), channel_id=1, source_target_pairs={{0,24},{4,28},{8,16},{12,20},{16,8},{20,12},{24,0},{28,4},{1,25},{... | collective-permute-start | bytes 147464 | tf_op jit(solution)/shard_map/ppermute | solution.py:309
  49.5 1.2 %collective-permute-done.12.refs_1_ = f32[80,256]{1,0:T(8,128)S(1)} collective-permute-done((f32[80,256]{1,0:T(8,128)S(1)}, f32[80,256]{1,0:T(8,128)S(1)}, u32[]{:S(2)}, u32[]{:S(2)}) %collective-permute-start.12) | collective-permute-done | bytes 81952 | tf_op jit(solution)/shard_map/ppermute | solution.py:331
  50.7 0.7 collective-permute-start.14
  51.5 1.2 %collective-permute-done.13.refs_2_ = f32[48,256]{1,0:T(8,128)S(1)} collective-permute-done((f32[48,256]{1,0:T(8,128)S(1)}, f32[48,256]{1,0:T(8,128)S(1)}, u32[]{:S(2)}, u32[]{:S(2)}) %collective-permute-start.13) | collective-permute-done | bytes 49184 | tf_op jit(solution)/shard_map/ppermute | solution.py:309
  52.7 0.3 collective-permute-start.15
  52.9 0.0 collective-permute-done.14.refs_3_
  52.9 3.9 %shard_map.65.refs_5_ = f32[64,64]{1,0:T(8,128)S(1)} custom-call(f32[80,256]{1,0:T(8,128)S(1)} %get-tuple-element.35.refs_0_, f32[80,256]{1,0:T(8,128)S(1)} %collective-permute-done.12.refs_1_, f32[48,256]{1,0:T(8,128)S(1)} %collective-permute-done.13.refs_2_, f32[80,256]{1,0:T(8,128)S(1)} %collective-permute-done.14.refs_3_, ...), custom_call_target="tpu_custom_call" | custom-call | bytes 4194304 | tf_op jit(solution)/shard_map/pallas_call | solution.py:299
  56.8 0.0 collective-permute-done.15.refs_4_
  56.8 0.9 shard_map.66.refs_0_
  57.8 1.5 %collective-permute-start.18 = (f32[80,256]{1,0:T(8,128)S(1)}, f32[80,256]{1,0:T(8,128)S(1)}, u32[]{:S(2)}, u32[]{:S(2)}) collective-permute-start(f32[80,256]{1,0:T(8,128)S(1)} %shard_map.66.refs_0_), channel_id=1, source_target_pairs={{0,3},{1,2},{2,1},{3,0},{4,7},{5,6},{6,5},{7,4},{8,11},{9,10},{10,... | collective-permute-start | bytes 245768 | tf_op jit(solution)/shard_map/ppermute | solution.py:309
  59.3 0.9 %collective-permute-start.17 = (f32[80,256]{1,0:T(8,128)S(1)}, f32[80,256]{1,0:T(8,128)S(1)}, u32[]{:S(2)}, u32[]{:S(2)}) collective-permute-start(f32[80,256]{1,0:T(8,128)S(1)} %shard_map.66.refs_0_), channel_id=1, source_target_pairs={{0,2},{1,3},{2,0},{3,1},{4,6},{5,7},{6,4},{7,5},{8,10},{9,11},{10,... | collective-permute-start | bytes 245768 | tf_op jit(solution)/shard_map/ppermute | solution.py:309
  60.2 1.1 %collective-permute-start.16 = (f32[80,256]{1,0:T(8,128)S(1)}, f32[80,256]{1,0:T(8,128)S(1)}, u32[]{:S(2)}, u32[]{:S(2)}) collective-permute-start(f32[80,256]{1,0:T(8,128)S(1)} %shard_map.66.refs_0_), channel_id=1, source_target_pairs={{0,1},{1,0},{2,3},{3,2},{4,5},{5,4},{6,7},{7,6},{8,9},{9,8},{10,11... | collective-permute-start | bytes 245768 | tf_op jit(solution)/shard_map/ppermute | solution.py:309
  61.3 2.4 %collective-permute-done.18.refs_3_ = f32[80,256]{1,0:T(8,128)S(1)} collective-permute-done((f32[80,256]{1,0:T(8,128)S(1)}, f32[80,256]{1,0:T(8,128)S(1)}, u32[]{:S(2)}, u32[]{:S(2)}) %collective-permute-start.18) | collective-permute-done | bytes 81952 | tf_op jit(solution)/shard_map/ppermute | solution.py:309
  63.7 1.4 %collective-permute-done.17.refs_2_ = f32[80,256]{1,0:T(8,128)S(1)} collective-permute-done((f32[80,256]{1,0:T(8,128)S(1)}, f32[80,256]{1,0:T(8,128)S(1)}, u32[]{:S(2)}, u32[]{:S(2)}) %collective-permute-start.17) | collective-permute-done | bytes 81952 | tf_op jit(solution)/shard_map/ppermute | solution.py:309
  65.1 6.1 %shard_map.67 = (f32[80,256]{1,0:T(8,128)S(1)}, f32[64,256]{1,0:T(8,128)S(1)}) custom-call(f32[80,256]{1,0:T(8,128)S(1)} %shard_map.66.refs_0_, f32[80,256]{1,0:T(8,128)S(1)} %collective-permute-done.16.refs_1_, f32[80,256]{1,0:T(8,128)S(1)} %collective-permute-done.17.refs_2_, f32[80,256]{1,0:T(8,128)S(1)} %collective-permute-done.18.refs_3_, ...), custom_call_target="tpu_custom_call" | custom-call | tf_op jit(solution)/shard_map/pallas_call | solution.py:299
  71.2 0.1 collective-permute-start.19
  71.3 1.3 %collective-permute-done.19.refs_1_ = f32[80,256]{1,0:T(8,128)S(1)} collective-permute-done((f32[80,256]{1,0:T(8,128)S(1)}, f32[80,256]{1,0:T(8,128)S(1)}, u32[]{:S(2)}, u32[]{:S(2)}) %collective-permute-start.19) | collective-permute-done | bytes 81952 | tf_op jit(solution)/shard_map/ppermute | solution.py:309
  72.6 1.2 %collective-permute-start.20 = (f32[80,256]{1,0:T(8,128)S(1)}, f32[80,256]{1,0:T(8,128)S(1)}, u32[]{:S(2)}, u32[]{:S(2)}) collective-permute-start(f32[80,256]{1,0:T(8,128)S(1)} %get-tuple-element.38.refs_0_), channel_id=1, source_target_pairs={{0,8},{4,20},{8,0},{12,28},{16,24},{20,4},{24,16},{28,12},{1,9},{5... | collective-permute-start | bytes 245768 | tf_op jit(solution)/shard_map/ppermute | solution.py:331
  73.8 2.6 %collective-permute-start.21 = (f32[48,256]{1,0:T(8,128)S(1)}, f32[48,256]{1,0:T(8,128)S(1)}, u32[]{:S(2)}, u32[]{:S(2)}) collective-permute-start(f32[48,256]{1,0:T(8,128)S(1)} %get-tuple-element.39), channel_id=1, source_target_pairs={{0,24},{4,28},{8,16},{12,20},{16,8},{20,12},{24,0},{28,4},{1,25},{... | collective-permute-start | bytes 147464 | tf_op jit(solution)/shard_map/ppermute | solution.py:309
  76.5 1.5 %collective-permute-done.20.refs_1_ = f32[80,256]{1,0:T(8,128)S(1)} collective-permute-done((f32[80,256]{1,0:T(8,128)S(1)}, f32[80,256]{1,0:T(8,128)S(1)}, u32[]{:S(2)}, u32[]{:S(2)}) %collective-permute-start.20) | collective-permute-done | bytes 81952 | tf_op jit(solution)/shard_map/ppermute | solution.py:331
  78.0 0.0 collective-permute-start.22
  78.0 2.3 %collective-permute-done.21.refs_2_ = f32[48,256]{1,0:T(8,128)S(1)} collective-permute-done((f32[48,256]{1,0:T(8,128)S(1)}, f32[48,256]{1,0:T(8,128)S(1)}, u32[]{:S(2)}, u32[]{:S(2)}) %collective-permute-start.21) | collective-permute-done | bytes 49184 | tf_op jit(solution)/shard_map/ppermute | solution.py:309
  80.3 0.0 collective-permute-start.23
  80.3 0.0 collective-permute-done.22.refs_3_
  80.3 3.9 %shard_map.69 = (f32[64,64]{1,0:T(8,128)S(1)}, f32[1,64]{1,0:T(1,128)S(1)}) custom-call(f32[80,256]{1,0:T(8,128)S(1)} %get-tuple-element.38.refs_0_, f32[80,256]{1,0:T(8,128)S(1)} %collective-permute-done.20.refs_1_, f32[48,256]{1,0:T(8,128)S(1)} %collective-permute-done.21.refs_2_, f32[80,256]{1,0:T(8,128)S(1)} %collective-permute-done.22.refs_3_, ...), custom_call_target="tpu_custom_call" | custom-call | bytes 4194304 | tf_op jit(solution)/shard_map/pallas_call | solution.py:299
  84.3 0.3 shard_map.71
  84.6 1.4 %collective-permute-start.26 = (f32[8,128]{1,0:T(8,128)S(1)}, f32[8,128]{1,0:T(8,128)S(1)}, u32[]{:S(2)}, u32[]{:S(2)}) collective-permute-start(f32[8,128]{1,0:T(8,128)S(1)} %get-tuple-element.44.refs_0_), channel_id=1, source_target_pairs={{0,3},{1,2},{2,1},{3,0},{4,7},{5,6},{6,5},{7,4},{8,11},{9,10},{10,... | collective-permute-start | bytes 12296 | tf_op jit(solution)/shard_map/ppermute | solution.py:309
  86.0 0.9 %collective-permute-start.25 = (f32[8,128]{1,0:T(8,128)S(1)}, f32[8,128]{1,0:T(8,128)S(1)}, u32[]{:S(2)}, u32[]{:S(2)}) collective-permute-start(f32[8,128]{1,0:T(8,128)S(1)} %get-tuple-element.44.refs_0_), channel_id=1, source_target_pairs={{0,2},{1,3},{2,0},{3,1},{4,6},{5,7},{6,4},{7,5},{8,10},{9,11},{10,... | collective-permute-start | bytes 12296 | tf_op jit(solution)/shard_map/ppermute | solution.py:309
  87.0 1.1 %collective-permute-start.24 = (f32[8,128]{1,0:T(8,128)S(1)}, f32[8,128]{1,0:T(8,128)S(1)}, u32[]{:S(2)}, u32[]{:S(2)}) collective-permute-start(f32[8,128]{1,0:T(8,128)S(1)} %get-tuple-element.44.refs_0_), channel_id=1, source_target_pairs={{0,1},{1,0},{2,3},{3,2},{4,5},{5,4},{6,7},{7,6},{8,9},{9,8},{10,11... | collective-permute-start | bytes 12296 | tf_op jit(solution)/shard_map/ppermute | solution.py:309
  88.1 0.7 shard_map.70
  88.8 0.3 collective-permute-done.26.refs_3_
  89.1 0.5 collective-permute-done.25.refs_2_
  89.7 0.9 %collective-permute-done.24.refs_1_ = f32[8,128]{1,0:T(8,128)S(1)} collective-permute-done((f32[8,128]{1,0:T(8,128)S(1)}, f32[8,128]{1,0:T(8,128)S(1)}, u32[]{:S(2)}, u32[]{:S(2)}) %collective-permute-start.24) | collective-permute-done | bytes 4128 | tf_op jit(solution)/shard_map/ppermute | solution.py:309
  90.6 0.7 shard_map.72
  (8 shorter events, 0.1 us)
Async XLA Ops:
  4.2 6.5 %collective-permute-start.2 = (f32[80,256]{1,0:T(8,128)S(1)}, f32[80,256]{1,0:T(8,128)S(1)}, u32[]{:S(2)}, u32[]{:S(2)}) collective-permute-start(f32[80,256]{1,0:T(8,128)S(1)} %get-tuple-element.26.refs_0_), channel_id=1, source_target_pairs={{0,3},{1,2},{2,1},{3,0},{4,7},{5,6},{6,5},{7,4},{8,11},{9,10},{10,... | collective-permute-start | bytes 245768 | tf_op jit(solution)/shard_map/ppermute | solution.py:309
  8.1 4.4 %collective-permute-start.1 = (f32[80,256]{1,0:T(8,128)S(1)}, f32[80,256]{1,0:T(8,128)S(1)}, u32[]{:S(2)}, u32[]{:S(2)}) collective-permute-start(f32[80,256]{1,0:T(8,128)S(1)} %get-tuple-element.26.refs_0_), channel_id=1, source_target_pairs={{0,2},{1,3},{2,0},{3,1},{4,6},{5,7},{6,4},{7,5},{8,10},{9,11},{10,... | collective-permute-start | bytes 245768 | tf_op jit(solution)/shard_map/ppermute | solution.py:309
  8.6 4.4 %collective-permute-start = (f32[80,256]{1,0:T(8,128)S(1)}, f32[80,256]{1,0:T(8,128)S(1)}, u32[]{:S(2)}, u32[]{:S(2)}) collective-permute-start(f32[80,256]{1,0:T(8,128)S(1)} %get-tuple-element.26.refs_0_), channel_id=1, source_target_pairs={{0,1},{1,0},{2,3},{3,2},{4,5},{5,4},{6,7},{7,6},{8,9},{9,8},{10,11... | collective-permute-start | bytes 245768 | tf_op jit(solution)/shard_map/ppermute | solution.py:309
  17.5 1.3 %collective-permute-start.3 = (f32[80,256]{1,0:T(8,128)S(1)}, f32[80,256]{1,0:T(8,128)S(1)}, u32[]{:S(2)}, u32[]{:S(2)}) collective-permute-start(f32[80,256]{1,0:T(8,128)S(1)} %shard_map.59.refs_0_), channel_id=1, source_target_pairs={{0,4},{4,0},{8,12},{12,8},{16,20},{20,16},{24,28},{28,24},{1,5},{5... | collective-permute-start | bytes 245768 | tf_op jit(solution)/shard_map/ppermute | solution.py:309
  18.9 5.4 %collective-permute-start.4 = (f32[80,256]{1,0:T(8,128)S(1)}, f32[80,256]{1,0:T(8,128)S(1)}, u32[]{:S(2)}, u32[]{:S(2)}) collective-permute-start(f32[80,256]{1,0:T(8,128)S(1)} %get-tuple-element.31.refs_0_), channel_id=1, source_target_pairs={{0,8},{4,20},{8,0},{12,28},{16,24},{20,4},{24,16},{28,12},{1,9},{5... | collective-permute-start | bytes 245768 | tf_op jit(solution)/shard_map/ppermute | solution.py:331
  20.5 6.3 %collective-permute-start.5 = (f32[48,256]{1,0:T(8,128)S(1)}, f32[48,256]{1,0:T(8,128)S(1)}, u32[]{:S(2)}, u32[]{:S(2)}) collective-permute-start(f32[48,256]{1,0:T(8,128)S(1)} %get-tuple-element.32), channel_id=1, source_target_pairs={{0,24},{4,28},{8,16},{12,20},{16,8},{20,12},{24,0},{28,4},{1,25},{... | collective-permute-start | bytes 147464 | tf_op jit(solution)/shard_map/ppermute | solution.py:309
  24.2 2.6 %collective-permute-start.6 = (f32[80,256]{1,0:T(8,128)S(1)}, f32[80,256]{1,0:T(8,128)S(1)}, u32[]{:S(2)}, u32[]{:S(2)}) collective-permute-start(f32[80,256]{1,0:T(8,128)S(1)} %collective-permute-done.4.refs_1_), channel_id=1, source_target_pairs={{0,4},{4,0},{8,12},{12,8},{16,20},{20,16},{24,28},{28,24},{1,5},{5... | collective-permute-start | bytes 245768 | tf_op jit(solution)/shard_map/ppermute | solution.py:309
  26.8 2.9 %collective-permute-start.7 = (f32[32,256]{1,0:T(8,128)S(1)}, f32[32,256]{1,0:T(8,128)S(1)}, u32[]{:S(2)}, u32[]{:S(2)}) collective-permute-start(f32[32,256]{1,0:T(8,128)S(1)} %slice.12), channel_id=1, source_target_pairs={{0,4},{4,0},{8,12},{12,8},{16,20},{20,16},{24,28},{28,24},{1,5},{5... | collective-permute-start | bytes 98312 | tf_op jit(solution)/shard_map/ppermute | solution.py:309
  30.7 6.0 %collective-permute-start.10 = (f32[80,256]{1,0:T(8,128)S(1)}, f32[80,256]{1,0:T(8,128)S(1)}, u32[]{:S(2)}, u32[]{:S(2)}) collective-permute-start(f32[80,256]{1,0:T(8,128)S(1)} %shard_map.62.refs_0_), channel_id=1, source_target_pairs={{0,3},{1,2},{2,1},{3,0},{4,7},{5,6},{6,5},{7,4},{8,11},{9,10},{10,... | collective-permute-start | bytes 245768 | tf_op jit(solution)/shard_map/ppermute | solution.py:309
  32.2 6.0 %collective-permute-start.9 = (f32[80,256]{1,0:T(8,128)S(1)}, f32[80,256]{1,0:T(8,128)S(1)}, u32[]{:S(2)}, u32[]{:S(2)}) collective-permute-start(f32[80,256]{1,0:T(8,128)S(1)} %shard_map.62.refs_0_), channel_id=1, source_target_pairs={{0,2},{1,3},{2,0},{3,1},{4,6},{5,7},{6,4},{7,5},{8,10},{9,11},{10,... | collective-permute-start | bytes 245768 | tf_op jit(solution)/shard_map/ppermute | solution.py:309
  33.2 5.1 %collective-permute-start.8 = (f32[80,256]{1,0:T(8,128)S(1)}, f32[80,256]{1,0:T(8,128)S(1)}, u32[]{:S(2)}, u32[]{:S(2)}) collective-permute-start(f32[80,256]{1,0:T(8,128)S(1)} %shard_map.62.refs_0_), channel_id=1, source_target_pairs={{0,1},{1,0},{2,3},{3,2},{4,5},{5,4},{6,7},{7,6},{8,9},{9,8},{10,11... | collective-permute-start | bytes 245768 | tf_op jit(solution)/shard_map/ppermute | solution.py:309
  44.5 1.3 %collective-permute-start.11 = (f32[80,256]{1,0:T(8,128)S(1)}, f32[80,256]{1,0:T(8,128)S(1)}, u32[]{:S(2)}, u32[]{:S(2)}) collective-permute-start(f32[80,256]{1,0:T(8,128)S(1)} %shard_map.63.refs_0_), channel_id=1, source_target_pairs={{0,4},{4,0},{8,12},{12,8},{16,20},{20,16},{24,28},{28,24},{1,5},{5... | collective-permute-start | bytes 245768 | tf_op jit(solution)/shard_map/ppermute | solution.py:309
  45.8 4.9 %collective-permute-start.12 = (f32[80,256]{1,0:T(8,128)S(1)}, f32[80,256]{1,0:T(8,128)S(1)}, u32[]{:S(2)}, u32[]{:S(2)}) collective-permute-start(f32[80,256]{1,0:T(8,128)S(1)} %get-tuple-element.35.refs_0_), channel_id=1, source_target_pairs={{0,8},{4,20},{8,0},{12,28},{16,24},{20,4},{24,16},{28,12},{1,9},{5... | collective-permute-start | bytes 245768 | tf_op jit(solution)/shard_map/ppermute | solution.py:331
  46.1 6.5 %collective-permute-start.13 = (f32[48,256]{1,0:T(8,128)S(1)}, f32[48,256]{1,0:T(8,128)S(1)}, u32[]{:S(2)}, u32[]{:S(2)}) collective-permute-start(f32[48,256]{1,0:T(8,128)S(1)} %get-tuple-element.36), channel_id=1, source_target_pairs={{0,24},{4,28},{8,16},{12,20},{16,8},{20,12},{24,0},{28,4},{1,25},{... | collective-permute-start | bytes 147464 | tf_op jit(solution)/shard_map/ppermute | solution.py:309
  50.7 2.2 %collective-permute-start.14 = (f32[80,256]{1,0:T(8,128)S(1)}, f32[80,256]{1,0:T(8,128)S(1)}, u32[]{:S(2)}, u32[]{:S(2)}) collective-permute-start(f32[80,256]{1,0:T(8,128)S(1)} %collective-permute-done.12.refs_1_), channel_id=1, source_target_pairs={{0,4},{4,0},{8,12},{12,8},{16,20},{20,16},{24,28},{28,24},{1,5},{5... | collective-permute-start | bytes 245768 | tf_op jit(solution)/shard_map/ppermute | solution.py:309
  52.7 4.2 %collective-permute-start.15 = (f32[32,256]{1,0:T(8,128)S(1)}, f32[32,256]{1,0:T(8,128)S(1)}, u32[]{:S(2)}, u32[]{:S(2)}) collective-permute-start(f32[32,256]{1,0:T(8,128)S(1)} %slice.13), channel_id=1, source_target_pairs={{0,4},{4,0},{8,12},{12,8},{16,20},{20,16},{24,28},{28,24},{1,5},{5... | collective-permute-start | bytes 98312 | tf_op jit(solution)/shard_map/ppermute | solution.py:309
  57.8 5.9 %collective-permute-start.18 = (f32[80,256]{1,0:T(8,128)S(1)}, f32[80,256]{1,0:T(8,128)S(1)}, u32[]{:S(2)}, u32[]{:S(2)}) collective-permute-start(f32[80,256]{1,0:T(8,128)S(1)} %shard_map.66.refs_0_), channel_id=1, source_target_pairs={{0,3},{1,2},{2,1},{3,0},{4,7},{5,6},{6,5},{7,4},{8,11},{9,10},{10,... | collective-permute-start | bytes 245768 | tf_op jit(solution)/shard_map/ppermute | solution.py:309
  59.3 5.8 %collective-permute-start.17 = (f32[80,256]{1,0:T(8,128)S(1)}, f32[80,256]{1,0:T(8,128)S(1)}, u32[]{:S(2)}, u32[]{:S(2)}) collective-permute-start(f32[80,256]{1,0:T(8,128)S(1)} %shard_map.66.refs_0_), channel_id=1, source_target_pairs={{0,2},{1,3},{2,0},{3,1},{4,6},{5,7},{6,4},{7,5},{8,10},{9,11},{10,... | collective-permute-start | bytes 245768 | tf_op jit(solution)/shard_map/ppermute | solution.py:309
  60.2 4.9 %collective-permute-start.16 = (f32[80,256]{1,0:T(8,128)S(1)}, f32[80,256]{1,0:T(8,128)S(1)}, u32[]{:S(2)}, u32[]{:S(2)}) collective-permute-start(f32[80,256]{1,0:T(8,128)S(1)} %shard_map.66.refs_0_), channel_id=1, source_target_pairs={{0,1},{1,0},{2,3},{3,2},{4,5},{5,4},{6,7},{7,6},{8,9},{9,8},{10,11... | collective-permute-start | bytes 245768 | tf_op jit(solution)/shard_map/ppermute | solution.py:309
  71.2 1.3 %collective-permute-start.19 = (f32[80,256]{1,0:T(8,128)S(1)}, f32[80,256]{1,0:T(8,128)S(1)}, u32[]{:S(2)}, u32[]{:S(2)}) collective-permute-start(f32[80,256]{1,0:T(8,128)S(1)} %get-tuple-element.37.refs_0_), channel_id=1, source_target_pairs={{0,4},{4,0},{8,12},{12,8},{16,20},{20,16},{24,28},{28,24},{1,5},{5... | collective-permute-start | bytes 245768 | tf_op jit(solution)/shard_map/ppermute | solution.py:309
  72.6 5.4 %collective-permute-start.20 = (f32[80,256]{1,0:T(8,128)S(1)}, f32[80,256]{1,0:T(8,128)S(1)}, u32[]{:S(2)}, u32[]{:S(2)}) collective-permute-start(f32[80,256]{1,0:T(8,128)S(1)} %get-tuple-element.38.refs_0_), channel_id=1, source_target_pairs={{0,8},{4,20},{8,0},{12,28},{16,24},{20,4},{24,16},{28,12},{1,9},{5... | collective-permute-start | bytes 245768 | tf_op jit(solution)/shard_map/ppermute | solution.py:331
  73.8 6.5 %collective-permute-start.21 = (f32[48,256]{1,0:T(8,128)S(1)}, f32[48,256]{1,0:T(8,128)S(1)}, u32[]{:S(2)}, u32[]{:S(2)}) collective-permute-start(f32[48,256]{1,0:T(8,128)S(1)} %get-tuple-element.39), channel_id=1, source_target_pairs={{0,24},{4,28},{8,16},{12,20},{16,8},{20,12},{24,0},{28,4},{1,25},{... | collective-permute-start | bytes 147464 | tf_op jit(solution)/shard_map/ppermute | solution.py:309
  78.0 2.3 %collective-permute-start.22 = (f32[80,256]{1,0:T(8,128)S(1)}, f32[80,256]{1,0:T(8,128)S(1)}, u32[]{:S(2)}, u32[]{:S(2)}) collective-permute-start(f32[80,256]{1,0:T(8,128)S(1)} %collective-permute-done.20.refs_1_), channel_id=1, source_target_pairs={{0,4},{4,0},{8,12},{12,8},{16,20},{20,16},{24,28},{28,24},{1,5},{5... | collective-permute-start | bytes 245768 | tf_op jit(solution)/shard_map/ppermute | solution.py:309
  80.3 3.9 %collective-permute-start.23 = (f32[32,256]{1,0:T(8,128)S(1)}, f32[32,256]{1,0:T(8,128)S(1)}, u32[]{:S(2)}, u32[]{:S(2)}) collective-permute-start(f32[32,256]{1,0:T(8,128)S(1)} %slice.14), channel_id=1, source_target_pairs={{0,4},{4,0},{8,12},{12,8},{16,20},{20,16},{24,28},{28,24},{1,5},{5... | collective-permute-start | bytes 98312 | tf_op jit(solution)/shard_map/ppermute | solution.py:309
  84.6 4.5 %collective-permute-start.26 = (f32[8,128]{1,0:T(8,128)S(1)}, f32[8,128]{1,0:T(8,128)S(1)}, u32[]{:S(2)}, u32[]{:S(2)}) collective-permute-start(f32[8,128]{1,0:T(8,128)S(1)} %get-tuple-element.44.refs_0_), channel_id=1, source_target_pairs={{0,3},{1,2},{2,1},{3,0},{4,7},{5,6},{6,5},{7,4},{8,11},{9,10},{10,... | collective-permute-start | bytes 12296 | tf_op jit(solution)/shard_map/ppermute | solution.py:309
  86.0 3.6 %collective-permute-start.25 = (f32[8,128]{1,0:T(8,128)S(1)}, f32[8,128]{1,0:T(8,128)S(1)}, u32[]{:S(2)}, u32[]{:S(2)}) collective-permute-start(f32[8,128]{1,0:T(8,128)S(1)} %get-tuple-element.44.refs_0_), channel_id=1, source_target_pairs={{0,2},{1,3},{2,0},{3,1},{4,6},{5,7},{6,4},{7,5},{8,10},{9,11},{10,... | collective-permute-start | bytes 12296 | tf_op jit(solution)/shard_map/ppermute | solution.py:309
  87.0 3.6 %collective-permute-start.24 = (f32[8,128]{1,0:T(8,128)S(1)}, f32[8,128]{1,0:T(8,128)S(1)}, u32[]{:S(2)}, u32[]{:S(2)}) collective-permute-start(f32[8,128]{1,0:T(8,128)S(1)} %get-tuple-element.44.refs_0_), channel_id=1, source_target_pairs={{0,1},{1,0},{2,3},{3,2},{4,5},{5,4},{6,7},{7,6},{8,9},{9,8},{10,11... | collective-permute-start | bytes 12296 | tf_op jit(solution)/shard_map/ppermute | solution.py:309

commit v3 on v2

--- a/solution.py
+++ b/solution.py
@@ -227,14 +227,15 @@
         scales_ref[0][...] = scales[0]
     outer = RELAX * scales[1] / column
     total, power = inverse_series(error, mask, 4)
-    inverse_ref[...] = outer * total
+    inverse_ref[:rank] = outer * total
     roots = 1.0 / jnp.sqrt(column), jnp.sqrt(row)
     rest = jnp.sum(jnp.square(power * roots[0] * roots[1]))
+    inverse_ref[rank:] = jnp.full((8, rank), rest, jnp.float32)
 
     @pl.when(jnp.logical_not(rest <= TOLERANCE))
     def _():
         symmetric = error * roots[0] * roots[1]
-        inverse_ref[...] = (outer / roots[0]) * careful_inverse(symmetric, mask, *scratch) / roots[1]
+        inverse_ref[:rank] = (outer / roots[0]) * careful_inverse(symmetric, mask, *scratch) / roots[1]
 
 
 def left_kernel(pieces_count, count, normalized, last, *refs):
@@ -268,16 +269,25 @@
 
 def right_kernel(last, *refs):
     trades, inverse_ref, refs, full_ref = refs[:5], refs[5], refs[6:-1], refs[-1]
-    rank = inverse_ref.shape[0]
-    solved = split_dot(split(inverse_ref[...]), split(traded_sum(rank, *trades, full_ref)))
-    if last:
-        solved_ref, squares_ref = refs
-        solved_ref[...] = solved
-        squares = jnp.sum(solved * solved, axis=1, keepdims=True)
-        row = jnp.sum(jnp.where(identity_mask(rank), squares, 0.0), axis=0, keepdims=True)
-        squares_ref[...] = jnp.concatenate([row, row], axis=1) * jnp.ones((8, 1), jnp.float32)
-    else:
+    rank = inverse_ref.shape[1]
+    inverse = inverse_ref[:rank]
+    summed = traded_sum(rank, *trades, full_ref)
+
+    full_ref[0] = split_dot(split(inverse), split(summed))
+
+    @pl.when(jnp.logical_not(jnp.max(inverse_ref[rank:]) <= TOLERANCE))
+    def _():
+        full_ref[0] = exact_dot(inverse, summed)
+
+    solved = full_ref[0]
+    if not last:
         pack(solved, *refs)
+        return
+    solved_ref, squares_ref = refs
+    solved_ref[...] = solved
+    squares = jnp.sum(solved * solved, axis=1, keepdims=True)
+    row = jnp.sum(jnp.where(identity_mask(rank), squares, 0.0), axis=0, keepdims=True)
+    squares_ref[...] = jnp.concatenate([row, row], axis=1) * jnp.ones((8, 1), jnp.float32)
 
 
 def result_kernel(scales_ref, solved_ref, result_ref, out_ref):
@@ -287,10 +297,19 @@
     out_ref[...] = row
 
 
-def finish_kernel(pieces_count, count, *refs):
-    pieces, (scales_a_ref, solved_ref, result_ref, scales_ref) = refs[:pieces_count], refs[pieces_count:]
+def shared_sum(own_ref, got_ref, far_ref, swapped_ref):
+    got, swapped, first = got_ref[...], swapped_ref[...], own_core() == 0
+    return (own_ref[...] + jnp.where(first, got, swapped)) + (jnp.where(first, swapped, got) + far_ref[...])
+
+
+def shared_kernel(*refs):
+    refs[-1][...] = shared_sum(*refs[:-1])
+
+
+def finish_kernel(count, *refs):
+    pieces, (scales_a_ref, solved_ref, result_ref, scales_ref) = refs[:4], refs[4:]
     rank = solved_ref.shape[0]
-    row = jnp.sqrt(tree_sum([ref[...] for ref in pieces])[0:1, :rank] / count + EPSILON)
+    row = jnp.sqrt(shared_sum(*pieces)[0:1, :rank] / count + EPSILON)
     result_ref[...] = solved_ref[...] / jnp.sum(jnp.where(identity_mask(rank), row, 0.0), axis=1, keepdims=True)
     scales_ref[...] = jnp.concatenate([scales_a_ref[...], row], axis=0)
 
@@ -332,6 +351,21 @@
         pieces = (x, got, half, swap(got, axis, 1), swap(half[: rank // 2], axis, 1))
         stride *= 4
     return pieces
+
+
+def exchange_shared(x, axis, core_axis):
+    size, cores, stride = lax.axis_size(axis), lax.axis_size(core_axis), 1
+    while True:
+        far = swap(x, axis, 3 * stride)
+        pairs = [
+            (d * size + e, d * size + (e ^ (stride << d % 2))) for d in range(cores) for e in range(size)
+        ]
+        got = lax.ppermute(x, (core_axis, axis), pairs)
+        pieces = (x, got, far, swap(got, core_axis, 1))
+        stride *= 4
+        if stride >= size:
+            return pieces
+        x = call(shared_kernel, x, *pieces)
 
 
 def shards(tensor, factor_b, factor_c):
@@ -368,7 +402,7 @@
         partial, *solved_a = call(kernel, outs, *pieces, gram_c, columns, high, low, scratch=scratch)
         pieces = exchange_by_cores(partial, "row", rank)
         kernel = functools.partial(invert_kernel, rows_all)
-        outs = (f32((rank, rank)), f32((1, rank))) if last else (f32((rank, rank)),)
+        outs = (f32((rank + 8, rank)), f32((1, rank))) if last else (f32((rank + 8, rank)),)
         inverse, *scales_a = call(kernel, outs, *pieces[:4], gram_c, scratch=scratch, cost_estimate=cost)
         kernel = functools.partial(right_kernel, last)
         if not last:
@@ -377,9 +411,9 @@
             )
         else:
             solved_b, squares = call(kernel, (f32(right), f32((8, 2 * rank))), *pieces, inverse, scratch=full)
-    pieces = exchange(squares, "col")
+    pieces = exchange_shared(squares, "col", "row")
     result_a, scales_a = call(result_kernel, (f32(left), f32((1, rank))), *scales_a, *solved_a, cost_estimate=cost)
-    kernel = functools.partial(finish_kernel, len(pieces), cols_all)
+    kernel = functools.partial(finish_kernel, cols_all)
     result_b, scales = call(kernel, (f32(right), f32((2, rank))), *pieces, scales_a, solved_b)
     return result_a, result_b, scales
 

time: 92.2 us -> 92.8 us (level); the launches traced: 91.3 us -> 93 us
  Pallas kernels: 34.6 us -> 36.8 us
    pallas_call x15, Pallas kernels: 34.6 us -> 36.8 us  [call(): pl.pallas_call(kernel, out_shape=out_shape, scratch_shapes=scratch, compi...]
    ppermute x24 -> x23, starting transfers between devices: 24.9 us -> 23.2 us  [swap(): lax.ppermute(x, axis, [(d, d ^ stride) for d in range(lax.axis_size(axis))])]
    ppermute x0 -> x1, waiting for transfers between devices: none -> 0.97 us  [exchange_shared(): got = lax.ppermute(x, (core_axis, axis), pairs)]
    ppermute x24 -> x23, waiting for transfers between devices: 23.8 us -> 23.2 us  [swap(): lax.ppermute(x, axis, [(d, d ^ stride) for d in range(lax.axis_size(axis))])]
  transfers between devices with their start and end apart: 27 -> 27, of which waited for: 20 -> 19; matrix products, arithmetic and copies ran while one was open for 0% -> 0% of each run, Pallas kernels for 13% -> 14%
where the time goes in v3:
time: 92.8 us; the launch traced here: 93 us
  Pallas kernels  36.8 us (40%)
  waiting for transfers between devices  28.1 us (30%)
  starting transfers between devices  27.3 us (29%)
    pallas_call x15, Pallas kernels, call(): pl.pallas_call(kernel, out_shape=out_shape, scratch_shapes=scratch, compi...  36.8 us
    ppermute x23, starting transfers between devices, swap(): lax.ppermute(x, axis, [(d, d ^ stride) for d in range(lax.axis_size(axis))])  23.2 us
    ppermute x23, waiting for transfers between devices, swap(): lax.ppermute(x, axis, [(d, d ^ stride) for d in range(lax.axis_size(axis))])  23.2 us
    ppermute x3, waiting for transfers between devices, exchange_by_cores(): lax.ppermute(x, axis, [(d, d ^ (stride if d % 2 == 0 else 2 * stride)) fo...  3.98 us
    ppermute x3, starting transfers between devices, exchange_by_cores(): lax.ppermute(x, axis, [(d, d ^ (stride if d % 2 == 0 else 2 * stride)) fo...  3.18 us
  transfers between devices with their start and end apart: 27, of which 19 were waited for; matrix products, arithmetic and copies ran while one was open for 0% of the time, Pallas kernels for 14%

profile of v3, /device:TPU:0, one launch (start us, length us, event | category | flops | bytes accessed | tf_op | source)
XLA Modules:
  0.0 93.0 jit_solution(7263021536527693976)
XLA Ops:
  0.6 3.6 %shard_map.58 = (bf16[16,256,256]{2,1,0:T(8,128)(2,1)S(1)}, bf16[16,256,256]{2,1,0:T(8,128)(2,1)S(1)}, bf16[16,256,256]{2,1,0:T(8,128)(2,1)S(1)}, bf16[16,256,25...) custom-call(f32[16,256,256]{2,1,0:T(8,128)} %tensor_hbm.1, ...), custom_call_target="tpu_custom_call" | custom-call | tf_op jit(solution)/shard_map/pallas_call | solution.py:318
  4.2 4.0 %collective-permute-start.2 = (f32[80,256]{1,0:T(8,128)S(1)}, f32[80,256]{1,0:T(8,128)S(1)}, u32[]{:S(2)}, u32[]{:S(2)}) collective-permute-start(f32[80,256]{1,0:T(8,128)S(1)} %get-tuple-element.26.refs_0_), channel_id=1, source_target_pairs={{0,3},{1,2},{2,1},{3,0},{4,7},{5,6},{6,5},{7,4},{8,11},{9,10},{10,... | collective-permute-start | bytes 245768 | tf_op jit(solution)/shard_map/ppermute | solution.py:328
  8.1 0.5 collective-permute-start.1
  8.7 0.1 collective-permute-start
  8.8 1.9 %collective-permute-done.2.refs_3_ = f32[80,256]{1,0:T(8,128)S(1)} collective-permute-done((f32[80,256]{1,0:T(8,128)S(1)}, f32[80,256]{1,0:T(8,128)S(1)}, u32[]{:S(2)}, u32[]{:S(2)}) %collective-permute-start.2) | collective-permute-done | bytes 81952 | tf_op jit(solution)/shard_map/ppermute | solution.py:328
  10.7 1.9 %collective-permute-done.1.refs_2_ = f32[80,256]{1,0:T(8,128)S(1)} collective-permute-done((f32[80,256]{1,0:T(8,128)S(1)}, f32[80,256]{1,0:T(8,128)S(1)}, u32[]{:S(2)}, u32[]{:S(2)}) %collective-permute-start.1) | collective-permute-done | bytes 81952 | tf_op jit(solution)/shard_map/ppermute | solution.py:328
  12.6 0.5 collective-permute-done.refs_1_
  13.1 4.4 %shard_map.59.refs_0_ = f32[80,256]{1,0:T(8,128)S(1)} custom-call(f32[80,256]{1,0:T(8,128)S(1)} %get-tuple-element.26.refs_0_, f32[80,256]{1,0:T(8,128)S(1)} %collective-permute-done.refs_1_, f32[80,256]{1,0:T(8,128)S(1)} %collective-permute-done.1.refs_2_, f32[80,256]{1,0:T(8,128)S(1)} %collective-permute-done.2.refs_3_, ...), custom_call_target="tpu_custom_call" | custom-call | tf_op jit(solution)/shard_map/pallas_call | solution.py:318
  17.5 0.1 collective-permute-start.3
  17.6 1.3 %collective-permute-done.3.refs_1_ = f32[80,256]{1,0:T(8,128)S(1)} collective-permute-done((f32[80,256]{1,0:T(8,128)S(1)}, f32[80,256]{1,0:T(8,128)S(1)}, u32[]{:S(2)}, u32[]{:S(2)}) %collective-permute-start.3) | collective-permute-done | bytes 81952 | tf_op jit(solution)/shard_map/ppermute | solution.py:328
  18.9 1.6 %collective-permute-start.4 = (f32[80,256]{1,0:T(8,128)S(1)}, f32[80,256]{1,0:T(8,128)S(1)}, u32[]{:S(2)}, u32[]{:S(2)}) collective-permute-start(f32[80,256]{1,0:T(8,128)S(1)} %get-tuple-element.31.refs_0_), channel_id=1, source_target_pairs={{0,8},{4,20},{8,0},{12,28},{16,24},{20,4},{24,16},{28,12},{1,9},{5... | collective-permute-start | bytes 245768 | tf_op jit(solution)/shard_map/ppermute | solution.py:350
  20.5 2.5 %collective-permute-start.5 = (f32[48,256]{1,0:T(8,128)S(1)}, f32[48,256]{1,0:T(8,128)S(1)}, u32[]{:S(2)}, u32[]{:S(2)}) collective-permute-start(f32[48,256]{1,0:T(8,128)S(1)} %get-tuple-element.32), channel_id=1, source_target_pairs={{0,24},{4,28},{8,16},{12,20},{16,8},{20,12},{24,0},{28,4},{1,25},{... | collective-permute-start | bytes 147464 | tf_op jit(solution)/shard_map/ppermute | solution.py:328
  23.0 1.3 %collective-permute-done.4.refs_1_ = f32[80,256]{1,0:T(8,128)S(1)} collective-permute-done((f32[80,256]{1,0:T(8,128)S(1)}, f32[80,256]{1,0:T(8,128)S(1)}, u32[]{:S(2)}, u32[]{:S(2)}) %collective-permute-start.4) | collective-permute-done | bytes 81952 | tf_op jit(solution)/shard_map/ppermute | solution.py:350
  24.3 0.0 collective-permute-start.6
  24.3 2.6 %collective-permute-done.5.refs_2_ = f32[48,256]{1,0:T(8,128)S(1)} collective-permute-done((f32[48,256]{1,0:T(8,128)S(1)}, f32[48,256]{1,0:T(8,128)S(1)}, u32[]{:S(2)}, u32[]{:S(2)}) %collective-permute-start.5) | collective-permute-done | bytes 49184 | tf_op jit(solution)/shard_map/ppermute | solution.py:328
  26.9 0.0 collective-permute-start.7
  26.9 0.0 collective-permute-done.6.refs_3_
  26.9 3.6 %shard_map.61.refs_5_ = f32[72,64]{1,0:T(8,128)S(1)} custom-call(f32[80,256]{1,0:T(8,128)S(1)} %get-tuple-element.31.refs_0_, f32[80,256]{1,0:T(8,128)S(1)} %collective-permute-done.4.refs_1_, f32[48,256]{1,0:T(8,128)S(1)} %collective-permute-done.5.refs_2_, f32[80,256]{1,0:T(8,128)S(1)} %collective-permute-done.6.refs_3_, ...), custom_call_target="tpu_custom_call" | custom-call | bytes 4194304 | tf_op jit(solution)/shard_map/pallas_call | solution.py:318
  30.5 0.0 collective-permute-done.7.refs_4_
  30.5 1.2 %shard_map.62.refs_0_ = f32[80,256]{1,0:T(8,128)S(1)} custom-call(f32[80,256]{1,0:T(8,128)S(1)} %get-tuple-element.31.refs_0_, f32[80,256]{1,0:T(8,128)S(1)} %collective-permute-done.4.refs_1_, f32[48,256]{1,0:T(8,128)S(1)} %collective-permute-done.5.refs_2_, f32[80,256]{1,0:T(8,128)S(1)} %collective-permute-done.6.refs_3_, ...), custom_call_target="tpu_custom_call" | custom-call | tf_op jit(solution)/shard_map/pallas_call | solution.py:318
  31.7 1.6 %collective-permute-start.10 = (f32[80,256]{1,0:T(8,128)S(1)}, f32[80,256]{1,0:T(8,128)S(1)}, u32[]{:S(2)}, u32[]{:S(2)}) collective-permute-start(f32[80,256]{1,0:T(8,128)S(1)} %shard_map.62.refs_0_), channel_id=1, source_target_pairs={{0,3},{1,2},{2,1},{3,0},{4,7},{5,6},{6,5},{7,4},{8,11},{9,10},{10,... | collective-permute-start | bytes 245768 | tf_op jit(solution)/shard_map/ppermute | solution.py:328
  33.3 1.0 %collective-permute-start.9 = (f32[80,256]{1,0:T(8,128)S(1)}, f32[80,256]{1,0:T(8,128)S(1)}, u32[]{:S(2)}, u32[]{:S(2)}) collective-permute-start(f32[80,256]{1,0:T(8,128)S(1)} %shard_map.62.refs_0_), channel_id=1, source_target_pairs={{0,2},{1,3},{2,0},{3,1},{4,6},{5,7},{6,4},{7,5},{8,10},{9,11},{10,... | collective-permute-start | bytes 245768 | tf_op jit(solution)/shard_map/ppermute | solution.py:328
  34.2 1.0 %collective-permute-start.8 = (f32[80,256]{1,0:T(8,128)S(1)}, f32[80,256]{1,0:T(8,128)S(1)}, u32[]{:S(2)}, u32[]{:S(2)}) collective-permute-start(f32[80,256]{1,0:T(8,128)S(1)} %shard_map.62.refs_0_), channel_id=1, source_target_pairs={{0,1},{1,0},{2,3},{3,2},{4,5},{5,4},{6,7},{7,6},{8,9},{9,8},{10,11... | collective-permute-start | bytes 245768 | tf_op jit(solution)/shard_map/ppermute | solution.py:328
  35.3 2.5 %collective-permute-done.10.refs_3_ = f32[80,256]{1,0:T(8,128)S(1)} collective-permute-done((f32[80,256]{1,0:T(8,128)S(1)}, f32[80,256]{1,0:T(8,128)S(1)}, u32[]{:S(2)}, u32[]{:S(2)}) %collective-permute-start.10) | collective-permute-done | bytes 81952 | tf_op jit(solution)/shard_map/ppermute | solution.py:328
  37.8 1.5 %collective-permute-done.9.refs_2_ = f32[80,256]{1,0:T(8,128)S(1)} collective-permute-done((f32[80,256]{1,0:T(8,128)S(1)}, f32[80,256]{1,0:T(8,128)S(1)}, u32[]{:S(2)}, u32[]{:S(2)}) %collective-permute-start.9) | collective-permute-done | bytes 81952 | tf_op jit(solution)/shard_map/ppermute | solution.py:328
  39.3 0.1 collective-permute-done.8.refs_1_
  39.4 6.1 %shard_map.63.refs_0_ = f32[80,256]{1,0:T(8,128)S(1)} custom-call(f32[80,256]{1,0:T(8,128)S(1)} %shard_map.62.refs_0_, f32[80,256]{1,0:T(8,128)S(1)} %collective-permute-done.8.refs_1_, f32[80,256]{1,0:T(8,128)S(1)} %collective-permute-done.9.refs_2_, f32[80,256]{1,0:T(8,128)S(1)} %collective-permute-done.10.refs_3_, ...), custom_call_target="tpu_custom_call" | custom-call | tf_op jit(solution)/shard_map/pallas_call | solution.py:318
  45.5 0.1 collective-permute-start.11
  45.6 1.3 %collective-permute-done.11.refs_1_ = f32[80,256]{1,0:T(8,128)S(1)} collective-permute-done((f32[80,256]{1,0:T(8,128)S(1)}, f32[80,256]{1,0:T(8,128)S(1)}, u32[]{:S(2)}, u32[]{:S(2)}) %collective-permute-start.11) | collective-permute-done | bytes 81952 | tf_op jit(solution)/shard_map/ppermute | solution.py:328
  46.9 0.3 collective-permute-start.12
  47.2 3.4 %collective-permute-start.13 = (f32[48,256]{1,0:T(8,128)S(1)}, f32[48,256]{1,0:T(8,128)S(1)}, u32[]{:S(2)}, u32[]{:S(2)}) collective-permute-start(f32[48,256]{1,0:T(8,128)S(1)} %get-tuple-element.36), channel_id=1, source_target_pairs={{0,24},{4,28},{8,16},{12,20},{16,8},{20,12},{24,0},{28,4},{1,25},{... | collective-permute-start | bytes 147464 | tf_op jit(solution)/shard_map/ppermute | solution.py:328
  50.5 1.2 %collective-permute-done.12.refs_1_ = f32[80,256]{1,0:T(8,128)S(1)} collective-permute-done((f32[80,256]{1,0:T(8,128)S(1)}, f32[80,256]{1,0:T(8,128)S(1)}, u32[]{:S(2)}, u32[]{:S(2)}) %collective-permute-start.12) | collective-permute-done | bytes 81952 | tf_op jit(solution)/shard_map/ppermute | solution.py:350
  51.7 0.7 collective-permute-start.14
  52.5 1.2 %collective-permute-done.13.refs_2_ = f32[48,256]{1,0:T(8,128)S(1)} collective-permute-done((f32[48,256]{1,0:T(8,128)S(1)}, f32[48,256]{1,0:T(8,128)S(1)}, u32[]{:S(2)}, u32[]{:S(2)}) %collective-permute-start.13) | collective-permute-done | bytes 49184 | tf_op jit(solution)/shard_map/ppermute | solution.py:328
  53.7 0.3 collective-permute-start.15
  53.9 0.0 collective-permute-done.14.refs_3_
  53.9 4.3 %shard_map.65.refs_5_ = f32[72,64]{1,0:T(8,128)S(1)} custom-call(f32[80,256]{1,0:T(8,128)S(1)} %get-tuple-element.35.refs_0_, f32[80,256]{1,0:T(8,128)S(1)} %collective-permute-done.12.refs_1_, f32[48,256]{1,0:T(8,128)S(1)} %collective-permute-done.13.refs_2_, f32[80,256]{1,0:T(8,128)S(1)} %collective-permute-done.14.refs_3_, ...), custom_call_target="tpu_custom_call" | custom-call | bytes 4194304 | tf_op jit(solution)/shard_map/pallas_call | solution.py:318
  58.2 0.0 collective-permute-done.15.refs_4_
  58.2 1.2 %shard_map.66.refs_0_ = f32[80,256]{1,0:T(8,128)S(1)} custom-call(f32[80,256]{1,0:T(8,128)S(1)} %get-tuple-element.35.refs_0_, f32[80,256]{1,0:T(8,128)S(1)} %collective-permute-done.12.refs_1_, f32[48,256]{1,0:T(8,128)S(1)} %collective-permute-done.13.refs_2_, f32[80,256]{1,0:T(8,128)S(1)} %collective-permute-done.14.refs_3_, ...), custom_call_target="tpu_custom_call" | custom-call | tf_op jit(solution)/shard_map/pallas_call | solution.py:318
  59.4 1.5 %collective-permute-start.18 = (f32[80,256]{1,0:T(8,128)S(1)}, f32[80,256]{1,0:T(8,128)S(1)}, u32[]{:S(2)}, u32[]{:S(2)}) collective-permute-start(f32[80,256]{1,0:T(8,128)S(1)} %shard_map.66.refs_0_), channel_id=1, source_target_pairs={{0,3},{1,2},{2,1},{3,0},{4,7},{5,6},{6,5},{7,4},{8,11},{9,10},{10,... | collective-permute-start | bytes 245768 | tf_op jit(solution)/shard_map/ppermute | solution.py:328
  60.9 0.9 %collective-permute-start.17 = (f32[80,256]{1,0:T(8,128)S(1)}, f32[80,256]{1,0:T(8,128)S(1)}, u32[]{:S(2)}, u32[]{:S(2)}) collective-permute-start(f32[80,256]{1,0:T(8,128)S(1)} %shard_map.66.refs_0_), channel_id=1, source_target_pairs={{0,2},{1,3},{2,0},{3,1},{4,6},{5,7},{6,4},{7,5},{8,10},{9,11},{10,... | collective-permute-start | bytes 245768 | tf_op jit(solution)/shard_map/ppermute | solution.py:328
  61.8 1.1 %collective-permute-start.16 = (f32[80,256]{1,0:T(8,128)S(1)}, f32[80,256]{1,0:T(8,128)S(1)}, u32[]{:S(2)}, u32[]{:S(2)}) collective-permute-start(f32[80,256]{1,0:T(8,128)S(1)} %shard_map.66.refs_0_), channel_id=1, source_target_pairs={{0,1},{1,0},{2,3},{3,2},{4,5},{5,4},{6,7},{7,6},{8,9},{9,8},{10,11... | collective-permute-start | bytes 245768 | tf_op jit(solution)/shard_map/ppermute | solution.py:328
  63.0 2.4 %collective-permute-done.18.refs_3_ = f32[80,256]{1,0:T(8,128)S(1)} collective-permute-done((f32[80,256]{1,0:T(8,128)S(1)}, f32[80,256]{1,0:T(8,128)S(1)}, u32[]{:S(2)}, u32[]{:S(2)}) %collective-permute-start.18) | collective-permute-done | bytes 81952 | tf_op jit(solution)/shard_map/ppermute | solution.py:328
  65.4 1.4 %collective-permute-done.17.refs_2_ = f32[80,256]{1,0:T(8,128)S(1)} collective-permute-done((f32[80,256]{1,0:T(8,128)S(1)}, f32[80,256]{1,0:T(8,128)S(1)}, u32[]{:S(2)}, u32[]{:S(2)}) %collective-permute-start.17) | collective-permute-done | bytes 81952 | tf_op jit(solution)/shard_map/ppermute | solution.py:328
  66.7 0.0 collective-permute-done.16.refs_1_
  66.7 6.2 %shard_map.67 = (f32[80,256]{1,0:T(8,128)S(1)}, f32[64,256]{1,0:T(8,128)S(1)}) custom-call(f32[80,256]{1,0:T(8,128)S(1)} %shard_map.66.refs_0_, f32[80,256]{1,0:T(8,128)S(1)} %collective-permute-done.16.refs_1_, f32[80,256]{1,0:T(8,128)S(1)} %collective-permute-done.17.refs_2_, f32[80,256]{1,0:T(8,128)S(1)} %collective-permute-done.18.refs_3_, ...), custom_call_target="tpu_custom_call" | custom-call | tf_op jit(solution)/shard_map/pallas_call | solution.py:318
  72.9 0.1 collective-permute-start.19
  73.0 1.3 %collective-permute-done.19.refs_1_ = f32[80,256]{1,0:T(8,128)S(1)} collective-permute-done((f32[80,256]{1,0:T(8,128)S(1)}, f32[80,256]{1,0:T(8,128)S(1)}, u32[]{:S(2)}, u32[]{:S(2)}) %collective-permute-start.19) | collective-permute-done | bytes 81952 | tf_op jit(solution)/shard_map/ppermute | solution.py:328
  74.3 1.3 %collective-permute-start.20 = (f32[80,256]{1,0:T(8,128)S(1)}, f32[80,256]{1,0:T(8,128)S(1)}, u32[]{:S(2)}, u32[]{:S(2)}) collective-permute-start(f32[80,256]{1,0:T(8,128)S(1)} %get-tuple-element.38.refs_0_), channel_id=1, source_target_pairs={{0,8},{4,20},{8,0},{12,28},{16,24},{20,4},{24,16},{28,12},{1,9},{5... | collective-permute-start | bytes 245768 | tf_op jit(solution)/shard_map/ppermute | solution.py:350
  75.5 2.6 %collective-permute-start.21 = (f32[48,256]{1,0:T(8,128)S(1)}, f32[48,256]{1,0:T(8,128)S(1)}, u32[]{:S(2)}, u32[]{:S(2)}) collective-permute-start(f32[48,256]{1,0:T(8,128)S(1)} %get-tuple-element.39), channel_id=1, source_target_pairs={{0,24},{4,28},{8,16},{12,20},{16,8},{20,12},{24,0},{28,4},{1,25},{... | collective-permute-start | bytes 147464 | tf_op jit(solution)/shard_map/ppermute | solution.py:328
  78.2 1.5 %collective-permute-done.20.refs_1_ = f32[80,256]{1,0:T(8,128)S(1)} collective-permute-done((f32[80,256]{1,0:T(8,128)S(1)}, f32[80,256]{1,0:T(8,128)S(1)}, u32[]{:S(2)}, u32[]{:S(2)}) %collective-permute-start.20) | collective-permute-done | bytes 81952 | tf_op jit(solution)/shard_map/ppermute | solution.py:350
  79.7 0.0 collective-permute-start.22
  79.7 2.3 %collective-permute-done.21.refs_2_ = f32[48,256]{1,0:T(8,128)S(1)} collective-permute-done((f32[48,256]{1,0:T(8,128)S(1)}, f32[48,256]{1,0:T(8,128)S(1)}, u32[]{:S(2)}, u32[]{:S(2)}) %collective-permute-start.21) | collective-permute-done | bytes 49184 | tf_op jit(solution)/shard_map/ppermute | solution.py:328
  82.0 0.0 collective-permute-start.23
  82.0 0.0 collective-permute-done.22.refs_3_
  82.0 4.3 %shard_map.69 = (f32[72,64]{1,0:T(8,128)S(1)}, f32[1,64]{1,0:T(1,128)S(1)}) custom-call(f32[80,256]{1,0:T(8,128)S(1)} %get-tuple-element.38.refs_0_, f32[80,256]{1,0:T(8,128)S(1)} %collective-permute-done.20.refs_1_, f32[48,256]{1,0:T(8,128)S(1)} %collective-permute-done.21.refs_2_, f32[80,256]{1,0:T(8,128)S(1)} %collective-permute-done.22.refs_3_, ...), custom_call_target="tpu_custom_call" | custom-call | bytes 4194304 | tf_op jit(solution)/shard_map/pallas_call | solution.py:318
  86.3 0.5 shard_map.71
  86.8 0.9 collective-permute-start.24
  87.7 1.7 %collective-permute-start.25 = (f32[8,128]{1,0:T(8,128)S(1)}, f32[8,128]{1,0:T(8,128)S(1)}, u32[]{:S(2)}, u32[]{:S(2)}) collective-permute-start(f32[8,128]{1,0:T(8,128)S(1)} %get-tuple-element.44.refs_0_), channel_id=1, source_target_pairs={{0,3},{1,2},{2,1},{3,0},{4,7},{5,6},{6,5},{7,4},{8,11},{9,10},{10,... | collective-permute-start | bytes 12296 | tf_op jit(solution)/shard_map/ppermute | solution.py:328
  89.5 1.0 %collective-permute-done.24.refs_1_ = f32[8,128]{1,0:T(8,128)S(1)} collective-permute-done((f32[8,128]{1,0:T(8,128)S(1)}, f32[8,128]{1,0:T(8,128)S(1)}, u32[]{:S(2)}, u32[]{:S(2)}) %collective-permute-start.24) | collective-permute-done | bytes 4128 | tf_op jit(solution)/shard_map/ppermute | solution.py:363
  90.4 0.7 shard_map.70
  91.2 1.1 %collective-permute-done.25.refs_2_ = f32[8,128]{1,0:T(8,128)S(1)} collective-permute-done((f32[8,128]{1,0:T(8,128)S(1)}, f32[8,128]{1,0:T(8,128)S(1)}, u32[]{:S(2)}, u32[]{:S(2)}) %collective-permute-start.25) | collective-permute-done | bytes 4128 | tf_op jit(solution)/shard_map/ppermute | solution.py:328
  92.2 0.0 collective-permute-done.26.refs_3_
  92.2 0.7 shard_map.72
  (8 shorter events, 0.1 us)
Async XLA Ops:
  4.2 6.5 %collective-permute-start.2 = (f32[80,256]{1,0:T(8,128)S(1)}, f32[80,256]{1,0:T(8,128)S(1)}, u32[]{:S(2)}, u32[]{:S(2)}) collective-permute-start(f32[80,256]{1,0:T(8,128)S(1)} %get-tuple-element.26.refs_0_), channel_id=1, source_target_pairs={{0,3},{1,2},{2,1},{3,0},{4,7},{5,6},{6,5},{7,4},{8,11},{9,10},{10,... | collective-permute-start | bytes 245768 | tf_op jit(solution)/shard_map/ppermute | solution.py:328
  8.1 4.4 %collective-permute-start.1 = (f32[80,256]{1,0:T(8,128)S(1)}, f32[80,256]{1,0:T(8,128)S(1)}, u32[]{:S(2)}, u32[]{:S(2)}) collective-permute-start(f32[80,256]{1,0:T(8,128)S(1)} %get-tuple-element.26.refs_0_), channel_id=1, source_target_pairs={{0,2},{1,3},{2,0},{3,1},{4,6},{5,7},{6,4},{7,5},{8,10},{9,11},{10,... | collective-permute-start | bytes 245768 | tf_op jit(solution)/shard_map/ppermute | solution.py:328
  8.7 4.4 %collective-permute-start = (f32[80,256]{1,0:T(8,128)S(1)}, f32[80,256]{1,0:T(8,128)S(1)}, u32[]{:S(2)}, u32[]{:S(2)}) collective-permute-start(f32[80,256]{1,0:T(8,128)S(1)} %get-tuple-element.26.refs_0_), channel_id=1, source_target_pairs={{0,1},{1,0},{2,3},{3,2},{4,5},{5,4},{6,7},{7,6},{8,9},{9,8},{10,11... | collective-permute-start | bytes 245768 | tf_op jit(solution)/shard_map/ppermute | solution.py:328
  17.5 1.3 %collective-permute-start.3 = (f32[80,256]{1,0:T(8,128)S(1)}, f32[80,256]{1,0:T(8,128)S(1)}, u32[]{:S(2)}, u32[]{:S(2)}) collective-permute-start(f32[80,256]{1,0:T(8,128)S(1)} %shard_map.59.refs_0_), channel_id=1, source_target_pairs={{0,4},{4,0},{8,12},{12,8},{16,20},{20,16},{24,28},{28,24},{1,5},{5... | collective-permute-start | bytes 245768 | tf_op jit(solution)/shard_map/ppermute | solution.py:328
  18.9 5.4 %collective-permute-start.4 = (f32[80,256]{1,0:T(8,128)S(1)}, f32[80,256]{1,0:T(8,128)S(1)}, u32[]{:S(2)}, u32[]{:S(2)}) collective-permute-start(f32[80,256]{1,0:T(8,128)S(1)} %get-tuple-element.31.refs_0_), channel_id=1, source_target_pairs={{0,8},{4,20},{8,0},{12,28},{16,24},{20,4},{24,16},{28,12},{1,9},{5... | collective-permute-start | bytes 245768 | tf_op jit(solution)/shard_map/ppermute | solution.py:350
  20.5 6.3 %collective-permute-start.5 = (f32[48,256]{1,0:T(8,128)S(1)}, f32[48,256]{1,0:T(8,128)S(1)}, u32[]{:S(2)}, u32[]{:S(2)}) collective-permute-start(f32[48,256]{1,0:T(8,128)S(1)} %get-tuple-element.32), channel_id=1, source_target_pairs={{0,24},{4,28},{8,16},{12,20},{16,8},{20,12},{24,0},{28,4},{1,25},{... | collective-permute-start | bytes 147464 | tf_op jit(solution)/shard_map/ppermute | solution.py:328
  24.3 2.6 %collective-permute-start.6 = (f32[80,256]{1,0:T(8,128)S(1)}, f32[80,256]{1,0:T(8,128)S(1)}, u32[]{:S(2)}, u32[]{:S(2)}) collective-permute-start(f32[80,256]{1,0:T(8,128)S(1)} %collective-permute-done.4.refs_1_), channel_id=1, source_target_pairs={{0,4},{4,0},{8,12},{12,8},{16,20},{20,16},{24,28},{28,24},{1,5},{5... | collective-permute-start | bytes 245768 | tf_op jit(solution)/shard_map/ppermute | solution.py:328
  26.9 3.6 %collective-permute-start.7 = (f32[32,256]{1,0:T(8,128)S(1)}, f32[32,256]{1,0:T(8,128)S(1)}, u32[]{:S(2)}, u32[]{:S(2)}) collective-permute-start(f32[32,256]{1,0:T(8,128)S(1)} %slice.12), channel_id=1, source_target_pairs={{0,4},{4,0},{8,12},{12,8},{16,20},{20,16},{24,28},{28,24},{1,5},{5... | collective-permute-start | bytes 98312 | tf_op jit(solution)/shard_map/ppermute | solution.py:328
  31.7 6.1 %collective-permute-start.10 = (f32[80,256]{1,0:T(8,128)S(1)}, f32[80,256]{1,0:T(8,128)S(1)}, u32[]{:S(2)}, u32[]{:S(2)}) collective-permute-start(f32[80,256]{1,0:T(8,128)S(1)} %shard_map.62.refs_0_), channel_id=1, source_target_pairs={{0,3},{1,2},{2,1},{3,0},{4,7},{5,6},{6,5},{7,4},{8,11},{9,10},{10,... | collective-permute-start | bytes 245768 | tf_op jit(solution)/shard_map/ppermute | solution.py:328
  33.3 6.0 %collective-permute-start.9 = (f32[80,256]{1,0:T(8,128)S(1)}, f32[80,256]{1,0:T(8,128)S(1)}, u32[]{:S(2)}, u32[]{:S(2)}) collective-permute-start(f32[80,256]{1,0:T(8,128)S(1)} %shard_map.62.refs_0_), channel_id=1, source_target_pairs={{0,2},{1,3},{2,0},{3,1},{4,6},{5,7},{6,4},{7,5},{8,10},{9,11},{10,... | collective-permute-start | bytes 245768 | tf_op jit(solution)/shard_map/ppermute | solution.py:328
  34.2 5.1 %collective-permute-start.8 = (f32[80,256]{1,0:T(8,128)S(1)}, f32[80,256]{1,0:T(8,128)S(1)}, u32[]{:S(2)}, u32[]{:S(2)}) collective-permute-start(f32[80,256]{1,0:T(8,128)S(1)} %shard_map.62.refs_0_), channel_id=1, source_target_pairs={{0,1},{1,0},{2,3},{3,2},{4,5},{5,4},{6,7},{7,6},{8,9},{9,8},{10,11... | collective-permute-start | bytes 245768 | tf_op jit(solution)/shard_map/ppermute | solution.py:328
  45.5 1.3 %collective-permute-start.11 = (f32[80,256]{1,0:T(8,128)S(1)}, f32[80,256]{1,0:T(8,128)S(1)}, u32[]{:S(2)}, u32[]{:S(2)}) collective-permute-start(f32[80,256]{1,0:T(8,128)S(1)} %shard_map.63.refs_0_), channel_id=1, source_target_pairs={{0,4},{4,0},{8,12},{12,8},{16,20},{20,16},{24,28},{28,24},{1,5},{5... | collective-permute-start | bytes 245768 | tf_op jit(solution)/shard_map/ppermute | solution.py:328
  46.9 4.9 %collective-permute-start.12 = (f32[80,256]{1,0:T(8,128)S(1)}, f32[80,256]{1,0:T(8,128)S(1)}, u32[]{:S(2)}, u32[]{:S(2)}) collective-permute-start(f32[80,256]{1,0:T(8,128)S(1)} %get-tuple-element.35.refs_0_), channel_id=1, source_target_pairs={{0,8},{4,20},{8,0},{12,28},{16,24},{20,4},{24,16},{28,12},{1,9},{5... | collective-permute-start | bytes 245768 | tf_op jit(solution)/shard_map/ppermute | solution.py:350
  47.2 6.5 %collective-permute-start.13 = (f32[48,256]{1,0:T(8,128)S(1)}, f32[48,256]{1,0:T(8,128)S(1)}, u32[]{:S(2)}, u32[]{:S(2)}) collective-permute-start(f32[48,256]{1,0:T(8,128)S(1)} %get-tuple-element.36), channel_id=1, source_target_pairs={{0,24},{4,28},{8,16},{12,20},{16,8},{20,12},{24,0},{28,4},{1,25},{... | collective-permute-start | bytes 147464 | tf_op jit(solution)/shard_map/ppermute | solution.py:328
  51.7 2.2 %collective-permute-start.14 = (f32[80,256]{1,0:T(8,128)S(1)}, f32[80,256]{1,0:T(8,128)S(1)}, u32[]{:S(2)}, u32[]{:S(2)}) collective-permute-start(f32[80,256]{1,0:T(8,128)S(1)} %collective-permute-done.12.refs_1_), channel_id=1, source_target_pairs={{0,4},{4,0},{8,12},{12,8},{16,20},{20,16},{24,28},{28,24},{1,5},{5... | collective-permute-start | bytes 245768 | tf_op jit(solution)/shard_map/ppermute | solution.py:328
  53.7 4.5 %collective-permute-start.15 = (f32[32,256]{1,0:T(8,128)S(1)}, f32[32,256]{1,0:T(8,128)S(1)}, u32[]{:S(2)}, u32[]{:S(2)}) collective-permute-start(f32[32,256]{1,0:T(8,128)S(1)} %slice.13), channel_id=1, source_target_pairs={{0,4},{4,0},{8,12},{12,8},{16,20},{20,16},{24,28},{28,24},{1,5},{5... | collective-permute-start | bytes 98312 | tf_op jit(solution)/shard_map/ppermute | solution.py:328
  59.4 6.0 %collective-permute-start.18 = (f32[80,256]{1,0:T(8,128)S(1)}, f32[80,256]{1,0:T(8,128)S(1)}, u32[]{:S(2)}, u32[]{:S(2)}) collective-permute-start(f32[80,256]{1,0:T(8,128)S(1)} %shard_map.66.refs_0_), channel_id=1, source_target_pairs={{0,3},{1,2},{2,1},{3,0},{4,7},{5,6},{6,5},{7,4},{8,11},{9,10},{10,... | collective-permute-start | bytes 245768 | tf_op jit(solution)/shard_map/ppermute | solution.py:328
  60.9 5.8 %collective-permute-start.17 = (f32[80,256]{1,0:T(8,128)S(1)}, f32[80,256]{1,0:T(8,128)S(1)}, u32[]{:S(2)}, u32[]{:S(2)}) collective-permute-start(f32[80,256]{1,0:T(8,128)S(1)} %shard_map.66.refs_0_), channel_id=1, source_target_pairs={{0,2},{1,3},{2,0},{3,1},{4,6},{5,7},{6,4},{7,5},{8,10},{9,11},{10,... | collective-permute-start | bytes 245768 | tf_op jit(solution)/shard_map/ppermute | solution.py:328
  61.8 4.9 %collective-permute-start.16 = (f32[80,256]{1,0:T(8,128)S(1)}, f32[80,256]{1,0:T(8,128)S(1)}, u32[]{:S(2)}, u32[]{:S(2)}) collective-permute-start(f32[80,256]{1,0:T(8,128)S(1)} %shard_map.66.refs_0_), channel_id=1, source_target_pairs={{0,1},{1,0},{2,3},{3,2},{4,5},{5,4},{6,7},{7,6},{8,9},{9,8},{10,11... | collective-permute-start | bytes 245768 | tf_op jit(solution)/shard_map/ppermute | solution.py:328
  72.9 1.3 %collective-permute-start.19 = (f32[80,256]{1,0:T(8,128)S(1)}, f32[80,256]{1,0:T(8,128)S(1)}, u32[]{:S(2)}, u32[]{:S(2)}) collective-permute-start(f32[80,256]{1,0:T(8,128)S(1)} %get-tuple-element.37.refs_0_), channel_id=1, source_target_pairs={{0,4},{4,0},{8,12},{12,8},{16,20},{20,16},{24,28},{28,24},{1,5},{5... | collective-permute-start | bytes 245768 | tf_op jit(solution)/shard_map/ppermute | solution.py:328
  74.3 5.4 %collective-permute-start.20 = (f32[80,256]{1,0:T(8,128)S(1)}, f32[80,256]{1,0:T(8,128)S(1)}, u32[]{:S(2)}, u32[]{:S(2)}) collective-permute-start(f32[80,256]{1,0:T(8,128)S(1)} %get-tuple-element.38.refs_0_), channel_id=1, source_target_pairs={{0,8},{4,20},{8,0},{12,28},{16,24},{20,4},{24,16},{28,12},{1,9},{5... | collective-permute-start | bytes 245768 | tf_op jit(solution)/shard_map/ppermute | solution.py:350
  75.5 6.5 %collective-permute-start.21 = (f32[48,256]{1,0:T(8,128)S(1)}, f32[48,256]{1,0:T(8,128)S(1)}, u32[]{:S(2)}, u32[]{:S(2)}) collective-permute-start(f32[48,256]{1,0:T(8,128)S(1)} %get-tuple-element.39), channel_id=1, source_target_pairs={{0,24},{4,28},{8,16},{12,20},{16,8},{20,12},{24,0},{28,4},{1,25},{... | collective-permute-start | bytes 147464 | tf_op jit(solution)/shard_map/ppermute | solution.py:328
  79.7 2.4 %collective-permute-start.22 = (f32[80,256]{1,0:T(8,128)S(1)}, f32[80,256]{1,0:T(8,128)S(1)}, u32[]{:S(2)}, u32[]{:S(2)}) collective-permute-start(f32[80,256]{1,0:T(8,128)S(1)} %collective-permute-done.20.refs_1_), channel_id=1, source_target_pairs={{0,4},{4,0},{8,12},{12,8},{16,20},{20,16},{24,28},{28,24},{1,5},{5... | collective-permute-start | bytes 245768 | tf_op jit(solution)/shard_map/ppermute | solution.py:328
  82.0 4.3 %collective-permute-start.23 = (f32[32,256]{1,0:T(8,128)S(1)}, f32[32,256]{1,0:T(8,128)S(1)}, u32[]{:S(2)}, u32[]{:S(2)}) collective-permute-start(f32[32,256]{1,0:T(8,128)S(1)} %slice.14), channel_id=1, source_target_pairs={{0,4},{4,0},{8,12},{12,8},{16,20},{20,16},{24,28},{28,24},{1,5},{5... | collective-permute-start | bytes 98312 | tf_op jit(solution)/shard_map/ppermute | solution.py:328
  86.8 3.6 %collective-permute-start.24 = (f32[8,128]{1,0:T(8,128)S(1)}, f32[8,128]{1,0:T(8,128)S(1)}, u32[]{:S(2)}, u32[]{:S(2)}) collective-permute-start(f32[8,128]{1,0:T(8,128)S(1)} %get-tuple-element.44.refs_0_), channel_id=1, source_target_pairs={{0,1},{1,0},{2,3},{3,2},{4,6},{5,7},{6,4},{7,5},{8,9},{9,8},{10,11... | collective-permute-start | bytes 12296 | tf_op jit(solution)/shard_map/ppermute | solution.py:363
  87.7 4.5 %collective-permute-start.25 = (f32[8,128]{1,0:T(8,128)S(1)}, f32[8,128]{1,0:T(8,128)S(1)}, u32[]{:S(2)}, u32[]{:S(2)}) collective-permute-start(f32[8,128]{1,0:T(8,128)S(1)} %get-tuple-element.44.refs_0_), channel_id=1, source_target_pairs={{0,3},{1,2},{2,1},{3,0},{4,7},{5,6},{6,5},{7,4},{8,11},{9,10},{10,... | collective-permute-start | bytes 12296 | tf_op jit(solution)/shard_map/ppermute | solution.py:328
  90.4 1.8 %collective-permute-start.26 = (f32[8,128]{1,0:T(8,128)S(1)}, f32[8,128]{1,0:T(8,128)S(1)}, u32[]{:S(2)}, u32[]{:S(2)}) collective-permute-start(f32[8,128]{1,0:T(8,128)S(1)} %collective-permute-done.24.refs_1_), channel_id=1, source_target_pairs={{0,4},{4,0},{8,12},{12,8},{16,20},{20,16},{24,28},{28,24},{1,5},{5... | collective-permute-start | bytes 12296 | tf_op jit(solution)/shard_map/ppermute | solution.py:328

commit v4 on v3

--- a/solution.py
+++ b/solution.py
@@ -44,13 +44,14 @@
     return rows == lax.broadcasted_iota(jnp.int32, (rank, rank), 1)
 
 
-def mttkrp(factor, columns_c, high_ref, low_ref, ready=None):
+def mttkrp(factor, wide_ref, high_ref, low_ref, ready=None):
     rank = factor.shape[0]
     both, cross = None, None
     for k in range(high_ref.shape[0]):
         if ready is not None:
             ready(k)
-        high, low = split(factor * columns_c[:, k : k + 1])
+        spread = wide_ref[k]
+        high, low = split(factor * jnp.concatenate([spread] * (factor.shape[1] // spread.shape[1]), axis=1))
         first = dot(jnp.concatenate([high, low], axis=0), high_ref[k])
         second = dot(high, low_ref[k])
         both = first if both is None else both + first
@@ -65,11 +66,11 @@
     return jnp.concatenate([gram[q * rows : (q + 1) * rows] for q in range(parts)], axis=1)
 
 
-def pack(solved, columns_ref, high_ref, low_ref, packed_ref):
+def pack(solved, wide_ref, high_ref, low_ref, packed_ref):
     rank, width = solved.shape
     parts = split(solved)
     packed_ref[rank:] = pack_gram(split_dot(parts, parts, (1, 1)), width)
-    packed_ref[:rank] = mttkrp(solved, columns_ref[...], high_ref, low_ref)
+    packed_ref[:rank] = mttkrp(solved, wide_ref, high_ref, low_ref)
 
 
 def unpack_gram(packed, rank):
@@ -138,7 +139,7 @@
 
 
 def start_kernel(tensor_hbm, factor_hbm, c_hbm, high_ref, low_ref, turned_high_ref, turned_low_ref, *refs):
-    gram_c_ref, columns_ref, out_ref, tensor_ref, factor_ref, c_ref, padded_ref, sems = refs
+    gram_c_ref, wide_ref, out_ref, tensor_ref, factor_ref, c_ref, padded_ref, sems = refs
     depth, rank = c_hbm.shape
     small = [
         pltpu.make_async_copy(c_hbm, c_ref, sems.at[depth]),
@@ -154,7 +155,8 @@
         copy.wait()
     padded_ref[:depth, :rank] = c_ref[...]
     columns_c = padded_ref[...].T[:rank, :depth]
-    columns_ref[...] = columns_c
+    for k in range(depth):
+        wide_ref[k] = jnp.broadcast_to(columns_c[:, k : k + 1], wide_ref.shape[1:])
     factor = factor_ref[...]
 
     def arrive(k):
@@ -174,7 +176,7 @@
             parts = split(factor)
             out_ref[rank:] = pack_gram(split_dot(parts, parts, (1, 1)), factor.shape[1])
 
-    out_ref[:rank] = mttkrp(factor, columns_c, turned_high_ref, turned_low_ref, ready)
+    out_ref[:rank] = mttkrp(factor, wide_ref, turned_high_ref, turned_low_ref, ready)
 
 
 def own_core():
@@ -380,9 +382,9 @@
     packed_a, packed_b = [(rank + rank * rank // n, n) for n in (height, width)]
     scratch = [pltpu.VMEM((rank, rank), jnp.float32)] * 2
     full = [pltpu.VMEM((3, rank, width), jnp.float32)]
-    high, low, turned_high, turned_low, gram_c, columns, partial = call(
+    high, low, turned_high, turned_low, gram_c, wide, partial = call(
         start_kernel,
-        (part, part, turned, turned, f32((rank, rank)), f32((rank, depth)), f32(packed_a)),
+        (part, part, turned, turned, f32((rank, rank)), f32((depth, rank, 128)), f32(packed_a)),
         *[pltpu.with_memory_space_constraint(x, pltpu.HBM) for x in (tensor, factor_b, factor_c)],
         in_specs=[pl.BlockSpec(memory_space=pltpu.HBM)] * 3,
         scratch=[
@@ -399,7 +401,7 @@
         pieces = exchange(partial, "col")
         kernel = functools.partial(left_kernel, len(pieces), cols_all, sweep > 0, last)
         outs = (f32(packed_b), f32(left)) if last else (f32(packed_b),)
-        partial, *solved_a = call(kernel, outs, *pieces, gram_c, columns, high, low, scratch=scratch)
+        partial, *solved_a = call(kernel, outs, *pieces, gram_c, wide, high, low, scratch=scratch)
         pieces = exchange_by_cores(partial, "row", rank)
         kernel = functools.partial(invert_kernel, rows_all)
         outs = (f32((rank + 8, rank)), f32((1, rank))) if last else (f32((rank + 8, rank)),)
@@ -407,7 +409,7 @@
         kernel = functools.partial(right_kernel, last)
         if not last:
             partial = call(
-                kernel, f32(packed_a), *pieces, inverse, columns, turned_high, turned_low, scratch=full
+                kernel, f32(packed_a), *pieces, inverse, wide, turned_high, turned_low, scratch=full
             )
         else:
             solved_b, squares = call(kernel, (f32(right), f32((8, 2 * rank))), *pieces, inverse, scratch=full)

time: 92.8 us -> 92 us (level)
  no operation moved by 1% of the time
where the time goes in v4:
time: 92 us; the launch traced here: 92.1 us
  Pallas kernels  35.9 us (39%)
  waiting for transfers between devices  28.1 us (31%)
  starting transfers between devices  27.3 us (30%)
    pallas_call x15, Pallas kernels, call(): pl.pallas_call(kernel, out_shape=out_shape, scratch_shapes=scratch, compi...  35.9 us
    ppermute x23, starting transfers between devices, swap(): lax.ppermute(x, axis, [(d, d ^ stride) for d in range(lax.axis_size(axis))])  23.2 us
    ppermute x23, waiting for transfers between devices, swap(): lax.ppermute(x, axis, [(d, d ^ stride) for d in range(lax.axis_size(axis))])  23.2 us
    ppermute x3, waiting for transfers between devices, exchange_by_cores(): lax.ppermute(x, axis, [(d, d ^ (stride if d % 2 == 0 else 2 * stride)) fo...  3.98 us
    ppermute x3, starting transfers between devices, exchange_by_cores(): lax.ppermute(x, axis, [(d, d ^ (stride if d % 2 == 0 else 2 * stride)) fo...  3.12 us
  transfers between devices with their start and end apart: 27, of which 19 were waited for; matrix products, arithmetic and copies ran while one was open for 0% of the time, Pallas kernels for 14%

profile of v4, /device:TPU:0, one launch (start us, length us, event | category | flops | bytes accessed | tf_op | source)
XLA Modules:
  0.0 92.1 jit_solution(16177814611153669959)
XLA Ops:
  0.6 3.5 %shard_map.58 = (bf16[16,256,256]{2,1,0:T(8,128)(2,1)S(1)}, bf16[16,256,256]{2,1,0:T(8,128)(2,1)S(1)}, bf16[16,256,256]{2,1,0:T(8,128)(2,1)S(1)}, bf16[16,256,25...) custom-call(f32[16,256,256]{2,1,0:T(8,128)} %tensor_hbm.1, ...), custom_call_target="tpu_custom_call" | custom-call | tf_op jit(solution)/shard_map/pallas_call | solution.py:320
  4.1 4.0 %collective-permute-start.2 = (f32[80,256]{1,0:T(8,128)S(1)}, f32[80,256]{1,0:T(8,128)S(1)}, u32[]{:S(2)}, u32[]{:S(2)}) collective-permute-start(f32[80,256]{1,0:T(8,128)S(1)} %get-tuple-element.26.refs_0_), channel_id=1, source_target_pairs={{0,3},{1,2},{2,1},{3,0},{4,7},{5,6},{6,5},{7,4},{8,11},{9,10},{10,... | collective-permute-start | bytes 245768 | tf_op jit(solution)/shard_map/ppermute | solution.py:330
  8.1 0.5 collective-permute-start.1
  8.6 0.1 collective-permute-start
  8.7 1.9 %collective-permute-done.2.refs_3_ = f32[80,256]{1,0:T(8,128)S(1)} collective-permute-done((f32[80,256]{1,0:T(8,128)S(1)}, f32[80,256]{1,0:T(8,128)S(1)}, u32[]{:S(2)}, u32[]{:S(2)}) %collective-permute-start.2) | collective-permute-done | bytes 81952 | tf_op jit(solution)/shard_map/ppermute | solution.py:330
  10.7 1.9 %collective-permute-done.1.refs_2_ = f32[80,256]{1,0:T(8,128)S(1)} collective-permute-done((f32[80,256]{1,0:T(8,128)S(1)}, f32[80,256]{1,0:T(8,128)S(1)}, u32[]{:S(2)}, u32[]{:S(2)}) %collective-permute-start.1) | collective-permute-done | bytes 81952 | tf_op jit(solution)/shard_map/ppermute | solution.py:330
  12.5 0.5 collective-permute-done.refs_1_
  13.0 4.4 %shard_map.59.refs_0_ = f32[80,256]{1,0:T(8,128)S(1)} custom-call(f32[80,256]{1,0:T(8,128)S(1)} %get-tuple-element.26.refs_0_, f32[80,256]{1,0:T(8,128)S(1)} %collective-permute-done.refs_1_, f32[80,256]{1,0:T(8,128)S(1)} %collective-permute-done.1.refs_2_, f32[80,256]{1,0:T(8,128)S(1)} %collective-permute-done.2.refs_3_, ...), custom_call_target="tpu_custom_call" | custom-call | tf_op jit(solution)/shard_map/pallas_call | solution.py:320
  17.4 0.1 collective-permute-start.3
  17.5 1.3 %collective-permute-done.3.refs_1_ = f32[80,256]{1,0:T(8,128)S(1)} collective-permute-done((f32[80,256]{1,0:T(8,128)S(1)}, f32[80,256]{1,0:T(8,128)S(1)}, u32[]{:S(2)}, u32[]{:S(2)}) %collective-permute-start.3) | collective-permute-done | bytes 81952 | tf_op jit(solution)/shard_map/ppermute | solution.py:330
  18.8 1.6 %collective-permute-start.4 = (f32[80,256]{1,0:T(8,128)S(1)}, f32[80,256]{1,0:T(8,128)S(1)}, u32[]{:S(2)}, u32[]{:S(2)}) collective-permute-start(f32[80,256]{1,0:T(8,128)S(1)} %get-tuple-element.31.refs_0_), channel_id=1, source_target_pairs={{0,8},{4,20},{8,0},{12,28},{16,24},{20,4},{24,16},{28,12},{1,9},{5... | collective-permute-start | bytes 245768 | tf_op jit(solution)/shard_map/ppermute | solution.py:352
  20.5 2.5 %collective-permute-start.5 = (f32[48,256]{1,0:T(8,128)S(1)}, f32[48,256]{1,0:T(8,128)S(1)}, u32[]{:S(2)}, u32[]{:S(2)}) collective-permute-start(f32[48,256]{1,0:T(8,128)S(1)} %get-tuple-element.32), channel_id=1, source_target_pairs={{0,24},{4,28},{8,16},{12,20},{16,8},{20,12},{24,0},{28,4},{1,25},{... | collective-permute-start | bytes 147464 | tf_op jit(solution)/shard_map/ppermute | solution.py:330
  22.9 1.3 %collective-permute-done.4.refs_1_ = f32[80,256]{1,0:T(8,128)S(1)} collective-permute-done((f32[80,256]{1,0:T(8,128)S(1)}, f32[80,256]{1,0:T(8,128)S(1)}, u32[]{:S(2)}, u32[]{:S(2)}) %collective-permute-start.4) | collective-permute-done | bytes 81952 | tf_op jit(solution)/shard_map/ppermute | solution.py:352
  24.2 0.0 collective-permute-start.6
  24.2 2.6 %collective-permute-done.5.refs_2_ = f32[48,256]{1,0:T(8,128)S(1)} collective-permute-done((f32[48,256]{1,0:T(8,128)S(1)}, f32[48,256]{1,0:T(8,128)S(1)}, u32[]{:S(2)}, u32[]{:S(2)}) %collective-permute-start.5) | collective-permute-done | bytes 49184 | tf_op jit(solution)/shard_map/ppermute | solution.py:330
  26.8 0.0 collective-permute-start.7
  26.8 0.0 collective-permute-done.6.refs_3_
  26.8 3.2 %shard_map.61.refs_5_ = f32[72,64]{1,0:T(8,128)S(1)} custom-call(f32[80,256]{1,0:T(8,128)S(1)} %get-tuple-element.31.refs_0_, f32[80,256]{1,0:T(8,128)S(1)} %collective-permute-done.4.refs_1_, f32[48,256]{1,0:T(8,128)S(1)} %collective-permute-done.5.refs_2_, f32[80,256]{1,0:T(8,128)S(1)} %collective-permute-done.6.refs_3_, ...), custom_call_target="tpu_custom_call" | custom-call | bytes 4194304 | tf_op jit(solution)/shard_map/pallas_call | solution.py:320
  30.1 0.0 collective-permute-done.7.refs_4_
  30.1 1.1 %shard_map.62.refs_0_ = f32[80,256]{1,0:T(8,128)S(1)} custom-call(f32[80,256]{1,0:T(8,128)S(1)} %get-tuple-element.31.refs_0_, f32[80,256]{1,0:T(8,128)S(1)} %collective-permute-done.4.refs_1_, f32[48,256]{1,0:T(8,128)S(1)} %collective-permute-done.5.refs_2_, f32[80,256]{1,0:T(8,128)S(1)} %collective-permute-done.6.refs_3_, ...), custom_call_target="tpu_custom_call" | custom-call | tf_op jit(solution)/shard_map/pallas_call | solution.py:320
  31.2 1.6 %collective-permute-start.10 = (f32[80,256]{1,0:T(8,128)S(1)}, f32[80,256]{1,0:T(8,128)S(1)}, u32[]{:S(2)}, u32[]{:S(2)}) collective-permute-start(f32[80,256]{1,0:T(8,128)S(1)} %shard_map.62.refs_0_), channel_id=1, source_target_pairs={{0,3},{1,2},{2,1},{3,0},{4,7},{5,6},{6,5},{7,4},{8,11},{9,10},{10,... | collective-permute-start | bytes 245768 | tf_op jit(solution)/shard_map/ppermute | solution.py:330
  32.8 1.0 %collective-permute-start.9 = (f32[80,256]{1,0:T(8,128)S(1)}, f32[80,256]{1,0:T(8,128)S(1)}, u32[]{:S(2)}, u32[]{:S(2)}) collective-permute-start(f32[80,256]{1,0:T(8,128)S(1)} %shard_map.62.refs_0_), channel_id=1, source_target_pairs={{0,2},{1,3},{2,0},{3,1},{4,6},{5,7},{6,4},{7,5},{8,10},{9,11},{10,... | collective-permute-start | bytes 245768 | tf_op jit(solution)/shard_map/ppermute | solution.py:330
  33.7 1.0 %collective-permute-start.8 = (f32[80,256]{1,0:T(8,128)S(1)}, f32[80,256]{1,0:T(8,128)S(1)}, u32[]{:S(2)}, u32[]{:S(2)}) collective-permute-start(f32[80,256]{1,0:T(8,128)S(1)} %shard_map.62.refs_0_), channel_id=1, source_target_pairs={{0,1},{1,0},{2,3},{3,2},{4,5},{5,4},{6,7},{7,6},{8,9},{9,8},{10,11... | collective-permute-start | bytes 245768 | tf_op jit(solution)/shard_map/ppermute | solution.py:330
  34.8 2.5 %collective-permute-done.10.refs_3_ = f32[80,256]{1,0:T(8,128)S(1)} collective-permute-done((f32[80,256]{1,0:T(8,128)S(1)}, f32[80,256]{1,0:T(8,128)S(1)}, u32[]{:S(2)}, u32[]{:S(2)}) %collective-permute-start.10) | collective-permute-done | bytes 81952 | tf_op jit(solution)/shard_map/ppermute | solution.py:330
  37.3 1.5 %collective-permute-done.9.refs_2_ = f32[80,256]{1,0:T(8,128)S(1)} collective-permute-done((f32[80,256]{1,0:T(8,128)S(1)}, f32[80,256]{1,0:T(8,128)S(1)}, u32[]{:S(2)}, u32[]{:S(2)}) %collective-permute-start.9) | collective-permute-done | bytes 81952 | tf_op jit(solution)/shard_map/ppermute | solution.py:330
  38.8 0.1 collective-permute-done.8.refs_1_
  38.9 5.8 %shard_map.63.refs_0_ = f32[80,256]{1,0:T(8,128)S(1)} custom-call(f32[80,256]{1,0:T(8,128)S(1)} %shard_map.62.refs_0_, f32[80,256]{1,0:T(8,128)S(1)} %collective-permute-done.8.refs_1_, f32[80,256]{1,0:T(8,128)S(1)} %collective-permute-done.9.refs_2_, f32[80,256]{1,0:T(8,128)S(1)} %collective-permute-done.10.refs_3_, ...), custom_call_target="tpu_custom_call" | custom-call | tf_op jit(solution)/shard_map/pallas_call | solution.py:320
  44.7 0.1 collective-permute-start.11
  44.8 1.3 %collective-permute-done.11.refs_1_ = f32[80,256]{1,0:T(8,128)S(1)} collective-permute-done((f32[80,256]{1,0:T(8,128)S(1)}, f32[80,256]{1,0:T(8,128)S(1)}, u32[]{:S(2)}, u32[]{:S(2)}) %collective-permute-start.11) | collective-permute-done | bytes 81952 | tf_op jit(solution)/shard_map/ppermute | solution.py:330
  46.0 0.3 collective-permute-start.12
  46.3 3.4 %collective-permute-start.13 = (f32[48,256]{1,0:T(8,128)S(1)}, f32[48,256]{1,0:T(8,128)S(1)}, u32[]{:S(2)}, u32[]{:S(2)}) collective-permute-start(f32[48,256]{1,0:T(8,128)S(1)} %get-tuple-element.36), channel_id=1, source_target_pairs={{0,24},{4,28},{8,16},{12,20},{16,8},{20,12},{24,0},{28,4},{1,25},{... | collective-permute-start | bytes 147464 | tf_op jit(solution)/shard_map/ppermute | solution.py:330
  49.7 1.2 %collective-permute-done.12.refs_1_ = f32[80,256]{1,0:T(8,128)S(1)} collective-permute-done((f32[80,256]{1,0:T(8,128)S(1)}, f32[80,256]{1,0:T(8,128)S(1)}, u32[]{:S(2)}, u32[]{:S(2)}) %collective-permute-start.12) | collective-permute-done | bytes 81952 | tf_op jit(solution)/shard_map/ppermute | solution.py:352
  50.9 0.7 collective-permute-start.14
  51.7 1.2 %collective-permute-done.13.refs_2_ = f32[48,256]{1,0:T(8,128)S(1)} collective-permute-done((f32[48,256]{1,0:T(8,128)S(1)}, f32[48,256]{1,0:T(8,128)S(1)}, u32[]{:S(2)}, u32[]{:S(2)}) %collective-permute-start.13) | collective-permute-done | bytes 49184 | tf_op jit(solution)/shard_map/ppermute | solution.py:330
  52.9 0.3 collective-permute-start.15
  53.1 0.0 collective-permute-done.14.refs_3_
  53.1 4.3 %shard_map.65.refs_5_ = f32[72,64]{1,0:T(8,128)S(1)} custom-call(f32[80,256]{1,0:T(8,128)S(1)} %get-tuple-element.35.refs_0_, f32[80,256]{1,0:T(8,128)S(1)} %collective-permute-done.12.refs_1_, f32[48,256]{1,0:T(8,128)S(1)} %collective-permute-done.13.refs_2_, f32[80,256]{1,0:T(8,128)S(1)} %collective-permute-done.14.refs_3_, ...), custom_call_target="tpu_custom_call" | custom-call | bytes 4194304 | tf_op jit(solution)/shard_map/pallas_call | solution.py:320
  57.4 0.0 collective-permute-done.15.refs_4_
  57.4 1.1 %shard_map.66.refs_0_ = f32[80,256]{1,0:T(8,128)S(1)} custom-call(f32[80,256]{1,0:T(8,128)S(1)} %get-tuple-element.35.refs_0_, f32[80,256]{1,0:T(8,128)S(1)} %collective-permute-done.12.refs_1_, f32[48,256]{1,0:T(8,128)S(1)} %collective-permute-done.13.refs_2_, f32[80,256]{1,0:T(8,128)S(1)} %collective-permute-done.14.refs_3_, ...), custom_call_target="tpu_custom_call" | custom-call | tf_op jit(solution)/shard_map/pallas_call | solution.py:320
  58.6 1.5 %collective-permute-start.18 = (f32[80,256]{1,0:T(8,128)S(1)}, f32[80,256]{1,0:T(8,128)S(1)}, u32[]{:S(2)}, u32[]{:S(2)}) collective-permute-start(f32[80,256]{1,0:T(8,128)S(1)} %shard_map.66.refs_0_), channel_id=1, source_target_pairs={{0,3},{1,2},{2,1},{3,0},{4,7},{5,6},{6,5},{7,4},{8,11},{9,10},{10,... | collective-permute-start | bytes 245768 | tf_op jit(solution)/shard_map/ppermute | solution.py:330
  60.0 1.0 %collective-permute-start.17 = (f32[80,256]{1,0:T(8,128)S(1)}, f32[80,256]{1,0:T(8,128)S(1)}, u32[]{:S(2)}, u32[]{:S(2)}) collective-permute-start(f32[80,256]{1,0:T(8,128)S(1)} %shard_map.66.refs_0_), channel_id=1, source_target_pairs={{0,2},{1,3},{2,0},{3,1},{4,6},{5,7},{6,4},{7,5},{8,10},{9,11},{10,... | collective-permute-start | bytes 245768 | tf_op jit(solution)/shard_map/ppermute | solution.py:330
  61.0 1.1 %collective-permute-start.16 = (f32[80,256]{1,0:T(8,128)S(1)}, f32[80,256]{1,0:T(8,128)S(1)}, u32[]{:S(2)}, u32[]{:S(2)}) collective-permute-start(f32[80,256]{1,0:T(8,128)S(1)} %shard_map.66.refs_0_), channel_id=1, source_target_pairs={{0,1},{1,0},{2,3},{3,2},{4,5},{5,4},{6,7},{7,6},{8,9},{9,8},{10,11... | collective-permute-start | bytes 245768 | tf_op jit(solution)/shard_map/ppermute | solution.py:330
  62.1 2.4 %collective-permute-done.18.refs_3_ = f32[80,256]{1,0:T(8,128)S(1)} collective-permute-done((f32[80,256]{1,0:T(8,128)S(1)}, f32[80,256]{1,0:T(8,128)S(1)}, u32[]{:S(2)}, u32[]{:S(2)}) %collective-permute-start.18) | collective-permute-done | bytes 81952 | tf_op jit(solution)/shard_map/ppermute | solution.py:330
  64.5 1.4 %collective-permute-done.17.refs_2_ = f32[80,256]{1,0:T(8,128)S(1)} collective-permute-done((f32[80,256]{1,0:T(8,128)S(1)}, f32[80,256]{1,0:T(8,128)S(1)}, u32[]{:S(2)}, u32[]{:S(2)}) %collective-permute-start.17) | collective-permute-done | bytes 81952 | tf_op jit(solution)/shard_map/ppermute | solution.py:330
  65.9 0.0 collective-permute-done.16.refs_1_
  65.9 6.1 %shard_map.67 = (f32[80,256]{1,0:T(8,128)S(1)}, f32[64,256]{1,0:T(8,128)S(1)}) custom-call(f32[80,256]{1,0:T(8,128)S(1)} %shard_map.66.refs_0_, f32[80,256]{1,0:T(8,128)S(1)} %collective-permute-done.16.refs_1_, f32[80,256]{1,0:T(8,128)S(1)} %collective-permute-done.17.refs_2_, f32[80,256]{1,0:T(8,128)S(1)} %collective-permute-done.18.refs_3_, ...), custom_call_target="tpu_custom_call" | custom-call | tf_op jit(solution)/shard_map/pallas_call | solution.py:320
  72.0 0.1 collective-permute-start.19
  72.1 1.3 %collective-permute-done.19.refs_1_ = f32[80,256]{1,0:T(8,128)S(1)} collective-permute-done((f32[80,256]{1,0:T(8,128)S(1)}, f32[80,256]{1,0:T(8,128)S(1)}, u32[]{:S(2)}, u32[]{:S(2)}) %collective-permute-start.19) | collective-permute-done | bytes 81952 | tf_op jit(solution)/shard_map/ppermute | solution.py:330
  73.4 1.2 %collective-permute-start.20 = (f32[80,256]{1,0:T(8,128)S(1)}, f32[80,256]{1,0:T(8,128)S(1)}, u32[]{:S(2)}, u32[]{:S(2)}) collective-permute-start(f32[80,256]{1,0:T(8,128)S(1)} %get-tuple-element.38.refs_0_), channel_id=1, source_target_pairs={{0,8},{4,20},{8,0},{12,28},{16,24},{20,4},{24,16},{28,12},{1,9},{5... | collective-permute-start | bytes 245768 | tf_op jit(solution)/shard_map/ppermute | solution.py:352
  74.6 2.6 %collective-permute-start.21 = (f32[48,256]{1,0:T(8,128)S(1)}, f32[48,256]{1,0:T(8,128)S(1)}, u32[]{:S(2)}, u32[]{:S(2)}) collective-permute-start(f32[48,256]{1,0:T(8,128)S(1)} %get-tuple-element.39), channel_id=1, source_target_pairs={{0,24},{4,28},{8,16},{12,20},{16,8},{20,12},{24,0},{28,4},{1,25},{... | collective-permute-start | bytes 147464 | tf_op jit(solution)/shard_map/ppermute | solution.py:330
  77.3 1.5 %collective-permute-done.20.refs_1_ = f32[80,256]{1,0:T(8,128)S(1)} collective-permute-done((f32[80,256]{1,0:T(8,128)S(1)}, f32[80,256]{1,0:T(8,128)S(1)}, u32[]{:S(2)}, u32[]{:S(2)}) %collective-permute-start.20) | collective-permute-done | bytes 81952 | tf_op jit(solution)/shard_map/ppermute | solution.py:352
  78.8 0.0 collective-permute-start.22
  78.8 2.3 %collective-permute-done.21.refs_2_ = f32[48,256]{1,0:T(8,128)S(1)} collective-permute-done((f32[48,256]{1,0:T(8,128)S(1)}, f32[48,256]{1,0:T(8,128)S(1)}, u32[]{:S(2)}, u32[]{:S(2)}) %collective-permute-start.21) | collective-permute-done | bytes 49184 | tf_op jit(solution)/shard_map/ppermute | solution.py:330
  81.1 0.0 collective-permute-done.22.refs_3_
  81.1 4.3 %shard_map.69 = (f32[72,64]{1,0:T(8,128)S(1)}, f32[1,64]{1,0:T(1,128)S(1)}) custom-call(f32[80,256]{1,0:T(8,128)S(1)} %get-tuple-element.38.refs_0_, f32[80,256]{1,0:T(8,128)S(1)} %collective-permute-done.20.refs_1_, f32[48,256]{1,0:T(8,128)S(1)} %collective-permute-done.21.refs_2_, f32[80,256]{1,0:T(8,128)S(1)} %collective-permute-done.22.refs_3_, ...), custom_call_target="tpu_custom_call" | custom-call | bytes 4194304 | tf_op jit(solution)/shard_map/pallas_call | solution.py:320
  85.4 0.5 shard_map.71
  85.9 0.9 collective-permute-start.24
  86.8 1.7 %collective-permute-start.25 = (f32[8,128]{1,0:T(8,128)S(1)}, f32[8,128]{1,0:T(8,128)S(1)}, u32[]{:S(2)}, u32[]{:S(2)}) collective-permute-start(f32[8,128]{1,0:T(8,128)S(1)} %get-tuple-element.44.refs_0_), channel_id=1, source_target_pairs={{0,3},{1,2},{2,1},{3,0},{4,7},{5,6},{6,5},{7,4},{8,11},{9,10},{10,... | collective-permute-start | bytes 12296 | tf_op jit(solution)/shard_map/ppermute | solution.py:330
  88.6 1.0 %collective-permute-done.24.refs_1_ = f32[8,128]{1,0:T(8,128)S(1)} collective-permute-done((f32[8,128]{1,0:T(8,128)S(1)}, f32[8,128]{1,0:T(8,128)S(1)}, u32[]{:S(2)}, u32[]{:S(2)}) %collective-permute-start.24) | collective-permute-done | bytes 4128 | tf_op jit(solution)/shard_map/ppermute | solution.py:365
  89.5 0.0 collective-permute-start.26
  89.6 0.7 shard_map.70
  90.3 1.1 %collective-permute-done.25.refs_2_ = f32[8,128]{1,0:T(8,128)S(1)} collective-permute-done((f32[8,128]{1,0:T(8,128)S(1)}, f32[8,128]{1,0:T(8,128)S(1)}, u32[]{:S(2)}, u32[]{:S(2)}) %collective-permute-start.25) | collective-permute-done | bytes 4128 | tf_op jit(solution)/shard_map/ppermute | solution.py:330
  91.3 0.0 collective-permute-done.26.refs_3_
  91.3 0.7 shard_map.72
  (8 shorter events, 0.1 us)
Async XLA Ops:
  4.1 6.5 %collective-permute-start.2 = (f32[80,256]{1,0:T(8,128)S(1)}, f32[80,256]{1,0:T(8,128)S(1)}, u32[]{:S(2)}, u32[]{:S(2)}) collective-permute-start(f32[80,256]{1,0:T(8,128)S(1)} %get-tuple-element.26.refs_0_), channel_id=1, source_target_pairs={{0,3},{1,2},{2,1},{3,0},{4,7},{5,6},{6,5},{7,4},{8,11},{9,10},{10,... | collective-permute-start | bytes 245768 | tf_op jit(solution)/shard_map/ppermute | solution.py:330
  8.1 4.4 %collective-permute-start.1 = (f32[80,256]{1,0:T(8,128)S(1)}, f32[80,256]{1,0:T(8,128)S(1)}, u32[]{:S(2)}, u32[]{:S(2)}) collective-permute-start(f32[80,256]{1,0:T(8,128)S(1)} %get-tuple-element.26.refs_0_), channel_id=1, source_target_pairs={{0,2},{1,3},{2,0},{3,1},{4,6},{5,7},{6,4},{7,5},{8,10},{9,11},{10,... | collective-permute-start | bytes 245768 | tf_op jit(solution)/shard_map/ppermute | solution.py:330
  8.6 4.4 %collective-permute-start = (f32[80,256]{1,0:T(8,128)S(1)}, f32[80,256]{1,0:T(8,128)S(1)}, u32[]{:S(2)}, u32[]{:S(2)}) collective-permute-start(f32[80,256]{1,0:T(8,128)S(1)} %get-tuple-element.26.refs_0_), channel_id=1, source_target_pairs={{0,1},{1,0},{2,3},{3,2},{4,5},{5,4},{6,7},{7,6},{8,9},{9,8},{10,11... | collective-permute-start | bytes 245768 | tf_op jit(solution)/shard_map/ppermute | solution.py:330
  17.4 1.3 %collective-permute-start.3 = (f32[80,256]{1,0:T(8,128)S(1)}, f32[80,256]{1,0:T(8,128)S(1)}, u32[]{:S(2)}, u32[]{:S(2)}) collective-permute-start(f32[80,256]{1,0:T(8,128)S(1)} %shard_map.59.refs_0_), channel_id=1, source_target_pairs={{0,4},{4,0},{8,12},{12,8},{16,20},{20,16},{24,28},{28,24},{1,5},{5... | collective-permute-start | bytes 245768 | tf_op jit(solution)/shard_map/ppermute | solution.py:330
  18.8 5.4 %collective-permute-start.4 = (f32[80,256]{1,0:T(8,128)S(1)}, f32[80,256]{1,0:T(8,128)S(1)}, u32[]{:S(2)}, u32[]{:S(2)}) collective-permute-start(f32[80,256]{1,0:T(8,128)S(1)} %get-tuple-element.31.refs_0_), channel_id=1, source_target_pairs={{0,8},{4,20},{8,0},{12,28},{16,24},{20,4},{24,16},{28,12},{1,9},{5... | collective-permute-start | bytes 245768 | tf_op jit(solution)/shard_map/ppermute | solution.py:352
  20.5 6.3 %collective-permute-start.5 = (f32[48,256]{1,0:T(8,128)S(1)}, f32[48,256]{1,0:T(8,128)S(1)}, u32[]{:S(2)}, u32[]{:S(2)}) collective-permute-start(f32[48,256]{1,0:T(8,128)S(1)} %get-tuple-element.32), channel_id=1, source_target_pairs={{0,24},{4,28},{8,16},{12,20},{16,8},{20,12},{24,0},{28,4},{1,25},{... | collective-permute-start | bytes 147464 | tf_op jit(solution)/shard_map/ppermute | solution.py:330
  24.2 2.6 %collective-permute-start.6 = (f32[80,256]{1,0:T(8,128)S(1)}, f32[80,256]{1,0:T(8,128)S(1)}, u32[]{:S(2)}, u32[]{:S(2)}) collective-permute-start(f32[80,256]{1,0:T(8,128)S(1)} %collective-permute-done.4.refs_1_), channel_id=1, source_target_pairs={{0,4},{4,0},{8,12},{12,8},{16,20},{20,16},{24,28},{28,24},{1,5},{5... | collective-permute-start | bytes 245768 | tf_op jit(solution)/shard_map/ppermute | solution.py:330
  26.8 3.3 %collective-permute-start.7 = (f32[32,256]{1,0:T(8,128)S(1)}, f32[32,256]{1,0:T(8,128)S(1)}, u32[]{:S(2)}, u32[]{:S(2)}) collective-permute-start(f32[32,256]{1,0:T(8,128)S(1)} %slice.12), channel_id=1, source_target_pairs={{0,4},{4,0},{8,12},{12,8},{16,20},{20,16},{24,28},{28,24},{1,5},{5... | collective-permute-start | bytes 98312 | tf_op jit(solution)/shard_map/ppermute | solution.py:330
  31.2 6.1 %collective-permute-start.10 = (f32[80,256]{1,0:T(8,128)S(1)}, f32[80,256]{1,0:T(8,128)S(1)}, u32[]{:S(2)}, u32[]{:S(2)}) collective-permute-start(f32[80,256]{1,0:T(8,128)S(1)} %shard_map.62.refs_0_), channel_id=1, source_target_pairs={{0,3},{1,2},{2,1},{3,0},{4,7},{5,6},{6,5},{7,4},{8,11},{9,10},{10,... | collective-permute-start | bytes 245768 | tf_op jit(solution)/shard_map/ppermute | solution.py:330
  32.8 6.0 %collective-permute-start.9 = (f32[80,256]{1,0:T(8,128)S(1)}, f32[80,256]{1,0:T(8,128)S(1)}, u32[]{:S(2)}, u32[]{:S(2)}) collective-permute-start(f32[80,256]{1,0:T(8,128)S(1)} %shard_map.62.refs_0_), channel_id=1, source_target_pairs={{0,2},{1,3},{2,0},{3,1},{4,6},{5,7},{6,4},{7,5},{8,10},{9,11},{10,... | collective-permute-start | bytes 245768 | tf_op jit(solution)/shard_map/ppermute | solution.py:330
  33.7 5.1 %collective-permute-start.8 = (f32[80,256]{1,0:T(8,128)S(1)}, f32[80,256]{1,0:T(8,128)S(1)}, u32[]{:S(2)}, u32[]{:S(2)}) collective-permute-start(f32[80,256]{1,0:T(8,128)S(1)} %shard_map.62.refs_0_), channel_id=1, source_target_pairs={{0,1},{1,0},{2,3},{3,2},{4,5},{5,4},{6,7},{7,6},{8,9},{9,8},{10,11... | collective-permute-start | bytes 245768 | tf_op jit(solution)/shard_map/ppermute | solution.py:330
  44.7 1.3 %collective-permute-start.11 = (f32[80,256]{1,0:T(8,128)S(1)}, f32[80,256]{1,0:T(8,128)S(1)}, u32[]{:S(2)}, u32[]{:S(2)}) collective-permute-start(f32[80,256]{1,0:T(8,128)S(1)} %shard_map.63.refs_0_), channel_id=1, source_target_pairs={{0,4},{4,0},{8,12},{12,8},{16,20},{20,16},{24,28},{28,24},{1,5},{5... | collective-permute-start | bytes 245768 | tf_op jit(solution)/shard_map/ppermute | solution.py:330
  46.0 4.9 %collective-permute-start.12 = (f32[80,256]{1,0:T(8,128)S(1)}, f32[80,256]{1,0:T(8,128)S(1)}, u32[]{:S(2)}, u32[]{:S(2)}) collective-permute-start(f32[80,256]{1,0:T(8,128)S(1)} %get-tuple-element.35.refs_0_), channel_id=1, source_target_pairs={{0,8},{4,20},{8,0},{12,28},{16,24},{20,4},{24,16},{28,12},{1,9},{5... | collective-permute-start | bytes 245768 | tf_op jit(solution)/shard_map/ppermute | solution.py:352
  46.3 6.5 %collective-permute-start.13 = (f32[48,256]{1,0:T(8,128)S(1)}, f32[48,256]{1,0:T(8,128)S(1)}, u32[]{:S(2)}, u32[]{:S(2)}) collective-permute-start(f32[48,256]{1,0:T(8,128)S(1)} %get-tuple-element.36), channel_id=1, source_target_pairs={{0,24},{4,28},{8,16},{12,20},{16,8},{20,12},{24,0},{28,4},{1,25},{... | collective-permute-start | bytes 147464 | tf_op jit(solution)/shard_map/ppermute | solution.py:330
  50.9 2.2 %collective-permute-start.14 = (f32[80,256]{1,0:T(8,128)S(1)}, f32[80,256]{1,0:T(8,128)S(1)}, u32[]{:S(2)}, u32[]{:S(2)}) collective-permute-start(f32[80,256]{1,0:T(8,128)S(1)} %collective-permute-done.12.refs_1_), channel_id=1, source_target_pairs={{0,4},{4,0},{8,12},{12,8},{16,20},{20,16},{24,28},{28,24},{1,5},{5... | collective-permute-start | bytes 245768 | tf_op jit(solution)/shard_map/ppermute | solution.py:330
  52.9 4.5 %collective-permute-start.15 = (f32[32,256]{1,0:T(8,128)S(1)}, f32[32,256]{1,0:T(8,128)S(1)}, u32[]{:S(2)}, u32[]{:S(2)}) collective-permute-start(f32[32,256]{1,0:T(8,128)S(1)} %slice.13), channel_id=1, source_target_pairs={{0,4},{4,0},{8,12},{12,8},{16,20},{20,16},{24,28},{28,24},{1,5},{5... | collective-permute-start | bytes 98312 | tf_op jit(solution)/shard_map/ppermute | solution.py:330
  58.6 6.0 %collective-permute-start.18 = (f32[80,256]{1,0:T(8,128)S(1)}, f32[80,256]{1,0:T(8,128)S(1)}, u32[]{:S(2)}, u32[]{:S(2)}) collective-permute-start(f32[80,256]{1,0:T(8,128)S(1)} %shard_map.66.refs_0_), channel_id=1, source_target_pairs={{0,3},{1,2},{2,1},{3,0},{4,7},{5,6},{6,5},{7,4},{8,11},{9,10},{10,... | collective-permute-start | bytes 245768 | tf_op jit(solution)/shard_map/ppermute | solution.py:330
  60.0 5.9 %collective-permute-start.17 = (f32[80,256]{1,0:T(8,128)S(1)}, f32[80,256]{1,0:T(8,128)S(1)}, u32[]{:S(2)}, u32[]{:S(2)}) collective-permute-start(f32[80,256]{1,0:T(8,128)S(1)} %shard_map.66.refs_0_), channel_id=1, source_target_pairs={{0,2},{1,3},{2,0},{3,1},{4,6},{5,7},{6,4},{7,5},{8,10},{9,11},{10,... | collective-permute-start | bytes 245768 | tf_op jit(solution)/shard_map/ppermute | solution.py:330
  61.0 4.9 %collective-permute-start.16 = (f32[80,256]{1,0:T(8,128)S(1)}, f32[80,256]{1,0:T(8,128)S(1)}, u32[]{:S(2)}, u32[]{:S(2)}) collective-permute-start(f32[80,256]{1,0:T(8,128)S(1)} %shard_map.66.refs_0_), channel_id=1, source_target_pairs={{0,1},{1,0},{2,3},{3,2},{4,5},{5,4},{6,7},{7,6},{8,9},{9,8},{10,11... | collective-permute-start | bytes 245768 | tf_op jit(solution)/shard_map/ppermute | solution.py:330
  72.0 1.3 %collective-permute-start.19 = (f32[80,256]{1,0:T(8,128)S(1)}, f32[80,256]{1,0:T(8,128)S(1)}, u32[]{:S(2)}, u32[]{:S(2)}) collective-permute-start(f32[80,256]{1,0:T(8,128)S(1)} %get-tuple-element.37.refs_0_), channel_id=1, source_target_pairs={{0,4},{4,0},{8,12},{12,8},{16,20},{20,16},{24,28},{28,24},{1,5},{5... | collective-permute-start | bytes 245768 | tf_op jit(solution)/shard_map/ppermute | solution.py:330
  73.4 5.4 %collective-permute-start.20 = (f32[80,256]{1,0:T(8,128)S(1)}, f32[80,256]{1,0:T(8,128)S(1)}, u32[]{:S(2)}, u32[]{:S(2)}) collective-permute-start(f32[80,256]{1,0:T(8,128)S(1)} %get-tuple-element.38.refs_0_), channel_id=1, source_target_pairs={{0,8},{4,20},{8,0},{12,28},{16,24},{20,4},{24,16},{28,12},{1,9},{5... | collective-permute-start | bytes 245768 | tf_op jit(solution)/shard_map/ppermute | solution.py:352
  74.6 6.5 %collective-permute-start.21 = (f32[48,256]{1,0:T(8,128)S(1)}, f32[48,256]{1,0:T(8,128)S(1)}, u32[]{:S(2)}, u32[]{:S(2)}) collective-permute-start(f32[48,256]{1,0:T(8,128)S(1)} %get-tuple-element.39), channel_id=1, source_target_pairs={{0,24},{4,28},{8,16},{12,20},{16,8},{20,12},{24,0},{28,4},{1,25},{... | collective-permute-start | bytes 147464 | tf_op jit(solution)/shard_map/ppermute | solution.py:330
  78.8 2.3 %collective-permute-start.22 = (f32[80,256]{1,0:T(8,128)S(1)}, f32[80,256]{1,0:T(8,128)S(1)}, u32[]{:S(2)}, u32[]{:S(2)}) collective-permute-start(f32[80,256]{1,0:T(8,128)S(1)} %collective-permute-done.20.refs_1_), channel_id=1, source_target_pairs={{0,4},{4,0},{8,12},{12,8},{16,20},{20,16},{24,28},{28,24},{1,5},{5... | collective-permute-start | bytes 245768 | tf_op jit(solution)/shard_map/ppermute | solution.py:330
  81.1 4.3 %collective-permute-start.23 = (f32[32,256]{1,0:T(8,128)S(1)}, f32[32,256]{1,0:T(8,128)S(1)}, u32[]{:S(2)}, u32[]{:S(2)}) collective-permute-start(f32[32,256]{1,0:T(8,128)S(1)} %slice.14), channel_id=1, source_target_pairs={{0,4},{4,0},{8,12},{12,8},{16,20},{20,16},{24,28},{28,24},{1,5},{5... | collective-permute-start | bytes 98312 | tf_op jit(solution)/shard_map/ppermute | solution.py:330
  85.9 3.6 %collective-permute-start.24 = (f32[8,128]{1,0:T(8,128)S(1)}, f32[8,128]{1,0:T(8,128)S(1)}, u32[]{:S(2)}, u32[]{:S(2)}) collective-permute-start(f32[8,128]{1,0:T(8,128)S(1)} %get-tuple-element.44.refs_0_), channel_id=1, source_target_pairs={{0,1},{1,0},{2,3},{3,2},{4,6},{5,7},{6,4},{7,5},{8,9},{9,8},{10,11... | collective-permute-start | bytes 12296 | tf_op jit(solution)/shard_map/ppermute | solution.py:365
  86.8 4.5 %collective-permute-start.25 = (f32[8,128]{1,0:T(8,128)S(1)}, f32[8,128]{1,0:T(8,128)S(1)}, u32[]{:S(2)}, u32[]{:S(2)}) collective-permute-start(f32[8,128]{1,0:T(8,128)S(1)} %get-tuple-element.44.refs_0_), channel_id=1, source_target_pairs={{0,3},{1,2},{2,1},{3,0},{4,7},{5,6},{6,5},{7,4},{8,11},{9,10},{10,... | collective-permute-start | bytes 12296 | tf_op jit(solution)/shard_map/ppermute | solution.py:330
  89.5 1.8 %collective-permute-start.26 = (f32[8,128]{1,0:T(8,128)S(1)}, f32[8,128]{1,0:T(8,128)S(1)}, u32[]{:S(2)}, u32[]{:S(2)}) collective-permute-start(f32[8,128]{1,0:T(8,128)S(1)} %collective-permute-done.24.refs_1_), channel_id=1, source_target_pairs={{0,4},{4,0},{8,12},{12,8},{16,20},{20,16},{24,28},{28,24},{1,5},{5... | collective-permute-start | bytes 12296 | tf_op jit(solution)/shard_map/ppermute | solution.py:330
